TPU v7x, 32 devices: a whole 2x2x4 slice. The times are simulated.
32 devices in a mesh: groups: 2 (over x), dp: 4 (over z), fsdp: 4 (over y, core).
Axes of the slice: x: 2, y: 2, z: 4, core: 2. Of those that a mesh axis runs over, the one named last changes fastest.
Arguments:
- acts: bfloat16 [7168, 8192], P(('groups', 'dp'), 'fsdp'), parts along dimension 0, may hold values from -6 to 6
- out_grad: bfloat16 [7168, 8192], P(('groups', 'dp'), 'fsdp'), parts along dimension 0, may hold values from -6 to 6
- gate_pre: bfloat16 [7168, 14336], P(('groups', 'dp'), 'fsdp'), parts along dimension 0, may hold values from -8 to 8
- down_weight: bfloat16 [14336, 8192], P('fsdp', 'dp'), may hold values from -0.0625 to 0.0625
- proj_in: bfloat16 [64, 8192], P(None, 'fsdp'), may hold values from -0.0625 to 0.0625
- proj_out: bfloat16 [64, 14336], P(None, 'fsdp'), may hold values from -0.046875 to 0.046875
- lengths: int32 [8, 16], P(('groups', 'dp')), parts along dimension 0, may hold values from 1 to 112, 896 in all within a row
Outputs:
- fisher: float32 [8192, 4096], P(('groups', 'dp', 'fsdp')), parts along dimension 0
There are 2 independent parts, one for each index of `groups`. A program takes and returns all parts, laid end to end along the dimension named above; an argument that names none is the same for every part. Nothing has to cross between parts.
Inputs may be any that keep to these rules, and one draw needn't show every extreme that they name: `lengths`: every row sums to 896, and some example of every row holds exactly 112 tokens.
All inputs are finite; a program needn't handle non-finite values.
Results may differ from a plain program's by a relative error of at most 0.0041.
Values may be sent and summed in bfloat16 or wider, within the bound.
No kernel may reach another device: no remote copies, remote signals or barrier semaphores. Data moves between devices by JAX's collectives and lax.ppermute only.
A program may use at most 256 MiB of HBM per device.

v0:
```python
import jax
import jax.numpy as jnp
from jax import lax
from jax.sharding import PartitionSpec as P


def per_device(acts, out_grad, gate_pre, down_weight, proj_in, proj_out, lengths):
    tok_rows = acts.shape[0]
    full_grad = lax.all_gather(out_grad, "fsdp", axis=1, tiled=True)
    upstream = lax.dot_general(
        full_grad,
        lax.all_gather(down_weight, "dp", axis=1, tiled=True),
        (((1,), (1,)), ((), ())),
        preferred_element_type=jnp.float32,
    )
    up_grad = (upstream * jax.nn.silu(gate_pre.astype(jnp.float32))).astype(jnp.bfloat16)
    rank_in = proj_in.shape[0]
    partial_in = lax.dot_general(
        acts, proj_in, (((1,), (1,)), ((), ())), preferred_element_type=jnp.float32
    )
    partial_out = lax.dot_general(
        up_grad, proj_out, (((1,), (1,)), ((), ())), preferred_element_type=jnp.float32
    )
    joined = lax.psum(jnp.concatenate([partial_in, partial_out], axis=1), "fsdp")
    factors_in = joined[:, :rank_in]
    factors_out = joined[:, rank_in:]
    counts = lengths[0]
    stop_at = jnp.cumsum(counts, dtype=jnp.int32)
    starts = stop_at - counts
    position = jnp.arange(tok_rows, dtype=jnp.int32)
    member = (
        (position[None, :] >= starts[:, None]) & (position[None, :] < stop_at[:, None])
    ).astype(jnp.float32)
    weighted = member[:, :, None] * factors_in[None, :, :]
    example_count = counts.shape[0]
    example_grads = jnp.einsum(
        "eti,tj->eij", weighted, factors_out, precision=lax.Precision.HIGHEST
    ).reshape(example_count, -1)
    dp_count = lax.axis_size("dp")
    fsdp_count = lax.axis_size("fsdp")
    column = lax.axis_index("fsdp")
    width_all = example_grads.shape[1]
    own_rows = width_all // (dp_count * fsdp_count)
    norm_scale = 1.0 / (example_count * dp_count)
    shaped = example_grads.reshape(example_count, dp_count, fsdp_count, own_rows)
    picked = lax.dynamic_index_in_dim(shaped, column, 2, keepdims=False).reshape(
        example_count, dp_count * own_rows
    )
    product = lax.dot_general(
        picked,
        example_grads,
        (((0,), (0,)), ((), ())),
        precision=lax.Precision.HIGHEST,
        preferred_element_type=jnp.float32,
    )
    return lax.psum_scatter(product * norm_scale, "dp", scatter_dimension=0, tiled=True)


def solution(mesh):
    placed = (
        P(("groups", "dp"), "fsdp"),
        P(("groups", "dp"), "fsdp"),
        P(("groups", "dp"), "fsdp"),
        P("fsdp", "dp"),
        P(None, "fsdp"),
        P(None, "fsdp"),
        P(("groups", "dp"), None),
    )
    return jax.shard_map(
        per_device,
        mesh=mesh,
        in_specs=placed,
        out_specs=P(("groups", "dp", "fsdp"), None),
        check_vma=False,
    )
```

profile of v0, /device:TPU:0, one launch (start us, length us, event | category | flops | bytes accessed | tf_op | source)
XLA Modules:
  0.0 1492.2 jit_solution(9719428167306209136)
XLA Ops:
  6.5 0.0 copy-start
  6.5 0.0 copy-start.2
  6.5 0.0 copy-start.1
  6.5 0.0 all-gather.3.cloned.1.call-start
  6.5 0.7 all-gather.3.cloned.1.call-update
  7.3 0.0 all-gather.5.cloned.1.call-start
  7.3 0.7 all-gather.5.cloned.1.call-update
  8.0 0.0 all-reduce.2.cloned.1.call-start
  8.1 0.0 copy-done.2
  8.1 0.1 copy.9
  8.2 0.1 reduce
  8.3 0.0 copy-done.1
  8.3 3.3 fusion.11
  11.6 94.1 %all-gather.3.cloned.1.call-done = bf16[896,8192]{1,0:T(8,128)(2,1)} async-done(((bf16[896,2048]{1,0:T(8,128)(2,1)}), bf16[896,8192]{1,0:T(8,128)(2,1)}) %all-gather.3.cloned.1.call-update) | async-done | bytes 14680080 | tf_op jit(solution)/shard_map/all_gather | solution.py:9
  105.7 976.0 %all-gather.5.cloned.1.call-done = bf16[3584,8192]{1,0:T(8,128)(2,1)} async-done(((bf16[3584,2048]{1,0:T(8,128)(2,1)}), bf16[3584,8192]{1,0:T(8,128)(2,1)}) %all-gather.5.cloned.1.call-update) | async-done | bytes 58720272 | tf_op jit(solution)/shard_map/all_gather | solution.py:12
  1081.7 64.7 %fusion.4 = bf16[896,3584]{1,0:T(8,128)(2,1)} fusion(bf16[896,3584]{1,0:T(8,128)(2,1)} %param.9, bf16[896,8192]{1,0:T(8,128)(2,1)} %all-gather.3.cloned.1.call-done, bf16[3584,8192]{1,0:T(8,128)(2,1)} %all-gather.5.cloned.1.call-done), kind=kOutput, calls=%fused_computation.6 | convolution fusion | flops 52635828224 | bytes 86245376 | tf_op jit(solution)/shard_map/dot_general | solution.py:10
  1146.4 0.0 copy-done
  1146.4 4.9 fusion.12
  1151.3 0.8 pad_maximum_fusion
  1152.1 0.0 all-reduce.2.cloned.1.call-update
  1152.1 0.2 reduce-scatter.2.cloned.1.call-start
  1152.3 0.1 fusion.10
  1152.4 31.0 %all-reduce.2.cloned.1.call-done = f32[896,128]{0,1:T(8,128)} async-done(((f32[896,128]{0,1:T(8,128)}), f32[896,128]{0,1:T(8,128)}) %all-reduce.2.cloned.1.call-update) | async-done | bytes 458768 | tf_op jit(solution)/shard_map/psum | solution.py:24
  1183.4 1.0 slice.8
  1184.3 4.2 fusion.5
  1188.5 0.2 reshape_reshape.3
  1188.7 0.2 reshape.83
  1188.9 0.2 dynamic-slice_reduce_fusion
  1189.2 16.0 %convolution_multiply_fusion = f32[1024,4096]{1,0:T(8,128)} fusion(f32[16,1024]{1,0:T(8,128)S(1)} %bitcast.16, f32[16,4096]{1,0:T(8,128)S(1)} %reshape.83), kind=kOutput, calls=%fused_computation.7 | convolution fusion | flops 809500672 | bytes 17104896 | tf_op jit(solution)/shard_map/dot_general | solution.py:49
  1205.2 0.0 reduce-scatter.2.cloned.1.call-update
  1205.2 280.5 %reduce-scatter.2.cloned.1.call-done = f32[256,4096]{1,0:T(8,128)} async-done(((f32[1024,4096]{1,0:T(8,128)}), f32[256,4096]{1,0:T(8,128)}) %reduce-scatter.2.cloned.1.call-update) | async-done | bytes 4194320 | tf_op jit(solution)/shard_map/reduce_scatter | solution.py:56
  (3 shorter events, 0.1 us)
Async XLA Ops:
  6.5 1139.8 %copy-start = (bf16[64,3584]{1,0:T(8,128)(2,1)S(1)}, bf16[64,3584]{1,0:T(8,128)(2,1)}, u32[]{:S(2)}) copy-start(bf16[64,3584]{1,0:T(8,128)(2,1)} %param.12) | copy-start | bytes 1376260
  6.5 1.5 copy-start.2
  6.5 1.8 copy-start.1
  6.5 99.1 %all-gather.3.cloned.1.call-start = ((), (), s32[]{:S(2)}) async-start(), calls=%async_computation.1 | async-start | bytes 18350080 | tf_op jit(solution)/shard_map/all_gather | solution.py:9
  7.3 1074.4 %all-gather.5.cloned.1.call-start = ((), (), s32[]{:S(2)}) async-start(), calls=%async_computation.2 | async-start | bytes 73400320 | tf_op jit(solution)/shard_map/all_gather | solution.py:12
  8.0 1175.4 %all-reduce.2.cloned.1.call-start = ((), (), s32[]{:S(2)}) async-start(), calls=%async_computation.3 | async-start | bytes 917504 | tf_op jit(solution)/shard_map/psum | solution.py:24
  1152.1 333.6 %reduce-scatter.2.cloned.1.call-start = ((), (), s32[]{:S(2)}) async-start(), calls=%async_computation.4 | async-start | bytes 20971520 | tf_op jit(solution)/shard_map/reduce_scatter | solution.py:56
Sparse Core Ops, SparseCore 0:
  8.9 96.7 all-gather.2
  107.3 974.3 all-gather.4
  1152.2 31.1 all-reduce.1
  1205.3 280.2 reduce-scatter.1
where the time goes:
time: 1490 us
  waiting for transfers between devices  1380 us (93%)
  matrix products  93 us (6%)
    all_gather x1, waiting for transfers between devices, per_device(): lax.all_gather(down_weight, 'dp', axis=1, tiled=True)  976 us
    reduce_scatter x1, waiting for transfers between devices, per_device(): lax.psum_scatter(product * norm_scale, 'dp', scatter_dimension=0, tiled=T...  280 us
    all_gather x1, waiting for transfers between devices, per_device(): full_grad = lax.all_gather(out_grad, 'fsdp', axis=1, tiled=True)  94.1 us
    dot_general x1, matrix products, per_device(): lax.dot_general(full_grad, lax.all_gather(down_weight, 'dp', axis=1, tile...  64.7 us
    psum x1, waiting for transfers between devices, per_device(): lax.psum(jnp.concatenate([partial_in, partial_out], axis=1), 'fsdp')  31 us
  transfers between devices with their start and end apart: 4, of which 4 were waited for; matrix products, arithmetic and copies ran while one was open for 0% of the time, Pallas kernels for 0%

commit v1 on v0

v1 whole, which is shorter than its diff:
```python
import functools

import jax
import jax.numpy as jnp
from jax import lax
from jax.experimental import pallas as pl
from jax.experimental.pallas import tpu as pltpu
from jax.sharding import PartitionSpec as P

MATES = [(0, 1), (1, 0), (2, 3), (3, 2)]
ACROSS = [(1, 2), (2, 1)]
OUTWARD = [(1, 0), (2, 3)]
INWARD = [(0, 1), (3, 2)]
CHUNK = 256
VMEM_LIMIT = 58 * 1024 * 1024


def dot_nt(left, right):
    return lax.dot_general(left, right, (((1,), (1,)), ((), ())), preferred_element_type=jnp.float32)


def early_kernel(place, grad_ref, own_ref, mate_ref, near_ref, part_ref):
    step = pl.program_id(1)

    @pl.when(step == 0)
    def _():
        part_ref[...] = dot_nt(grad_ref[0], own_ref[...])

    @pl.when(step == 1)
    def _():
        part_ref[...] += dot_nt(grad_ref[0], mate_ref[...])

    @pl.when(step == 2)
    def _():
        part_ref[...] += dot_nt(grad_ref[0], near_ref[...])


def early_part(place, grads, down_weight, mate_weight, near_weight):
    hidden, width = mate_weight.shape
    tokens_dev = grads.shape[1]
    tile = tokens_dev // 2
    tiles = 2 * tokens_dev // tile
    per = tokens_dev // tile
    return pl.pallas_call(
        early_kernel,
        grid_spec=pltpu.PrefetchScalarGridSpec(
            num_scalar_prefetch=1,
            grid=(tiles, 3),
            in_specs=[
                pl.BlockSpec(
                    (1, tile, width),
                    lambda i, k, place: ((i // per ^ place[0]) * 4 + place[1 + k], i % per, 0),
                ),
                pl.BlockSpec((hidden, width), lambda i, k, place: (place[0], 0), pipeline_mode=pl.Buffered(1)),
                pl.BlockSpec((hidden, width), lambda i, k, place: (0, 0), pipeline_mode=pl.Buffered(1)),
                pl.BlockSpec((hidden, width), lambda i, k, place: (0, 0), pipeline_mode=pl.Buffered(1)),
            ],
            out_specs=pl.BlockSpec((tile, hidden), lambda i, k, place: (i, 0)),
        ),
        out_shape=jax.ShapeDtypeStruct((2 * tokens_dev, hidden), jnp.float32),
        compiler_params=pltpu.CompilerParams(vmem_limit_bytes=VMEM_LIMIT),
        cost_estimate=pl.CostEstimate(
            flops=2 * 2 * tokens_dev * hidden * width * 3,
            bytes_accessed=2 * 2 * tokens_dev * width * 3 + 6 * hidden * width + 8 * tokens_dev * hidden,
            transcendentals=0,
        ),
        name="early_part",
    )(place, grads, down_weight, mate_weight, near_weight)


def late_kernel(
    place, part_ref, grad_ref, far_ref, out_ref, gate_ref, guest_grad_ref, guest_gate_ref, proj_ref, sum_ref, new_ref
):
    inner = place[5] == 1
    far = far_ref[...]
    weight = jnp.where(inner, far, out_ref[...])
    rank = proj_ref.shape[0]

    def project(upstream, gate, exact):
        gate = gate.astype(jnp.float32)
        up_grad = upstream * (gate / (1.0 + jnp.exp(-gate)))
        high = up_grad.astype(jnp.bfloat16)
        low = jnp.where(exact, 0.0, up_grad - high.astype(jnp.float32)).astype(jnp.bfloat16)
        return dot_nt(high, proj_ref[...]) + dot_nt(low, proj_ref[...])

    upstream = part_ref[...] + dot_nt(grad_ref[0], weight)
    new_ref[:, :rank] = sum_ref[:, :rank] + project(upstream, gate_ref[...], inner)
    guest = dot_nt(guest_grad_ref[0], far)
    new_ref[:, rank:] = sum_ref[:, rank:] + project(guest, guest_gate_ref[...], False)


def late_part(place, chunk, part, grads, far, out, gates, guest_grads, guest_gates, proj_out, sums):
    tokens_dev, width = grads.shape[1:]
    hidden = part.shape[1]
    tile = tokens_dev // 2
    per = tokens_dev // tile
    wide = far.shape[0]
    count = hidden // wide
    rank = proj_out.shape[0]
    row = lambda i, place: (i, 0)
    return pl.pallas_call(
        late_kernel,
        grid_spec=pltpu.PrefetchScalarGridSpec(
            num_scalar_prefetch=1,
            grid=(2 * per,),
            in_specs=[
                pl.BlockSpec((tile, wide), lambda i, place: (i, chunk)),
                pl.BlockSpec(
                    (1, tile, width), lambda i, place: ((i // per ^ place[0]) * 4 + place[4], i % per, 0)
                ),
                pl.BlockSpec((wide, width), lambda i, place: (0, 0)),
                pl.BlockSpec((wide, width), lambda i, place: (0, 0)),
                pl.BlockSpec((tile, wide), lambda i, place: (i, chunk)),
                pl.BlockSpec((1, tile, width), lambda i, place: (i // per ^ place[0], i % per, 0)),
                pl.BlockSpec((tile, wide), row),
                pl.BlockSpec((rank, wide), lambda i, place: (0, place[0] * count + chunk)),
                pl.BlockSpec((tile, 2 * rank), row),
            ],
            out_specs=pl.BlockSpec((tile, 2 * rank), row),
        ),
        out_shape=jax.ShapeDtypeStruct(sums.shape, jnp.float32),
        input_output_aliases={9: 0},
        compiler_params=pltpu.CompilerParams(vmem_limit_bytes=VMEM_LIMIT),
        cost_estimate=pl.CostEstimate(
            flops=2 * 4 * tokens_dev * wide * (width + 2 * rank),
            bytes_accessed=8 * tokens_dev * width + 4 * wide * width + 16 * tokens_dev * wide,
            transcendentals=4 * tokens_dev * wide,
        ),
        name="late_part",
    )(place, part, grads, far, out, gates, guest_grads, guest_gates, proj_out, sums)


def example_sums(counts, factors_in, factors_out):
    tok_rows = factors_in.shape[0]
    stop_at = jnp.cumsum(counts, dtype=jnp.int32)
    starts = stop_at - counts
    position = jnp.arange(tok_rows, dtype=jnp.int32)
    member = (
        (position[None, :] >= starts[:, None]) & (position[None, :] < stop_at[:, None])
    ).astype(jnp.float32)
    weighted = member[:, :, None] * factors_in[None, :, :]
    return jnp.einsum(
        "eti,tj->eij", weighted, factors_out, precision=lax.Precision.HIGHEST
    ).reshape(counts.shape[0], -1)


def own_fisher(example_grads):
    every = lax.all_gather(example_grads, "dp", axis=0, tiled=True)
    fsdp_count = lax.axis_size("fsdp")
    own_rows = every.shape[1] // (lax.axis_size("dp") * fsdp_count)
    block = lax.axis_index("dp") * fsdp_count + lax.axis_index("fsdp")
    picked = lax.dynamic_slice_in_dim(every, block * own_rows, own_rows, 1)
    return lax.dot_general(
        picked * (1.0 / every.shape[0]),
        every,
        (((0,), (0,)), ((), ())),
        precision=lax.Precision.HIGHEST,
        preferred_element_type=jnp.float32,
    )


def line_plan(acts, out_grad, gate_pre, down_weight, proj_in, proj_out, lengths):
    x, z, column = lax.axis_index("groups"), lax.axis_index("dp"), lax.axis_index("fsdp")
    inner = (z == 1) | (z == 2)
    near_block, far_block = jnp.where(z < 2, 2, 1), jnp.where(z < 2, 3, 0)
    place = jnp.stack(
        [x, z, z ^ 1, near_block, jnp.where(inner, far_block, near_block), inner.astype(jnp.int32)]
    ).astype(jnp.int32)
    tokens_dev, width = out_grad.shape
    hidden = down_weight.shape[0] // 2
    rank = proj_out.shape[0]

    own_weight = lax.dynamic_slice_in_dim(down_weight, x * hidden, hidden, 0)
    mate_weight = lax.ppermute(own_weight, "dp", MATES)
    near_weight = lax.ppermute(own_weight, "dp", ACROSS)
    grads = lax.all_gather(out_grad, ("groups", "fsdp"), axis=0)
    gate_self = lax.dynamic_slice_in_dim(gate_pre, x * hidden, hidden, 1)
    gate_other = lax.dynamic_slice_in_dim(gate_pre, (1 - x) * hidden, hidden, 1)
    gates = jnp.concatenate([gate_self, lax.ppermute(gate_other, "groups", [(0, 1), (1, 0)])])
    factors_in = lax.psum(dot_nt(acts, proj_in), "fsdp")

    mate_weight, near_weight, gates, grads = lax.optimization_barrier((mate_weight, near_weight, gates, grads))
    piece_rows = tokens_dev // lax.axis_size("fsdp")
    piece = lax.dynamic_slice(
        grads, (x * 4 + far_block, column * piece_rows, 0), (1, piece_rows, width)
    )[0]
    piece = lax.ppermute(piece, "dp", INWARD)
    guest_grads = lax.all_gather(piece, ("groups", "fsdp"), axis=0, tiled=True).reshape(2, tokens_dev, width)
    part = early_part(place, grads, down_weight, mate_weight, near_weight)
    sums = jnp.zeros((2 * tokens_dev, 2 * rank), jnp.float32)
    for chunk in range(hidden // CHUNK):
        rows = slice(chunk * CHUNK, (chunk + 1) * CHUNK)
        far = lax.ppermute(mate_weight[rows], "dp", ACROSS)
        out = lax.ppermute(near_weight[rows], "dp", OUTWARD)
        guest_gates = lax.ppermute(gates[:, rows], "dp", INWARD)
        sums = late_part(place, chunk, part, grads, far, out, gates, guest_grads, guest_gates, proj_out, sums)

    mine = sums[:, :rank] + lax.ppermute(sums[:, rank:], "dp", OUTWARD)
    mine = mine[:tokens_dev] + lax.ppermute(mine[tokens_dev:], "groups", [(0, 1), (1, 0)])
    factors_out = lax.psum(mine, "fsdp")
    return own_fisher(example_sums(lengths[0], factors_in, factors_out))


def ring_plan(acts, out_grad, gate_pre, down_weight, proj_in, proj_out, lengths):
    full_grad = lax.all_gather(out_grad, "fsdp", axis=1, tiled=True)
    upstream = dot_nt(full_grad, lax.all_gather(down_weight, "dp", axis=1, tiled=True))
    up_grad = (upstream * jax.nn.silu(gate_pre.astype(jnp.float32))).astype(jnp.bfloat16)
    rank_in = proj_in.shape[0]
    joined = lax.psum(jnp.concatenate([dot_nt(acts, proj_in), dot_nt(up_grad, proj_out)], axis=1), "fsdp")
    return own_fisher(example_sums(lengths[0], joined[:, :rank_in], joined[:, rank_in:]))


def solution(mesh):
    placed = (
        P(("groups", "dp"), "fsdp"),
        P(("groups", "dp"), "fsdp"),
        P(("groups", "dp"), "fsdp"),
        P("fsdp", "dp"),
        P(None, "fsdp"),
        P(None, "fsdp"),
        P(("groups", "dp"), None),
    )
    line = (mesh.shape["groups"], mesh.shape["dp"], mesh.shape["fsdp"]) == (2, 4, 4)
    return jax.shard_map(
        line_plan if line else ring_plan,
        mesh=mesh,
        in_specs=placed,
        out_specs=P(("groups", "dp", "fsdp"), None),
        check_vma=False,
    )
```

time: 1490 us -> 672 us (0.45)
  waiting for transfers between devices: 1380 us -> 354 us
  Pallas kernels: 0 us -> 167 us
  matrix products: 93 us -> 15 us
  starting transfers between devices: 0.3 us -> 71.6 us
  local copies, waits for them, and re-layouts: 1.66 us -> 42.4 us
    all_gather x2 -> x3, waiting for transfers between devices: 1070 us -> 66.4 us  [the longest x1 38.3 us: line_plan(): grads = lax.all_gather(out_grad, ('groups', 'fsdp'), axis=0)]
    reduce_scatter x1 -> x0, waiting for transfers between devices: 280 us -> none  [per_device(): lax.psum_scatter(product * norm_scale, 'dp', scatter_dimension=0, tiled=T...]
    ppermute x0 -> x27, waiting for transfers between devices: none -> 254 us  [the longest x1 130 us: line_plan(): lax.ppermute(gate_other, 'groups', [(0, 1), (1, 0)])]
    pallas_call x0 -> x8, Pallas kernels: none -> 167 us  [the longest x7 114 us: late_part(): pl.pallas_call(late_kernel, grid_spec=pltpu.PrefetchScalarGridSpec(num_sc...]
    dot_general x5 -> x3, matrix products: 93 us -> 15 us  [the longest x1 6.8 us: own_fisher(): lax.dot_general(picked * (1.0 / every.shape[0]), every, (((0,), (0,)), ((...]
    ppermute x0 -> x27, starting transfers between devices: none -> 71.2 us  [the longest x7 42.3 us: line_plan(): guest_gates = lax.ppermute(gates[:, rows], 'dp', INWARD)]
    slice x1 -> x6, local copies, waits for them, and re-layouts: 0.95 us -> 19 us  [the longest x1 6.2 us: line_plan(): far = lax.ppermute(mate_weight[rows], 'dp', ACROSS)]
  transfers between devices with their start and end apart: 4 -> 31, of which waited for: 4 -> 14; matrix products, arithmetic and copies ran while one was open for 0% -> 6% of each run, Pallas kernels for 0% -> 22%
where the time goes in v1:
time: 672 us; the launch traced here: 671 us
  waiting for transfers between devices  354 us (53%)
  Pallas kernels  167 us (25%)
  starting transfers between devices  71.6 us (11%)
  local copies, waits for them, and re-layouts  42.4 us (6%)
  matrix products  15 us (2%)
  between operations  13.6 us (2%)
  other arithmetic  7.31 us (1%)
    ppermute x1, waiting for transfers between devices, line_plan(): lax.ppermute(gate_other, 'groups', [(0, 1), (1, 0)])  130 us
    pallas_call x7, Pallas kernels, late_part(): pl.pallas_call(late_kernel, grid_spec=pltpu.PrefetchScalarGridSpec(num_sc...  114 us
    ppermute x7, waiting for transfers between devices, line_plan(): guest_gates = lax.ppermute(gates[:, rows], 'dp', INWARD)  79.4 us
    pallas_call x1, Pallas kernels, early_part(): pl.pallas_call(early_kernel, grid_spec=pltpu.PrefetchScalarGridSpec(num_s...  53.2 us
    ppermute x7, starting transfers between devices, line_plan(): guest_gates = lax.ppermute(gates[:, rows], 'dp', INWARD)  42.3 us
    all_gather x1, waiting for transfers between devices, line_plan(): grads = lax.all_gather(out_grad, ('groups', 'fsdp'), axis=0)  38.3 us
    psum x1, waiting for transfers between devices, line_plan(): factors_in = lax.psum(dot_nt(acts, proj_in), 'fsdp')  32.8 us
    all_gather x1, waiting for transfers between devices, own_fisher(): every = lax.all_gather(example_grads, 'dp', axis=0, tiled=True)  28.1 us
  transfers between devices with their start and end apart: 31, of which 14 were waited for; matrix products, arithmetic and copies ran while one was open for 6% of the time, Pallas kernels for 22%

profile of v1, /device:TPU:0, one launch (start us, length us, event | category | flops | bytes accessed | tf_op | source)
XLA Modules:
  0.0 671.0 jit_solution(8204131672534580193)
XLA Ops:
  7.3 7.5 %constant_dynamic-slice_fusion.2 = bf16[1792,2048]{1,0:T(8,128)(2,1)} fusion(bf16[3584,2048]{1,0:T(8,128)(2,1)} %own_ref.1, s32[]{:T(128)S(6)} %select_n.30), kind=kLoop, calls=%fused_computation.20 | loop fusion | bytes 14680068 | tf_op jit(solution)/shard_map/dynamic_slice | solution.py:173
  14.8 3.0 collective-permute-start
  17.8 4.6 collective-permute-start.1
  22.4 6.0 constant_dynamic-slice_fusion.1
  28.4 1.4 collective-permute-start.2
  29.8 130.4 %collective-permute-done.2 = bf16[896,1792]{1,0:T(8,128)(2,1)} collective-permute-done((bf16[896,1792]{1,0:T(8,128)(2,1)}, bf16[896,1792]{1,0:T(8,128)(2,1)}, u32[]{:S(2)}, u32[]{:S(2)}) %collective-permute-start.2) | collective-permute-done | bytes 3211296 | tf_op jit(solution)/shard_map/ppermute | solution.py:179
  160.2 5.0 pad_maximum_fusion.gate_ref
  165.2 10.9 %collective-permute-done.mate_ref = bf16[1792,2048]{1,0:T(8,128)(2,1)} collective-permute-done((bf16[1792,2048]{1,0:T(8,128)(2,1)}, bf16[1792,2048]{1,0:T(8,128)(2,1)}, u32[]{:S(2)}, u32[]{:S(2)}) %collective-permute-start) | collective-permute-done | bytes 7340064 | tf_op jit(solution)/shard_map/ppermute | solution.py:174
  176.1 38.3 %all-gather.9.cloned.1.call-done = bf16[7168,2048]{1,0:T(8,128)(2,1)} async-done(((bf16[896,2048]{1,0:T(8,128)(2,1)}), bf16[7168,2048]{1,0:T(8,128)(2,1)}) %all-gather.9.cloned.1.call-update) | async-done | bytes 29360144 | tf_op jit(solution)/shard_map/all_gather | solution.py:176
  215.7 3.4 collective-permute-start.5
  219.2 20.0 %collective-permute-done.5 = bf16[224,2048]{1,0:T(8,128)(2,1)S(1)} collective-permute-done((bf16[224,2048]{1,0:T(8,128)(2,1)S(1)}, bf16[224,2048]{1,0:T(8,128)(2,1)S(1)}, u32[]{:S(2)}, u32[]{:S(2)}) %collective-permute-start.5) | collective-permute-done | bytes 917536 | tf_op jit(solution)/shard_map/ppermute | solution.py:187
  240.1 4.9 fusion.15
  245.0 5.3 collective-permute-start.9
  250.3 2.2 collective-permute-start.12
  252.5 2.2 collective-permute-start.15
  254.8 6.2 fusion.14
  262.4 7.7 %collective-permute-done.9.guest_gate_ref = bf16[1792,256]{1,0:T(8,128)(2,1)} collective-permute-done((bf16[1792,256]{1,0:T(8,128)(2,1)S(1)}, bf16[1792,256]{1,0:T(8,128)(2,1)}, u32[]{:S(2)}, u32[]{:S(2)}) %collective-permute-start.9) | collective-permute-done | bytes 917536 | tf_op jit(solution)/shard_map/ppermute | solution.py:195
  270.2 4.5 collective-permute-start.18
  274.7 15.1 %collective-permute-done.12.guest_gate_ref = bf16[1792,256]{1,0:T(8,128)(2,1)} collective-permute-done((bf16[1792,256]{1,0:T(8,128)(2,1)S(1)}, bf16[1792,256]{1,0:T(8,128)(2,1)}, u32[]{:S(2)}, u32[]{:S(2)}) %collective-permute-start.12) | collective-permute-done | bytes 917536 | tf_op jit(solution)/shard_map/ppermute | solution.py:195
  289.8 5.5 collective-permute-start.21
  295.3 14.2 %collective-permute-done.15.guest_gate_ref = bf16[1792,256]{1,0:T(8,128)(2,1)} collective-permute-done((bf16[1792,256]{1,0:T(8,128)(2,1)S(1)}, bf16[1792,256]{1,0:T(8,128)(2,1)}, u32[]{:S(2)}, u32[]{:S(2)}) %collective-permute-start.15) | collective-permute-done | bytes 917536 | tf_op jit(solution)/shard_map/ppermute | solution.py:195
  309.5 5.5 collective-permute-start.24
  315.6 6.2 fusion.13
  321.7 7.5 %collective-permute-done.18.guest_gate_ref = bf16[1792,256]{1,0:T(8,128)(2,1)S(1)} collective-permute-done((bf16[1792,256]{1,0:T(8,128)(2,1)}, bf16[1792,256]{1,0:T(8,128)(2,1)S(1)}, u32[]{:S(2)}, u32[]{:S(2)}) %collective-permute-start.18) | collective-permute-done | bytes 917536 | tf_op jit(solution)/shard_map/ppermute | solution.py:195
  330.9 18.0 %collective-permute-done.21.guest_gate_ref = bf16[1792,256]{1,0:T(8,128)(2,1)} collective-permute-done((bf16[1792,256]{1,0:T(8,128)(2,1)}, bf16[1792,256]{1,0:T(8,128)(2,1)}, u32[]{:S(2)}, u32[]{:S(2)}) %collective-permute-start.21) | collective-permute-done | bytes 917536 | tf_op jit(solution)/shard_map/ppermute | solution.py:195
  350.2 16.8 %collective-permute-done.24.guest_gate_ref = bf16[1792,256]{1,0:T(8,128)(2,1)} collective-permute-done((bf16[1792,256]{1,0:T(8,128)(2,1)}, bf16[1792,256]{1,0:T(8,128)(2,1)}, u32[]{:S(2)}, u32[]{:S(2)}) %collective-permute-start.24) | collective-permute-done | bytes 917536 | tf_op jit(solution)/shard_map/ppermute | solution.py:195
  369.1 1.5 collective-permute-start.23
  370.5 53.2 %early_part.1.part_ref = f32[1792,1792]{1,0:T(8,128)} custom-call(s32[6]{0:T(128)} %stack.31.place, bf16[8,896,2048]{2,1,0:T(8,128)(2,1)} %bitcast.20, bf16[3584,2048]{1,0:T(8,128)(2,1)} %own_ref.1, bf16[1792,2048]{1,0:T(8,128)(2,1)} %collective-permute-done.mate_ref, bf16[1792,2048]{1,0:T(8,128)(2,1)} %collective-permute-done.1.near_ref), custom_call_target="tpu_custom_call" | custom-call | flops 39460012032 | bytes 56885248 | tf_op jit(solution)/shard_map/early_part/pallas_call | solution.py:44
  423.7 1.3 collective-permute-start.11
  426.8 1.5 collective-permute-start.14
  429.3 16.2 %late_part.7.sum_ref = f32[1792,128]{1,0:T(8,128)} custom-call(s32[6]{0:T(128)} %stack.31.place, f32[1792,1792]{1,0:T(8,128)} %early_part.1.part_ref, bf16[8,896,2048]{2,1,0:T(8,128)(2,1)} %bitcast.21, bf16[256,2048]{1,0:T(8,128)(2,1)} %copy-done.10, bf16[256,2048]{1,0:T(8,128)(2,1)} %collective-permute-done.23.out_ref, ...), custom_call_target="tpu_custom_call", output_to_operand_aliasing={{}: (9, {})} | custom-call | flops 3992977408 | bytes 20447232 | tf_op jit(solution)/shard_map/late_part/pallas_call | solution.py:101
  445.6 16.2 %late_part.8.sum_ref = f32[1792,128]{1,0:T(8,128)} custom-call(s32[6]{0:T(128)} %stack.31.place, f32[1792,1792]{1,0:T(8,128)} %early_part.1.part_ref, bf16[8,896,2048]{2,1,0:T(8,128)(2,1)} %bitcast.22, bf16[256,2048]{1,0:T(8,128)(2,1)} %copy-done.2, bf16[256,2048]{1,0:T(8,128)(2,1)} %copy-done.8, ...), custom_call_target="tpu_custom_call", output_to_operand_aliasing={{}: (9, {})} | custom-call | flops 3992977408 | bytes 20447232 | tf_op jit(solution)/shard_map/late_part/pallas_call | solution.py:101
  462.5 1.3 collective-permute-start.8
  463.9 16.2 %late_part.9.sum_ref = f32[1792,128]{1,0:T(8,128)} custom-call(s32[6]{0:T(128)} %stack.31.place, f32[1792,1792]{1,0:T(8,128)} %early_part.1.part_ref, bf16[8,896,2048]{2,1,0:T(8,128)(2,1)} %bitcast.23, bf16[256,2048]{1,0:T(8,128)(2,1)} %copy-done.3, bf16[256,2048]{1,0:T(8,128)(2,1)} %collective-permute-done.17.out_ref, ...), custom_call_target="tpu_custom_call", output_to_operand_aliasing={{}: (9, {})} | custom-call | flops 3992977408 | bytes 20447232 | tf_op jit(solution)/shard_map/late_part/pallas_call | solution.py:101
  482.2 17.1 %collective-permute-start.6 = (bf16[1792,256]{1,0:T(8,128)(2,1)}, bf16[1792,256]{1,0:T(8,128)(2,1)}, u32[]{:S(2)}, u32[]{:S(2)}) collective-permute-start(bf16[1792,256]{1,0:T(8,128)(2,1)} %get-tuple-element.35), channel_id=1, source_target_pairs={{0,4},{12,8},{1,5},{13,9},{2,6},{14,10},{3,7},{15,11},{16,20},{28,... | collective-permute-start | bytes 2752520 | tf_op jit(solution)/shard_map/ppermute | solution.py:195
  499.2 16.2 %late_part.10.sum_ref = f32[1792,128]{1,0:T(8,128)} custom-call(s32[6]{0:T(128)} %stack.31.place, f32[1792,1792]{1,0:T(8,128)} %early_part.1.part_ref, bf16[8,896,2048]{2,1,0:T(8,128)(2,1)} %bitcast.24, bf16[256,2048]{1,0:T(8,128)(2,1)} %copy-done.5, bf16[256,2048]{1,0:T(8,128)(2,1)} %collective-permute-done.14.out_ref, ...), custom_call_target="tpu_custom_call", output_to_operand_aliasing={{}: (9, {})} | custom-call | flops 3992977408 | bytes 20447232 | tf_op jit(solution)/shard_map/late_part/pallas_call | solution.py:101
  515.5 16.2 %late_part.11.sum_ref = f32[1792,128]{1,0:T(8,128)} custom-call(s32[6]{0:T(128)} %stack.31.place, f32[1792,1792]{1,0:T(8,128)} %early_part.1.part_ref, bf16[8,896,2048]{2,1,0:T(8,128)(2,1)} %bitcast.25, bf16[256,2048]{1,0:T(8,128)(2,1)} %copy-done.1, bf16[256,2048]{1,0:T(8,128)(2,1)} %copy-done.4, ...), custom_call_target="tpu_custom_call", output_to_operand_aliasing={{}: (9, {})} | custom-call | flops 3992977408 | bytes 20447232 | tf_op jit(solution)/shard_map/late_part/pallas_call | solution.py:101
  532.7 16.2 %late_part.12.sum_ref = f32[1792,128]{1,0:T(8,128)} custom-call(s32[6]{0:T(128)} %stack.31.place, f32[1792,1792]{1,0:T(8,128)} %early_part.1.part_ref, bf16[8,896,2048]{2,1,0:T(8,128)(2,1)} %bitcast.26, bf16[256,2048]{1,0:T(8,128)(2,1)} %copy-done.6, bf16[256,2048]{1,0:T(8,128)(2,1)} %collective-permute-done.8.out_ref, ...), custom_call_target="tpu_custom_call", output_to_operand_aliasing={{}: (9, {})} | custom-call | flops 3992977408 | bytes 20447232 | tf_op jit(solution)/shard_map/late_part/pallas_call | solution.py:101
  550.9 16.2 %late_part.13 = f32[1792,128]{1,0:T(8,128)} custom-call(s32[6]{0:T(128)} %stack.31.place, f32[1792,1792]{1,0:T(8,128)} %early_part.1.part_ref, bf16[8,896,2048]{2,1,0:T(8,128)(2,1)} %bitcast.27, bf16[256,2048]{1,0:T(8,128)(2,1)} %copy-done.7, bf16[256,2048]{1,0:T(8,128)(2,1)} %copy-done.9, ...), custom_call_target="tpu_custom_call", output_to_operand_aliasing={{}: (9, {})} | custom-call | flops 3992977408 | bytes 20447232 | tf_op jit(solution)/shard_map/late_part/pallas_call | solution.py:101
  567.1 1.5 slice.101
  568.9 1.3 collective-permute-start.25
  570.4 9.7 %collective-permute-done.25 = f32[1792,64]{0,1:T(8,128)S(1)} collective-permute-done((f32[1792,64]{0,1:T(8,128)S(1)}, f32[1792,64]{0,1:T(8,128)S(1)}, u32[]{:S(2)}, u32[]{:S(2)}) %collective-permute-start.25) | collective-permute-done | bytes 458784 | tf_op jit(solution)/shard_map/ppermute | solution.py:198
  582.4 3.9 fusion.16
  586.3 4.0 collective-permute-done.26
  591.6 32.8 %all-reduce.3.cloned.1.call-done = (f32[896,64]{0,1:T(8,128)}, f32[896,64]{1,0:T(8,128)}) async-done(((f32[896,64]{0,1:T(8,128)}, f32[896,64]{1,0:T(8,128)}), (f32[896,64]{0,1:T(8,128)}, f32[896,64]{1,0:T(8,128)})) %all-reduce.3.cloned.1.call-update) | async-done | bytes 458768 | tf_op jit(solution)/shard_map/psum | solution.py:180
  624.4 4.3 fusion
  629.6 28.1 %all-gather.7.cloned.1.call-done = f32[64,4096]{1,0:T(8,128)} async-done(((f32[16,4096]{1,0:T(8,128)}), f32[64,4096]{1,0:T(8,128)}) %all-gather.7.cloned.1.call-update) | async-done | bytes 1048592 | tf_op jit(solution)/shard_map/all_gather | solution.py:148
  657.7 6.8 %fusion.5 = f32[256,4096]{1,0:T(8,128)} fusion(f32[64,4096]{1,0:T(8,128)} %all-gather.7.cloned.1.call-done, s32[]{:T(128)S(6)} %select_n.34), kind=kOutput, calls=%fused_computation.9 | convolution fusion | flops 805322752 | bytes 5308420 | tf_op jit(solution)/shard_map/dot_general | solution.py:153
  (78 shorter events, 23.3 us)
Async XLA Ops:
  6.5 575.9 %copy-start = (bf16[64,2048]{1,0:T(8,128)(2,1)S(1)}, bf16[64,2048]{1,0:T(8,128)(2,1)}, u32[]{:S(2)}) copy-start(bf16[64,2048]{1,0:T(8,128)(2,1)} %param.11) | copy-start | bytes 786436
  6.5 207.9 %all-gather.9.cloned.1.call-start = ((), (), s32[]{:S(2)}) async-start(), calls=%async_computation.2 | async-start | bytes 33030144 | tf_op jit(solution)/shard_map/all_gather | solution.py:176
  7.3 421.1 %all-gather.5.cloned.1.call-start = ((), (), s32[]{:S(2)}) async-start(), calls=%async_computation | async-start | bytes 8257536 | tf_op jit(solution)/shard_map/all_gather | solution.py:188
  14.8 161.3 %collective-permute-start = (bf16[1792,2048]{1,0:T(8,128)(2,1)}, bf16[1792,2048]{1,0:T(8,128)(2,1)}, u32[]{:S(2)}, u32[]{:S(2)}) collective-permute-start(bf16[1792,2048]{1,0:T(8,128)(2,1)} %constant_dynamic-slice_fusion.2), channel_id=1, source_target_pairs={{0,4},{4,0},{8,12},{12,8},{1,5},{5,1},{9,13},{13,9},{2,6},{6,2},{1... | collective-permute-start | bytes 22020104 | tf_op jit(solution)/shard_map/ppermute | solution.py:174
  17.8 158.3 %collective-permute-start.1 = (bf16[1792,2048]{1,0:T(8,128)(2,1)}, bf16[1792,2048]{1,0:T(8,128)(2,1)}, u32[]{:S(2)}, u32[]{:S(2)}) collective-permute-start(bf16[1792,2048]{1,0:T(8,128)(2,1)} %constant_dynamic-slice_fusion.2), channel_id=1, source_target_pairs={{4,8},{8,4},{5,9},{9,5},{6,10},{10,6},{7,11},{11,7},{20,24},{24,20... | collective-permute-start | bytes 22020104 | tf_op jit(solution)/shard_map/ppermute | solution.py:175
  28.4 131.9 %collective-permute-start.2 = (bf16[896,1792]{1,0:T(8,128)(2,1)}, bf16[896,1792]{1,0:T(8,128)(2,1)}, u32[]{:S(2)}, u32[]{:S(2)}) collective-permute-start(bf16[896,1792]{1,0:T(8,128)(2,1)} %get-tuple-element.37), channel_id=1, source_target_pairs={{0,16},{16,0},{1,17},{17,1},{2,18},{18,2},{3,19},{19,3},{4,20},{20... | collective-permute-start | bytes 9633800 | tf_op jit(solution)/shard_map/ppermute | solution.py:179
  215.7 23.4 %collective-permute-start.5 = (bf16[224,2048]{1,0:T(8,128)(2,1)S(1)}, bf16[224,2048]{1,0:T(8,128)(2,1)S(1)}, u32[]{:S(2)}, u32[]{:S(2)}) collective-permute-start(bf16[224,2048]{1,0:T(8,128)(2,1)S(1)} %dynamic-slice_bitcast_fusion), channel_id=1, source_target_pairs={{0,4},{12,8},{1,5},{13,9},{2,6},{14,10},{3,7},{15,11},{16,20},{28,... | collective-permute-start | bytes 2752520 | tf_op jit(solution)/shard_map/ppermute | solution.py:187
  239.1 0.9 copy-start.12
  240.1 384.3 %all-reduce.3.cloned.1.call-start = ((), (), s32[]{:S(2)}) async-start(), calls=%async_computation.3 | async-start | bytes 1376256 | tf_op jit(solution)/shard_map/psum | solution.py:180
  245.0 25.2 %collective-permute-start.9 = (bf16[1792,256]{1,0:T(8,128)(2,1)S(1)}, bf16[1792,256]{1,0:T(8,128)(2,1)}, u32[]{:S(2)}, u32[]{:S(2)}) collective-permute-start(bf16[1792,256]{1,0:T(8,128)(2,1)S(1)} %get-tuple-element.34), channel_id=1, source_target_pairs={{0,4},{12,8},{1,5},{13,9},{2,6},{14,10},{3,7},{15,11},{16,20},{28,... | collective-permute-start | bytes 2752520 | tf_op jit(solution)/shard_map/ppermute | solution.py:195
  250.3 39.5 %collective-permute-start.12 = (bf16[1792,256]{1,0:T(8,128)(2,1)S(1)}, bf16[1792,256]{1,0:T(8,128)(2,1)}, u32[]{:S(2)}, u32[]{:S(2)}) collective-permute-start(bf16[1792,256]{1,0:T(8,128)(2,1)S(1)} %get-tuple-element.33), channel_id=1, source_target_pairs={{0,4},{12,8},{1,5},{13,9},{2,6},{14,10},{3,7},{15,11},{16,20},{28,... | collective-permute-start | bytes 2752520 | tf_op jit(solution)/shard_map/ppermute | solution.py:195
  252.5 56.9 %collective-permute-start.15 = (bf16[1792,256]{1,0:T(8,128)(2,1)S(1)}, bf16[1792,256]{1,0:T(8,128)(2,1)}, u32[]{:S(2)}, u32[]{:S(2)}) collective-permute-start(bf16[1792,256]{1,0:T(8,128)(2,1)S(1)} %get-tuple-element.32), channel_id=1, source_target_pairs={{0,4},{12,8},{1,5},{13,9},{2,6},{14,10},{3,7},{15,11},{16,20},{28,... | collective-permute-start | bytes 2752520 | tf_op jit(solution)/shard_map/ppermute | solution.py:195
  261.0 107.3 %collective-permute-start.10 = (bf16[256,2048]{1,0:T(8,128)(2,1)}, bf16[256,2048]{1,0:T(8,128)(2,1)S(1)}, u32[]{:S(2)}, u32[]{:S(2)}) collective-permute-start(bf16[256,2048]{1,0:T(8,128)(2,1)} %get-tuple-element.26), channel_id=1, source_target_pairs={{4,8},{8,4},{5,9},{9,5},{6,10},{10,6},{7,11},{11,7},{20,24},{24,20... | collective-permute-start | bytes 3145736 | tf_op jit(solution)/shard_map/ppermute | solution.py:193
  261.7 107.4 %collective-permute-start.19 = (bf16[256,2048]{1,0:T(8,128)(2,1)}, bf16[256,2048]{1,0:T(8,128)(2,1)S(1)}, u32[]{:S(2)}, u32[]{:S(2)}) collective-permute-start(bf16[256,2048]{1,0:T(8,128)(2,1)} %get-tuple-element.23), channel_id=1, source_target_pairs={{4,8},{8,4},{5,9},{9,5},{6,10},{10,6},{7,11},{11,7},{20,24},{24,20... | collective-permute-start | bytes 3145736 | tf_op jit(solution)/shard_map/ppermute | solution.py:193
  270.2 59.1 %collective-permute-start.18 = (bf16[1792,256]{1,0:T(8,128)(2,1)}, bf16[1792,256]{1,0:T(8,128)(2,1)S(1)}, u32[]{:S(2)}, u32[]{:S(2)}) collective-permute-start(bf16[1792,256]{1,0:T(8,128)(2,1)} %get-tuple-element.31), channel_id=1, source_target_pairs={{0,4},{12,8},{1,5},{13,9},{2,6},{14,10},{3,7},{15,11},{16,20},{28,... | collective-permute-start | bytes 2752520 | tf_op jit(solution)/shard_map/ppermute | solution.py:195
  289.8 59.1 %collective-permute-start.21 = (bf16[1792,256]{1,0:T(8,128)(2,1)}, bf16[1792,256]{1,0:T(8,128)(2,1)}, u32[]{:S(2)}, u32[]{:S(2)}) collective-permute-start(bf16[1792,256]{1,0:T(8,128)(2,1)} %get-tuple-element.30), channel_id=1, source_target_pairs={{0,4},{12,8},{1,5},{13,9},{2,6},{14,10},{3,7},{15,11},{16,20},{28,... | collective-permute-start | bytes 2752520 | tf_op jit(solution)/shard_map/ppermute | solution.py:195
  309.5 57.5 %collective-permute-start.24 = (bf16[1792,256]{1,0:T(8,128)(2,1)}, bf16[1792,256]{1,0:T(8,128)(2,1)}, u32[]{:S(2)}, u32[]{:S(2)}) collective-permute-start(bf16[1792,256]{1,0:T(8,128)(2,1)} %get-tuple-element.29), channel_id=1, source_target_pairs={{0,4},{12,8},{1,5},{13,9},{2,6},{14,10},{3,7},{15,11},{16,20},{28,... | collective-permute-start | bytes 2752520 | tf_op jit(solution)/shard_map/ppermute | solution.py:195
  329.3 0.9 copy-start.11
  330.2 131.6 %collective-permute-start.16 = (bf16[256,2048]{1,0:T(8,128)(2,1)}, bf16[256,2048]{1,0:T(8,128)(2,1)S(1)}, u32[]{:S(2)}, u32[]{:S(2)}) collective-permute-start(bf16[256,2048]{1,0:T(8,128)(2,1)} %get-tuple-element.24), channel_id=1, source_target_pairs={{4,8},{8,4},{5,9},{9,5},{6,10},{10,6},{7,11},{11,7},{20,24},{24,20... | collective-permute-start | bytes 3145736 | tf_op jit(solution)/shard_map/ppermute | solution.py:193
  348.9 113.6 %collective-permute-start.17 = (bf16[256,2048]{1,0:T(8,128)(2,1)}, bf16[256,2048]{1,0:T(8,128)(2,1)}, u32[]{:S(2)}, u32[]{:S(2)}) collective-permute-start(bf16[256,2048]{1,0:T(8,128)(2,1)} %get-tuple-element.17), channel_id=1, source_target_pairs={{4,0},{8,12},{5,1},{9,13},{6,2},{10,14},{7,3},{11,15},{20,16},{24,... | collective-permute-start | bytes 3145736 | tf_op jit(solution)/shard_map/ppermute | solution.py:194
  367.0 56.7 %collective-permute-start.20 = (bf16[256,2048]{1,0:T(8,128)(2,1)}, bf16[256,2048]{1,0:T(8,128)(2,1)S(1)}, u32[]{:S(2)}, u32[]{:S(2)}) collective-permute-start(bf16[256,2048]{1,0:T(8,128)(2,1)} %get-tuple-element.16), channel_id=1, source_target_pairs={{4,0},{8,12},{5,1},{9,13},{6,2},{10,14},{7,3},{11,15},{20,16},{24,... | collective-permute-start | bytes 3145736 | tf_op jit(solution)/shard_map/ppermute | solution.py:194
  368.3 55.4 %copy-start.1 = (bf16[256,2048]{1,0:T(8,128)(2,1)}, bf16[256,2048]{1,0:T(8,128)(2,1)S(1)}, u32[]{:S(2)}) copy-start(bf16[256,2048]{1,0:T(8,128)(2,1)S(1)} %collective-permute-done.10.far_ref) | copy-start | bytes 3145732
  368.3 56.7 %collective-permute-start.22 = (bf16[256,2048]{1,0:T(8,128)(2,1)}, bf16[256,2048]{1,0:T(8,128)(2,1)S(1)}, u32[]{:S(2)}, u32[]{:S(2)}) collective-permute-start(bf16[256,2048]{1,0:T(8,128)(2,1)} %get-tuple-element.22), channel_id=1, source_target_pairs={{4,8},{8,4},{5,9},{9,5},{6,10},{10,6},{7,11},{11,7},{20,24},{24,20... | collective-permute-start | bytes 3145736 | tf_op jit(solution)/shard_map/ppermute | solution.py:193
  369.0 54.7 %copy-start.2 = (bf16[256,2048]{1,0:T(8,128)(2,1)}, bf16[256,2048]{1,0:T(8,128)(2,1)S(1)}, u32[]{:S(2)}) copy-start(bf16[256,2048]{1,0:T(8,128)(2,1)S(1)} %collective-permute-done.19.far_ref) | copy-start | bytes 3145732
  369.1 57.7 %collective-permute-start.23 = (bf16[256,2048]{1,0:T(8,128)(2,1)}, bf16[256,2048]{1,0:T(8,128)(2,1)}, u32[]{:S(2)}, u32[]{:S(2)}) collective-permute-start(bf16[256,2048]{1,0:T(8,128)(2,1)} %get-tuple-element.15), channel_id=1, source_target_pairs={{4,0},{8,12},{5,1},{9,13},{6,2},{10,14},{7,3},{11,15},{20,16},{24,... | collective-permute-start | bytes 3145736 | tf_op jit(solution)/shard_map/ppermute | solution.py:194
  423.7 1.3 copy-start.8
  423.7 56.3 %collective-permute-start.11 = (bf16[256,2048]{1,0:T(8,128)(2,1)}, bf16[256,2048]{1,0:T(8,128)(2,1)S(1)}, u32[]{:S(2)}, u32[]{:S(2)}) collective-permute-start(bf16[256,2048]{1,0:T(8,128)(2,1)} %get-tuple-element.19), channel_id=1, source_target_pairs={{4,0},{8,12},{5,1},{9,13},{6,2},{10,14},{7,3},{11,15},{20,16},{24,... | collective-permute-start | bytes 3145736 | tf_op jit(solution)/shard_map/ppermute | solution.py:194
  425.1 1.0 copy-start.10
  426.0 54.8 %collective-permute-start.13 = (bf16[256,2048]{1,0:T(8,128)(2,1)}, bf16[256,2048]{1,0:T(8,128)(2,1)S(1)}, u32[]{:S(2)}, u32[]{:S(2)}) collective-permute-start(bf16[256,2048]{1,0:T(8,128)(2,1)} %get-tuple-element.25), channel_id=1, source_target_pairs={{4,8},{8,4},{5,9},{9,5},{6,10},{10,6},{7,11},{11,7},{20,24},{24,20... | collective-permute-start | bytes 3145736 | tf_op jit(solution)/shard_map/ppermute | solution.py:193
  426.8 55.4 %collective-permute-start.14 = (bf16[256,2048]{1,0:T(8,128)(2,1)}, bf16[256,2048]{1,0:T(8,128)(2,1)}, u32[]{:S(2)}, u32[]{:S(2)}) collective-permute-start(bf16[256,2048]{1,0:T(8,128)(2,1)} %get-tuple-element.18), channel_id=1, source_target_pairs={{4,0},{8,12},{5,1},{9,13},{6,2},{10,14},{7,3},{11,15},{20,16},{24,... | collective-permute-start | bytes 3145736 | tf_op jit(solution)/shard_map/ppermute | solution.py:194
  461.8 2.1 copy-start.3
  461.8 69.9 %collective-permute-start.7 = (bf16[256,2048]{1,0:T(8,128)(2,1)}, bf16[256,2048]{1,0:T(8,128)(2,1)S(1)}, u32[]{:S(2)}, u32[]{:S(2)}) collective-permute-start(bf16[256,2048]{1,0:T(8,128)(2,1)} %get-tuple-element.27), channel_id=1, source_target_pairs={{4,8},{8,4},{5,9},{9,5},{6,10},{10,6},{7,11},{11,7},{20,24},{24,20... | collective-permute-start | bytes 3145736 | tf_op jit(solution)/shard_map/ppermute | solution.py:193
  462.5 69.2 %collective-permute-start.8 = (bf16[256,2048]{1,0:T(8,128)(2,1)}, bf16[256,2048]{1,0:T(8,128)(2,1)}, u32[]{:S(2)}, u32[]{:S(2)}) collective-permute-start(bf16[256,2048]{1,0:T(8,128)(2,1)} %get-tuple-element.20), channel_id=1, source_target_pairs={{4,0},{8,12},{5,1},{9,13},{6,2},{10,14},{7,3},{11,15},{20,16},{24,... | collective-permute-start | bytes 3145736 | tf_op jit(solution)/shard_map/ppermute | solution.py:194
  480.1 35.4 %copy-start.4 = (bf16[256,2048]{1,0:T(8,128)(2,1)}, bf16[256,2048]{1,0:T(8,128)(2,1)S(1)}, u32[]{:S(2)}) copy-start(bf16[256,2048]{1,0:T(8,128)(2,1)S(1)} %collective-permute-done.11.out_ref) | copy-start | bytes 3145732
  480.1 68.8 %collective-permute-start.3 = (bf16[256,2048]{1,0:T(8,128)(2,1)}, bf16[256,2048]{1,0:T(8,128)(2,1)S(1)}, u32[]{:S(2)}, u32[]{:S(2)}) collective-permute-start(bf16[256,2048]{1,0:T(8,128)(2,1)} %get-tuple-element.28), channel_id=1, source_target_pairs={{4,8},{8,4},{5,9},{9,5},{6,10},{10,6},{7,11},{11,7},{20,24},{24,20... | collective-permute-start | bytes 3145736 | tf_op jit(solution)/shard_map/ppermute | solution.py:193
  480.9 18.4 %copy-start.5 = (bf16[256,2048]{1,0:T(8,128)(2,1)}, bf16[256,2048]{1,0:T(8,128)(2,1)S(1)}, u32[]{:S(2)}) copy-start(bf16[256,2048]{1,0:T(8,128)(2,1)S(1)} %collective-permute-done.13.far_ref) | copy-start | bytes 3145732
  480.9 68.1 %collective-permute-start.4 = (bf16[256,2048]{1,0:T(8,128)(2,1)}, bf16[256,2048]{1,0:T(8,128)(2,1)S(1)}, u32[]{:S(2)}, u32[]{:S(2)}) collective-permute-start(bf16[256,2048]{1,0:T(8,128)(2,1)} %get-tuple-element.21), channel_id=1, source_target_pairs={{4,0},{8,12},{5,1},{9,13},{6,2},{10,14},{7,3},{11,15},{20,16},{24,... | collective-permute-start | bytes 3145736 | tf_op jit(solution)/shard_map/ppermute | solution.py:194
  482.2 66.7 %collective-permute-start.6 = (bf16[1792,256]{1,0:T(8,128)(2,1)}, bf16[1792,256]{1,0:T(8,128)(2,1)}, u32[]{:S(2)}, u32[]{:S(2)}) collective-permute-start(bf16[1792,256]{1,0:T(8,128)(2,1)} %get-tuple-element.35), channel_id=1, source_target_pairs={{0,4},{12,8},{1,5},{13,9},{2,6},{14,10},{3,7},{15,11},{16,20},{28,... | collective-permute-start | bytes 2752520 | tf_op jit(solution)/shard_map/ppermute | solution.py:195
  531.7 1.0 copy-start.6
  548.9 21.3 %copy-start.13 = (s32[1,16]{1,0:T(1,128)S(1)}, s32[1,16]{1,0:T(1,128)}, u32[]{:S(2)}) copy-start(s32[1,16]{1,0:T(1,128)} %param.13) | copy-start | bytes 196
  548.9 1.0 copy-start.7
  549.9 1.0 copy-start.9
  568.9 11.3 %collective-permute-start.25 = (f32[1792,64]{0,1:T(8,128)S(1)}, f32[1792,64]{0,1:T(8,128)S(1)}, u32[]{:S(2)}, u32[]{:S(2)}) collective-permute-start(f32[1792,64]{0,1:T(8,128)S(1)} %copy.20), channel_id=1, source_target_pairs={{4,0},{8,12},{5,1},{9,13},{6,2},{10,14},{7,3},{11,15},{20,16},{24,... | collective-permute-start | bytes 1376264 | tf_op jit(solution)/shard_map/ppermute | solution.py:198
  581.8 8.5 %collective-permute-start.26 = (f32[896,64]{1,0:T(8,128)S(1)}, f32[896,64]{1,0:T(8,128)S(1)}, u32[]{:S(2)}, u32[]{:S(2)}) collective-permute-start(f32[896,64]{1,0:T(8,128)S(1)} %slice.103), channel_id=1, source_target_pairs={{0,16},{16,0},{1,17},{17,1},{2,18},{18,2},{3,19},{19,3},{4,20},{20... | collective-permute-start | bytes 688136 | tf_op jit(solution)/shard_map/ppermute | solution.py:199
  591.2 66.5 %all-gather.7.cloned.1.call-start = ((), (), s32[]{:S(2)}) async-start(), calls=%async_computation.1 | async-start | bytes 1310720 | tf_op jit(solution)/shard_map/all_gather | solution.py:148
Sparse Core Ops, SparseCore 0:
  9.2 205.1 all-gather.8
  240.2 50.0 all-gather.4
  591.3 33.0 all-reduce.2
  629.7 27.9 all-gather.6

commit v2 on v1

v2 whole, which is shorter than its diff:
```python
import functools

import jax
import jax.numpy as jnp
from jax import lax
from jax.experimental import pallas as pl
from jax.experimental.pallas import tpu as pltpu
from jax.sharding import PartitionSpec as P

MATES = [(0, 1), (1, 0), (2, 3), (3, 2)]
ACROSS = [(1, 2), (2, 1)]
OUTWARD = [(1, 0), (2, 3)]
INWARD = [(0, 1), (3, 2)]
SWAP = [(0, 1), (1, 0)]
UNIT = 256
FIRST_UNITS = 4
LATE = ((4, (1, 3)), (2, (2,)), (1, (1,)))
EARLY_COST = 2 * 10**7
LATE_COST = 1 << 20
VMEM_LIMIT = 58 * 1024 * 1024


def dot_nt(left, right):
    return lax.dot_general(left, right, (((1,), (1,)), ((), ())), preferred_element_type=jnp.float32)


def early_kernel(place, grad_ref, own_ref, mate_ref, near_ref, part_ref):
    step = pl.program_id(1)

    @pl.when(step == 0)
    def _():
        part_ref[...] = dot_nt(grad_ref[0], own_ref[...])

    @pl.when(step == 1)
    def _():
        part_ref[...] += dot_nt(grad_ref[0], mate_ref[...])

    @pl.when(step == 2)
    def _():
        part_ref[...] += dot_nt(grad_ref[0], near_ref[...])


def early_part(place, grads, own, mate, near):
    hidden, width = own.shape
    tokens_dev = grads.shape[1]
    tile = tokens_dev // 2
    whole = pl.BlockSpec((hidden, width), lambda i, k, place: (0, 0), pipeline_mode=pl.Buffered(1))
    return pl.pallas_call(
        early_kernel,
        grid_spec=pltpu.PrefetchScalarGridSpec(
            num_scalar_prefetch=1,
            grid=(tokens_dev // tile, 3),
            in_specs=[pl.BlockSpec((1, tile, width), lambda i, k, place: (place[1 + k], i, 0)), whole, whole, whole],
            out_specs=pl.BlockSpec((tile, hidden), lambda i, k, place: (i, 0)),
        ),
        out_shape=jax.ShapeDtypeStruct((tokens_dev, hidden), jnp.float32),
        compiler_params=pltpu.CompilerParams(vmem_limit_bytes=VMEM_LIMIT),
        cost_estimate=pl.CostEstimate(flops=EARLY_COST * hidden, bytes_accessed=0, transcendentals=0),
        name="early_part",
    )(place, grads, own, mate, near)


def pack_kernel(place, self_ref, other_ref, near_ref, packed_ref):
    inner = place[5] == 1

    @pl.when(inner)
    def _():
        packed_ref[...] = near_ref[...]

    @pl.when(jnp.logical_not(inner))
    def _():
        rows = packed_ref.shape[0] // 4
        count = packed_ref.shape[1] // UNIT
        for piece in range(4):
            source = self_ref if piece < 2 else other_ref
            for at in range(count):
                start = (piece % 2 * count + at) * rows
                packed_ref[piece * rows : (piece + 1) * rows, at * UNIT : (at + 1) * UNIT] = source[
                    start : start + rows, :
                ]


def pack(place, first, units, gates, near, near_first):
    tokens_dev = gates[0].shape[0]
    wide = 2 * tokens_dev
    gate = pl.BlockSpec((tokens_dev, UNIT), lambda i, place: (0, first + i))
    return pl.pallas_call(
        pack_kernel,
        grid_spec=pltpu.PrefetchScalarGridSpec(
            num_scalar_prefetch=1,
            grid=(units,),
            in_specs=[gate, gate, pl.BlockSpec((UNIT, wide), lambda i, place: (first - near_first + i, 0))],
            out_specs=pl.BlockSpec((UNIT, wide), lambda i, place: (i, 0)),
        ),
        out_shape=jax.ShapeDtypeStruct((units * UNIT, wide), near.dtype),
        compiler_params=pltpu.CompilerParams(vmem_limit_bytes=VMEM_LIMIT),
        cost_estimate=pl.CostEstimate(flops=0, bytes_accessed=1 << 20, transcendentals=0),
        name="pack",
    )(place, *gates, near)


def late_kernel(far_pieces, trade_pieces, per, place, *refs):
    refs = list(refs)
    take = lambda count: [refs.pop(0) for _ in range(count)]
    parts, grads, gate_refs, far_refs = take(2), take(2), take(2), take(far_pieces)
    guest_grad_ref, proj_ref, sum_ref, rest_ref = take(4)
    trade_refs = take(len(trade_pieces))
    packed_refs = take(sum(trade_pieces))
    (new_ref,) = refs
    inner = place[5] == 1
    rank = proj_ref.shape[0]
    step = pl.program_id(0)

    def project(upstream, gate, exact):
        gate = gate.astype(jnp.float32)
        up_grad = upstream * (gate / (1.0 + jnp.exp(-gate)))
        high = up_grad.astype(jnp.bfloat16)
        total = dot_nt(high, proj_ref[...])
        if exact:
            low = (up_grad - high.astype(jnp.float32)).astype(jnp.bfloat16)
            total = total + dot_nt(low, proj_ref[...])
        return total

    for group in range(2):

        @pl.when((step // per == group) & inner)
        def _(group=group):
            far = jnp.concatenate([ref[...] for ref in far_refs], axis=0)
            upstream = parts[group][...] + dot_nt(grads[group][0], far)
            new_ref[:, :rank] = sum_ref[:, :rank] + project(upstream, gate_refs[group][...], False)
            slabs = []
            for packed_ref in packed_refs:
                packed = packed_ref[...]
                slabs.append(
                    jnp.concatenate(
                        [packed[:, at : at + UNIT] for at in range(0, packed.shape[1], UNIT)], axis=0
                    )
                )
            guest = dot_nt(guest_grad_ref[0], far)
            new_ref[:, rank:] = sum_ref[:, rank:] + project(guest, jnp.concatenate(slabs, axis=1), True)

        @pl.when((step // per == group) & jnp.logical_not(inner))
        def _(group=group):
            weight = jnp.concatenate([ref[...] for ref in trade_refs], axis=0)
            weight = jnp.concatenate([weight, rest_ref[...]], axis=1)
            upstream = parts[group][...] + dot_nt(grads[group][0], weight)
            new_ref[:, :rank] = sum_ref[:, :rank] + project(upstream, gate_refs[group][...], True)
            new_ref[:, rank:] = sum_ref[:, rank:]


def late_part(place, first, base, parts, grads, fars, trades, rest, gates, guest_grads, proj_out, sums):
    tokens_dev, width = grads[0].shape[1:]
    tile = tokens_dev // 2
    per = tokens_dev // tile
    trade_pieces = tuple(trade.shape[0] // UNIT for trade in trades)
    units = sum(trade_pieces)
    wide = units * UNIT
    chunk, local = first // units, (first - base) // units
    trade_width = trades[0].shape[1]
    packed_rows = tile * UNIT // trade_width
    tiles = UNIT // packed_rows
    rank = proj_out.shape[0]
    at = (lambda i: jnp.minimum(i, per - 1), lambda i: jnp.maximum(i - per, 0))
    held = lambda array: pl.BlockSpec(array.shape, lambda i, place: (0, 0))
    summed = pl.BlockSpec((tile, 2 * rank), lambda i, place: ((i // per ^ place[0]) * per + i % per, 0))
    in_specs = (
        [pl.BlockSpec((tile, wide), lambda i, place, f=f: (f(i), local)) for f in at]
        + [pl.BlockSpec((1, tile, width), lambda i, place, f=f: (place[4], f(i), 0)) for f in at]
        + [pl.BlockSpec((tile, wide), lambda i, place, f=f: (f(i), chunk)) for f in at]
        + [held(far) for far in fars]
        + [
            pl.BlockSpec((1, tile, width), lambda i, place: (i // per ^ place[0], i % per, 0)),
            pl.BlockSpec((rank, wide), lambda i, place: (0, chunk)),
            summed,
            pl.BlockSpec((wide, rest.shape[1]), lambda i, place: (local, 0)),
        ]
        + [held(trade) for trade in trades]
        + [
            pl.BlockSpec((packed_rows, trade_width), lambda i, place, u=u: (u * tiles + i, 0))
            for pieces in trade_pieces
            for u in range(pieces)
        ]
    )
    return pl.pallas_call(
        functools.partial(late_kernel, len(fars), trade_pieces, per),
        grid_spec=pltpu.PrefetchScalarGridSpec(
            num_scalar_prefetch=1,
            grid=(2 * per,),
            in_specs=in_specs,
            out_specs=summed,
        ),
        out_shape=jax.ShapeDtypeStruct(sums.shape, jnp.float32),
        input_output_aliases={1 + 6 + len(fars) + 2: 0},
        compiler_params=pltpu.CompilerParams(vmem_limit_bytes=VMEM_LIMIT),
        cost_estimate=pl.CostEstimate(flops=LATE_COST, bytes_accessed=0, transcendentals=0),
        name="late_part",
    )(
        place, *parts, *grads, *gates, *fars, guest_grads, proj_out, sums, rest, *trades,
        *[trade for trade, pieces in zip(trades, trade_pieces) for _ in range(pieces)],
    )


def example_sums(counts, factors_in, factors_out):
    tok_rows = factors_in.shape[0]
    stop_at = jnp.cumsum(counts, dtype=jnp.int32)
    starts = stop_at - counts
    position = jnp.arange(tok_rows, dtype=jnp.int32)
    member = (
        (position[None, :] >= starts[:, None]) & (position[None, :] < stop_at[:, None])
    ).astype(jnp.float32)
    weighted = member[:, :, None] * factors_in[None, :, :]
    return jnp.einsum(
        "eti,tj->eij", weighted, factors_out, precision=lax.Precision.HIGHEST
    ).reshape(counts.shape[0], -1)


def own_fisher(example_grads):
    every = lax.all_gather(example_grads.astype(jnp.bfloat16), "dp", axis=0, tiled=True)
    fsdp_count = lax.axis_size("fsdp")
    own_rows = every.shape[1] // (lax.axis_size("dp") * fsdp_count)
    block = lax.axis_index("dp") * fsdp_count + lax.axis_index("fsdp")
    picked = lax.dynamic_slice_in_dim(every, block * own_rows, own_rows, 1)
    product = lax.dot_general(
        picked, every, (((0,), (0,)), ((), ())), preferred_element_type=jnp.float32
    )
    return product * (1.0 / every.shape[0])


def line_plan(acts, out_grad, gate_pre, down_weight, proj_in, proj_out, lengths):
    x, z, column = lax.axis_index("groups"), lax.axis_index("dp"), lax.axis_index("fsdp")
    inner = (z == 1) | (z == 2)
    near_block, far_block = jnp.where(z < 2, 2, 1), jnp.where(z < 2, 3, 0)
    place = jnp.stack(
        [x, z, z ^ 1, near_block, jnp.where(inner, far_block, near_block), inner.astype(jnp.int32)]
    ).astype(jnp.int32)
    tokens_dev, width = out_grad.shape
    hidden = down_weight.shape[0] // 2
    rank = proj_out.shape[0]
    cut = FIRST_UNITS * UNIT
    fsdp_count = lax.axis_size("fsdp")

    own_proj = lax.dynamic_slice_in_dim(proj_out, x * hidden, hidden, 1)
    own_first = lax.dynamic_slice_in_dim(down_weight, x * hidden, cut, 0)
    own_second = lax.dynamic_slice_in_dim(down_weight, x * hidden + cut, hidden - cut, 0)
    grads_self = lax.all_gather(out_grad, "fsdp", axis=0)
    grad_other = lax.ppermute(out_grad, "groups", SWAP)
    mate_first = lax.ppermute(own_first, "dp", MATES)
    near_first = lax.ppermute(own_first, "dp", ACROSS)
    gate_self = lax.dynamic_slice_in_dim(gate_pre, x * hidden, hidden, 1)
    gate_send = lax.dynamic_slice_in_dim(gate_pre, (1 - x) * hidden, hidden, 1)
    share_in = dot_nt(acts, proj_in)

    grads_self, grad_other, mate_first, near_first, gate_send, own_second, share_in = lax.optimization_barrier(
        (grads_self, grad_other, mate_first, near_first, gate_send, own_second, share_in)
    )
    mate_second = lax.ppermute(own_second, "dp", MATES)
    near_second = lax.ppermute(own_second, "dp", ACROSS)
    gate_other = lax.ppermute(gate_send, "groups", SWAP)
    grads_other = lax.all_gather(grad_other, "fsdp", axis=0)
    piece_rows = tokens_dev // fsdp_count
    piece = lax.dynamic_slice(grads_self, (far_block, column * piece_rows, 0), (1, piece_rows, width))[0]
    trade_width = 2 * tokens_dev
    lanes = width - trade_width
    slots = width // lanes
    slot_rows = cut // slots
    edge = near_first[:, trade_width:].reshape(slots, slot_rows, lanes).swapaxes(0, 1).reshape(slot_rows, width)
    edge = jnp.pad(edge, ((0, piece_rows - slot_rows), (0, 0)))
    piece = lax.ppermute(jnp.where(inner, edge, piece), "dp", MATES)
    far_start = lax.ppermute(mate_first[: LATE[0][1][0] * UNIT], "dp", ACROSS)
    part_self = early_part(place, grads_self, own_first, mate_first, near_first)

    mate_second, near_second, gate_other, piece, part_self, share_in, far_start = lax.optimization_barrier(
        (mate_second, near_second, gate_other, piece, part_self, share_in, far_start)
    )
    rest_first = piece[:slot_rows].reshape(slot_rows, slots, lanes).swapaxes(0, 1).reshape(cut, lanes)
    guest_grads = lax.all_gather(piece, ("groups", "fsdp"), axis=0, tiled=True).reshape(2, tokens_dev, width)
    factors_in = lax.psum(share_in, "fsdp")
    mates, nears = (mate_first, mate_second), (near_first, near_second)
    gates = (gate_self, gate_other)
    rests = (rest_first, lax.ppermute(near_second[:, trade_width:], "dp", OUTWARD))
    turn = place
    done = []
    parts_first, parts_second = [part_self], []
    for grads, share in ((grads_self, 1), (grads_other, 0), (grads_other, 1)):
        weights = (own_second, mate_second, near_second) if share else (own_first, mate_first, near_first)
        part = early_part(turn, grads, *weights)
        (parts_second if share else parts_first).append(part)
        done.append(part)
        turn, done[-1] = lax.optimization_barrier((place, part))
        (parts_second if share else parts_first)[-1] = done[-1]
    sums = jnp.zeros((2 * tokens_dev, 2 * rank), jnp.float32)

    def after(operand, order):
        return lax.optimization_barrier((operand, done[order - 1]))[0] if order else operand

    chunks = []
    first = 0
    for order, (units, far_pieces) in enumerate(LATE):
        half = int(first * UNIT >= cut)
        base = half * FIRST_UNITS
        fars = []
        at = first
        for count in far_pieces:
            if at:
                rows = after(mates[half][(at - base) * UNIT : (at - base + count) * UNIT], order)
                fars.append(lax.ppermute(rows, "dp", ACROSS))
            else:
                fars.append(far_start)
            at += count
        packed = pack(after(place, order), first, units, gates, nears[half], base)
        chunks.append((first, half, base, fars, lax.ppermute(packed, "dp", MATES)))
        first += units
    for first, half, base, fars, trade in chunks:
        if half and first == base:
            sums, factors_in = lax.optimization_barrier((sums, factors_in))
        sums = late_part(
            place, first, base, parts_second if half else parts_first, (grads_self, grads_other),
            fars, [trade], rests[half], gates, guest_grads, own_proj, sums,
        )

    spread = lax.all_to_all(
        sums.reshape(2 * fsdp_count, piece_rows, 2 * rank), ("groups", "fsdp"), split_axis=0, concat_axis=0
    ).sum(axis=0)
    mine = spread[:, :rank] + lax.ppermute(spread[:, rank:], "dp", OUTWARD)
    factors_out = lax.all_gather(mine, "fsdp", axis=0, tiled=True)
    return own_fisher(example_sums(lengths[0], factors_in, factors_out))


def ring_plan(acts, out_grad, gate_pre, down_weight, proj_in, proj_out, lengths):
    full_grad = lax.all_gather(out_grad, "fsdp", axis=1, tiled=True)
    upstream = dot_nt(full_grad, lax.all_gather(down_weight, "dp", axis=1, tiled=True))
    up_grad = (upstream * jax.nn.silu(gate_pre.astype(jnp.float32))).astype(jnp.bfloat16)
    rank_in = proj_in.shape[0]
    joined = lax.psum(jnp.concatenate([dot_nt(acts, proj_in), dot_nt(up_grad, proj_out)], axis=1), "fsdp")
    return own_fisher(example_sums(lengths[0], joined[:, :rank_in], joined[:, rank_in:]))


def solution(mesh):
    placed = (
        P(("groups", "dp"), "fsdp"),
        P(("groups", "dp"), "fsdp"),
        P(("groups", "dp"), "fsdp"),
        P("fsdp", "dp"),
        P(None, "fsdp"),
        P(None, "fsdp"),
        P(("groups", "dp"), None),
    )
    line = (mesh.shape["groups"], mesh.shape["dp"], mesh.shape["fsdp"]) == (2, 4, 4)
    return jax.shard_map(
        line_plan if line else ring_plan,
        mesh=mesh,
        in_specs=placed,
        out_specs=P(("groups", "dp", "fsdp"), None),
        check_vma=False,
    )
```

time: 672 us -> 458 us (0.68); the launches traced: 671 us -> 450 us
  waiting for transfers between devices: 354 us -> 178 us
  starting transfers between devices: 71.6 us -> 41.2 us
  blocking collectives: 0 us -> 21.6 us
  Pallas kernels: 167 us -> 148 us
  matrix products: 15 us -> 7.74 us
    ppermute x27 -> x16, waiting for transfers between devices: 254 us -> 165 us  [the longest x1 66.4 us: line_plan(): grad_other = lax.ppermute(out_grad, 'groups', SWAP)]
    all_gather x2, waiting for transfers between devices: 66.4 us -> 0.02 us  [the longest x1 0.02 us: line_plan(): grads_other = lax.all_gather(grad_other, 'fsdp', axis=0)]
    pallas_call x7 -> x6, Pallas kernels: 114 us -> 73.1 us  [the longest x3 60.3 us: late_part(): pl.pallas_call(functools.partial(late_kernel, len(fars), trade_pieces, pe...]
    ppermute x27 -> x16, starting transfers between devices: 71.2 us -> 37.2 us  [the longest x3 10.3 us: line_plan(): chunks.append((first, half, base, fars, lax.ppermute(packed, 'dp', MATES)))]
    psum x1, waiting for transfers between devices: 32.8 us -> 0.02 us  [line_plan(): factors_in = lax.psum(share_in, 'fsdp')]
    all_gather x0 -> x2, blocking collectives: none -> 21.6 us  [the longest x1 15.8 us: own_fisher(): lax.all_gather(example_grads.astype(jnp.bfloat16), 'dp', axis=0, tiled=True)]
    pallas_call x1 -> x4, Pallas kernels: 53.2 us -> 74.5 us  [early_part(): pl.pallas_call(early_kernel, grid_spec=pltpu.PrefetchScalarGridSpec(num_s...]
    all_to_all x0 -> x1, waiting for transfers between devices: none -> 12.7 us  [line_plan(): lax.all_to_all(sums.reshape(2 * fsdp_count, piece_rows, 2 * rank), ('grou...]
  transfers between devices with their start and end apart: 31 -> 21, of which waited for: 14 -> 6; matrix products, arithmetic and copies ran while one was open for 6% -> 8% of each run, Pallas kernels for 22% -> 30%
where the time goes in v2:
time: 458 us; the launch traced here: 450 us
  waiting for transfers between devices  178 us (39%)
  Pallas kernels  148 us (32%)
  starting transfers between devices  41.2 us (9%)
  local copies, waits for them, and re-layouts  37.8 us (8%)
  blocking collectives  21.6 us (5%)
  between operations  13.9 us (3%)
  matrix products  7.74 us (2%)
    pallas_call x4, Pallas kernels, early_part(): pl.pallas_call(early_kernel, grid_spec=pltpu.PrefetchScalarGridSpec(num_s...  74.5 us
    ppermute x1, waiting for transfers between devices, line_plan(): grad_other = lax.ppermute(out_grad, 'groups', SWAP)  66.4 us
    pallas_call x3, Pallas kernels, late_part(): pl.pallas_call(functools.partial(late_kernel, len(fars), trade_pieces, pe...  60.3 us
    ppermute x1, waiting for transfers between devices, line_plan(): piece = lax.ppermute(jnp.where(inner, edge, piece), 'dp', MATES)  55.5 us
    ppermute x1, waiting for transfers between devices, line_plan(): mine = spread[:, :rank] + lax.ppermute(spread[:, rank:], 'dp', OUTWARD)  22.2 us
    all_gather x1, blocking collectives, own_fisher(): lax.all_gather(example_grads.astype(jnp.bfloat16), 'dp', axis=0, tiled=True)  15.8 us
    ppermute x3, waiting for transfers between devices, line_plan(): chunks.append((first, half, base, fars, lax.ppermute(packed, 'dp', MATES)))  13.7 us
    pallas_call x3, Pallas kernels, pack(): pl.pallas_call(pack_kernel, grid_spec=pltpu.PrefetchScalarGridSpec(num_sc...  12.9 us
  transfers between devices with their start and end apart: 21, of which 6 were waited for; matrix products, arithmetic and copies ran while one was open for 8% of the time, Pallas kernels for 30%

profile of v2, /device:TPU:0, one launch (start us, length us, event | category | flops | bytes accessed | tf_op | source)
XLA Modules:
  0.0 450.2 jit_solution(12075866023981091493)
XLA Ops:
  7.3 4.8 %constant_dynamic-slice_fusion.4.own_ref = bf16[1024,2048]{1,0:T(8,128)(2,1)} fusion(bf16[3584,2048]{1,0:T(8,128)(2,1)} %param.10, s32[]{:T(128)S(6)} %select_n.40), kind=kLoop, calls=%fused_computation.20 | loop fusion | bytes 8388612 | tf_op jit(solution)/shard_map/dynamic_slice | solution.py:243
  12.1 3.0 collective-permute-start.1
  15.1 2.6 collective-permute-start.2
  17.8 1.5 collective-permute-start
  19.2 4.7 %constant_dynamic-slice_fusion.2.own_ref = bf16[768,2048]{1,0:T(8,128)(2,1)} fusion(bf16[3584,2048]{1,0:T(8,128)(2,1)} %param.10, s32[]{:T(128)S(6)} %select_n.42), kind=kLoop, calls=%fused_computation.18 | loop fusion | bytes 6291460 | tf_op jit(solution)/shard_map/dynamic_slice | solution.py:244
  24.0 1.9 fusion.12
  25.9 6.6 %constant_dynamic-slice_fusion.1 = (bf16[896,1792]{1,0:T(8,128)(2,1)}, bf16[896,1792]{1,0:T(8,128)(2,1)}) fusion(bf16[896,3584]{1,0:T(8,128)(2,1)} %param.9, s32[]{:T(128)S(6)} %select_n.40, s32[]{:T(128)S(6)} %select_n.41), kind=kLoop, calls=%fused_computation.17 | loop fusion | bytes 12845064 | tf_op jit(solution)/shard_map/dynamic_slice | solution.py:249
  32.5 66.4 %collective-permute-done = bf16[896,2048]{1,0:T(8,128)(2,1)} collective-permute-done((bf16[896,2048]{1,0:T(8,128)(2,1)}, bf16[896,2048]{1,0:T(8,128)(2,1)}, u32[]{:S(2)}, u32[]{:S(2)}) %collective-permute-start) | collective-permute-done | bytes 3670048 | tf_op jit(solution)/shard_map/ppermute | solution.py:246
  98.9 7.2 %collective-permute-done.1.mate_ref = bf16[1024,2048]{1,0:T(8,128)(2,1)} collective-permute-done((bf16[1024,2048]{1,0:T(8,128)(2,1)}, bf16[1024,2048]{1,0:T(8,128)(2,1)}, u32[]{:S(2)}, u32[]{:S(2)}) %collective-permute-start.1) | collective-permute-done | bytes 4194336 | tf_op jit(solution)/shard_map/ppermute | solution.py:247
  106.1 1.7 collective-permute-start.5
  107.8 4.6 %collective-permute-start.3 = (bf16[768,2048]{1,0:T(8,128)(2,1)}, bf16[768,2048]{1,0:T(8,128)(2,1)}, u32[]{:S(2)}, u32[]{:S(2)}) collective-permute-start(bf16[768,2048]{1,0:T(8,128)(2,1)} %constant_dynamic-slice_fusion.2.own_ref), channel_id=1, source_target_pairs={{0,4},{4,0},{8,12},{12,8},{1,5},{5,1},{9,13},{13,9},{2,6},{6,2},{1... | collective-permute-start | bytes 9437192 | tf_op jit(solution)/shard_map/ppermute | solution.py:256
  112.4 2.3 collective-permute-start.4
  115.4 1.2 slice.27
  116.6 1.6 bitcast_select_fusion
  118.2 1.4 collective-permute-start.6
  119.6 1.5 slice.28
  121.9 21.9 %early_part.4.refs_0_ = f32[896,1024]{1,0:T(8,128)} custom-call(s32[6]{0:T(128)} %stack.31.place, bf16[4,896,2048]{2,1,0:T(8,128)(2,1)} %bitcast.36, bf16[1024,2048]{1,0:T(8,128)(2,1)} %constant_dynamic-slice_fusion.4.own_ref, bf16[1024,2048]{1,0:T(8,128)(2,1)} %collective-permute-done.1.mate_ref, bf16[1024,2048]{1,0:T(8,128)(2,1)} %collective-permute-done.2.near_ref), custom_call_target="tpu_custom_call" | custom-call | flops 20480000000 | tf_op jit(solution)/shard_map/early_part/pallas_call | solution.py:48
  143.8 55.5 %collective-permute-done.6 = bf16[224,2048]{1,0:T(8,128)(2,1)S(1)} collective-permute-done((bf16[224,2048]{1,0:T(8,128)(2,1)S(1)}, bf16[224,2048]{1,0:T(8,128)(2,1)S(1)}, u32[]{:S(2)}, u32[]{:S(2)}) %collective-permute-start.6) | collective-permute-done | bytes 917536 | tf_op jit(solution)/shard_map/ppermute | solution.py:268
  200.2 6.0 %pack.3 = bf16[1024,1792]{1,0:T(8,128)(2,1)} custom-call(s32[6]{0:T(128)} %stack.31.place, bf16[896,1792]{1,0:T(8,128)(2,1)} %get-tuple-element.55.self_ref.refs_4_, bf16[896,1792]{1,0:T(8,128)(2,1)} %collective-permute-done.5.other_ref.refs_5_, bf16[1024,2048]{1,0:T(8,128)(2,1)} %collective-permute-done.2.near_ref), custom_call_target="tpu_custom_call" | custom-call | bytes 1048576 | tf_op jit(solution)/shard_map/pack/pallas_call | solution.py:87
  206.2 5.5 %collective-permute-start.9 = (bf16[1024,1792]{1,0:T(8,128)(2,1)}, bf16[1024,1792]{1,0:T(8,128)(2,1)}, u32[]{:S(2)}, u32[]{:S(2)}) collective-permute-start(bf16[1024,1792]{1,0:T(8,128)(2,1)} %pack.3), channel_id=1, source_target_pairs={{0,4},{4,0},{8,12},{12,8},{1,5},{5,1},{9,13},{13,9},{2,6},{6,2},{1... | collective-permute-start | bytes 11010056 | tf_op jit(solution)/shard_map/ppermute | solution.py:311
  212.5 4.4 slice.29
  216.8 2.6 collective-permute-start.8
  219.5 2.3 slice.31
  221.8 3.2 slice.32
  225.1 1.8 slice.33
  226.8 16.4 %early_part.5.refs_0_ = f32[896,768]{1,0:T(8,128)} custom-call(s32[6]{0:T(128)} %stack.31.place, bf16[4,896,2048]{2,1,0:T(8,128)(2,1)} %bitcast.37, bf16[768,2048]{1,0:T(8,128)(2,1)} %constant_dynamic-slice_fusion.2.own_ref, bf16[768,2048]{1,0:T(8,128)(2,1)} %collective-permute-done.3.mate_ref, bf16[768,2048]{1,0:T(8,128)(2,1)} %collective-permute-done.4.near_ref), custom_call_target="tpu_custom_call" | custom-call | flops 15360000000 | tf_op jit(solution)/shard_map/early_part/pallas_call | solution.py:48
  243.2 2.0 collective-permute-start.11
  246.1 1.3 collective-permute-start.12
  247.4 3.7 pack.4
  251.1 2.8 collective-permute-start.13
  253.9 19.9 %early_part.6.refs_1_ = f32[896,1024]{1,0:T(8,128)} custom-call(s32[6]{0:T(128)} %stack.31.place, bf16[4,896,2048]{2,1,0:T(8,128)(2,1)} %bitcast.41, bf16[1024,2048]{1,0:T(8,128)(2,1)} %constant_dynamic-slice_fusion.4.own_ref, bf16[1024,2048]{1,0:T(8,128)(2,1)} %collective-permute-done.1.mate_ref, bf16[1024,2048]{1,0:T(8,128)(2,1)} %collective-permute-done.2.near_ref), custom_call_target="tpu_custom_call" | custom-call | flops 20480000000 | tf_op jit(solution)/shard_map/early_part/pallas_call | solution.py:48
  273.8 3.2 pack.5
  277.0 1.7 collective-permute-start.10
  278.7 13.7 %collective-permute-done.9.refs_12_.refs_13_.refs_14_.refs_15_.refs_16_ = bf16[1024,1792]{1,0:T(8,128)(2,1)} collective-permute-done((bf16[1024,1792]{1,0:T(8,128)(2,1)}, bf16[1024,1792]{1,0:T(8,128)(2,1)}, u32[]{:S(2)}, u32[]{:S(2)}) %collective-permute-start.9) | collective-permute-done | bytes 3670048 | tf_op jit(solution)/shard_map/ppermute | solution.py:311
  292.3 2.0 collective-permute-start.14
  294.4 16.4 %early_part.7.refs_1_ = f32[896,768]{1,0:T(8,128)} custom-call(s32[6]{0:T(128)} %stack.31.place, bf16[4,896,2048]{2,1,0:T(8,128)(2,1)} %bitcast.42, bf16[768,2048]{1,0:T(8,128)(2,1)} %constant_dynamic-slice_fusion.2.own_ref, bf16[768,2048]{1,0:T(8,128)(2,1)} %collective-permute-done.3.mate_ref, bf16[768,2048]{1,0:T(8,128)(2,1)} %collective-permute-done.4.near_ref), custom_call_target="tpu_custom_call" | custom-call | flops 15360000000 | tf_op jit(solution)/shard_map/early_part/pallas_call | solution.py:48
  310.7 1.0 broadcast_in_dim.2.refs_10_
  311.7 32.5 %late_part.3.refs_9_ = f32[1792,128]{1,0:T(8,128)} custom-call(s32[6]{0:T(128)} %stack.31.place, f32[896,1024]{1,0:T(8,128)} %early_part.4.refs_0_, f32[896,1024]{1,0:T(8,128)} %early_part.6.refs_1_, bf16[4,896,2048]{2,1,0:T(8,128)(2,1)} %bitcast.38, bf16[4,896,2048]{2,1,0:T(8,128)(2,1)} %bitcast.43, ...), custom_call_target="tpu_custom_call", output_to_operand_aliasing={{}: (11, {})} | custom-call | flops 1048576 | tf_op jit(solution)/shard_map/late_part/pallas_call | solution.py:184
  345.6 15.5 %late_part.4.refs_9_ = f32[1792,128]{1,0:T(8,128)} custom-call(s32[6]{0:T(128)} %stack.31.place, f32[896,768]{1,0:T(8,128)} %early_part.5.refs_0_, f32[896,768]{1,0:T(8,128)} %early_part.7.refs_1_, bf16[4,896,2048]{2,1,0:T(8,128)(2,1)} %bitcast.39, bf16[4,896,2048]{2,1,0:T(8,128)(2,1)} %bitcast.44, ...), custom_call_target="tpu_custom_call", output_to_operand_aliasing={{}: (10, {})} | custom-call | flops 1048576 | tf_op jit(solution)/shard_map/late_part/pallas_call | solution.py:184
  362.1 12.3 %late_part.5 = f32[1792,128]{1,0:T(8,128)} custom-call(s32[6]{0:T(128)} %stack.31.place, f32[896,768]{1,0:T(8,128)} %early_part.5.refs_0_, f32[896,768]{1,0:T(8,128)} %early_part.7.refs_1_, bf16[4,896,2048]{2,1,0:T(8,128)(2,1)} %bitcast.40, bf16[4,896,2048]{2,1,0:T(8,128)(2,1)} %bitcast.45, ...), custom_call_target="tpu_custom_call", output_to_operand_aliasing={{}: (10, {})} | custom-call | flops 1048576 | tf_op jit(solution)/shard_map/late_part/pallas_call | solution.py:184
  374.4 3.9 all-to-all-start
  378.6 12.7 %all-to-all-done = f32[8,224,128]{2,1,0:T(8,128)S(1)} async-done(((f32[8,224,128]{2,1,0:T(8,128)}), f32[8,224,128]{2,1,0:T(8,128)S(1)}, u32[]{:S(2)}, u32[]{:S(2)}) %all-to-all-start) | async-done | bytes 917536 | tf_op jit(solution)/shard_map/all_to_all | solution.py:321
  391.5 1.3 collective-permute-start.15
  392.9 22.2 %collective-permute-done.15 = f32[224,64]{1,0:T(8,128)S(1)} collective-permute-done((f32[224,64]{1,0:T(8,128)S(1)}, f32[224,64]{1,0:T(8,128)S(1)}, u32[]{:S(2)}, u32[]{:S(2)}) %collective-permute-start.15) | collective-permute-done | bytes 57376 | tf_op jit(solution)/shard_map/ppermute | solution.py:324
  415.2 5.8 %all-gather.2 = f32[4,224,64]{1,2,0:T(8,128)S(1)} all-gather(f32[1,224,64]{1,2,0:T(8,128)S(1)} %copy.20), channel_id=1, replica_groups=mesh['groups'=2,'dp'=4,'fsdp'=4] {'fsdp'}, dimensions={0}, use_global_device_ids=true | all-gather | bytes 286720 | tf_op jit(solution)/shard_map/all_gather | solution.py:325
  421.3 3.1 fusion.4
  424.7 15.8 %all_gather.27 = bf16[64,4096]{1,0:T(8,128)(2,1)S(1)} all-gather(bf16[16,4096]{1,0:T(8,128)(2,1)S(1)} %convert_element_type.18), channel_id=1, replica_groups=mesh['groups'=2,'dp'=4,'fsdp'=4] {'dp'}, dimensions={0}, use_global_device_ids=true | all-gather | bytes 655360 | tf_op jit(solution)/shard_map/all_gather | solution.py:218
  440.5 2.7 convolution_multiply_fusion
  (65 shorter events, 8.4 us)
Async XLA Ops:
  6.5 205.2 %copy-start = (bf16[64,3584]{1,0:T(8,128)(2,1)S(1)}, bf16[64,3584]{1,0:T(8,128)(2,1)}, u32[]{:S(2)}) copy-start(bf16[64,3584]{1,0:T(8,128)(2,1)} %param.12) | copy-start | bytes 1376260
  6.5 99.5 %all-gather.9.cloned.1.call-start = ((), (), s32[]{:S(2)}) async-start(), calls=%async_computation.3 | async-start | bytes 18350080 | tf_op jit(solution)/shard_map/all_gather | solution.py:245
  7.3 246.7 %all-gather.11.cloned.1.call-start = ((), (), s32[]{:S(2)}) async-start(), calls=%async_computation.4 | async-start | bytes 18350080 | tf_op jit(solution)/shard_map/all_gather | solution.py:259
  12.1 11.9 %copy-start.9 = (bf16[64,2048]{1,0:T(8,128)(2,1)S(1)}, bf16[64,2048]{1,0:T(8,128)(2,1)}, u32[]{:S(2)}) copy-start(bf16[64,2048]{1,0:T(8,128)(2,1)} %param.11) | copy-start | bytes 786436
  12.1 93.9 %collective-permute-start.1 = (bf16[1024,2048]{1,0:T(8,128)(2,1)}, bf16[1024,2048]{1,0:T(8,128)(2,1)}, u32[]{:S(2)}, u32[]{:S(2)}) collective-permute-start(bf16[1024,2048]{1,0:T(8,128)(2,1)} %constant_dynamic-slice_fusion.4.own_ref), channel_id=1, source_target_pairs={{0,4},{4,0},{8,12},{12,8},{1,5},{5,1},{9,13},{13,9},{2,6},{6,2},{1... | collective-permute-start | bytes 12582920 | tf_op jit(solution)/shard_map/ppermute | solution.py:247
  15.1 90.9 %collective-permute-start.2 = (bf16[1024,2048]{1,0:T(8,128)(2,1)}, bf16[1024,2048]{1,0:T(8,128)(2,1)}, u32[]{:S(2)}, u32[]{:S(2)}) collective-permute-start(bf16[1024,2048]{1,0:T(8,128)(2,1)} %constant_dynamic-slice_fusion.4.own_ref), channel_id=1, source_target_pairs={{4,8},{8,4},{5,9},{9,5},{6,10},{10,6},{7,11},{11,7},{20,24},{24,20... | collective-permute-start | bytes 12582920 | tf_op jit(solution)/shard_map/ppermute | solution.py:248
  17.8 81.1 %collective-permute-start = (bf16[896,2048]{1,0:T(8,128)(2,1)}, bf16[896,2048]{1,0:T(8,128)(2,1)}, u32[]{:S(2)}, u32[]{:S(2)}) collective-permute-start(bf16[896,2048]{1,0:T(8,128)(2,1)} %param.8), channel_id=1, source_target_pairs={{0,16},{16,0},{1,17},{17,1},{2,18},{18,2},{3,19},{19,3},{4,20},{20... | collective-permute-start | bytes 11010056 | tf_op jit(solution)/shard_map/ppermute | solution.py:246
  19.2 4.7 %copy-start.3 = (bf16[896,2048]{1,0:T(8,128)(2,1)S(1)}, bf16[896,2048]{1,0:T(8,128)(2,1)}, u32[]{:S(2)}) copy-start(bf16[896,2048]{1,0:T(8,128)(2,1)} %param.7) | copy-start | bytes 11010052
  106.0 204.7 %all-gather.7.cloned.1.call-start = ((), (), s32[]{:S(2)}) async-start(), calls=%async_computation.1 | async-start | bytes 8257536 | tf_op jit(solution)/shard_map/all_gather | solution.py:276
  106.1 93.2 %collective-permute-start.5 = (bf16[896,1792]{1,0:T(8,128)(2,1)}, bf16[896,1792]{1,0:T(8,128)(2,1)}, u32[]{:S(2)}, u32[]{:S(2)}) collective-permute-start(bf16[896,1792]{1,0:T(8,128)(2,1)} %get-tuple-element.31), channel_id=1, source_target_pairs={{0,16},{16,0},{1,17},{17,1},{2,18},{18,2},{3,19},{19,3},{4,20},{20... | collective-permute-start | bytes 9633800 | tf_op jit(solution)/shard_map/ppermute | solution.py:258
  107.8 91.4 %collective-permute-start.3 = (bf16[768,2048]{1,0:T(8,128)(2,1)}, bf16[768,2048]{1,0:T(8,128)(2,1)}, u32[]{:S(2)}, u32[]{:S(2)}) collective-permute-start(bf16[768,2048]{1,0:T(8,128)(2,1)} %constant_dynamic-slice_fusion.2.own_ref), channel_id=1, source_target_pairs={{0,4},{4,0},{8,12},{12,8},{1,5},{5,1},{9,13},{13,9},{2,6},{6,2},{1... | collective-permute-start | bytes 9437192 | tf_op jit(solution)/shard_map/ppermute | solution.py:256
  112.4 86.8 %collective-permute-start.4 = (bf16[768,2048]{1,0:T(8,128)(2,1)}, bf16[768,2048]{1,0:T(8,128)(2,1)}, u32[]{:S(2)}, u32[]{:S(2)}) collective-permute-start(bf16[768,2048]{1,0:T(8,128)(2,1)} %constant_dynamic-slice_fusion.2.own_ref), channel_id=1, source_target_pairs={{4,8},{8,4},{5,9},{9,5},{6,10},{10,6},{7,11},{11,7},{20,24},{24,20... | collective-permute-start | bytes 9437192 | tf_op jit(solution)/shard_map/ppermute | solution.py:257
  118.2 81.0 %collective-permute-start.6 = (bf16[224,2048]{1,0:T(8,128)(2,1)S(1)}, bf16[224,2048]{1,0:T(8,128)(2,1)S(1)}, u32[]{:S(2)}, u32[]{:S(2)}) collective-permute-start(bf16[224,2048]{1,0:T(8,128)(2,1)S(1)} %bitcast_select_fusion), channel_id=1, source_target_pairs={{0,4},{4,0},{8,12},{12,8},{1,5},{5,1},{9,13},{13,9},{2,6},{6,2},{1... | collective-permute-start | bytes 2752520 | tf_op jit(solution)/shard_map/ppermute | solution.py:268
  121.1 78.1 %collective-permute-start.7 = (bf16[256,2048]{1,0:T(8,128)(2,1)S(1)}, bf16[256,2048]{1,0:T(8,128)(2,1)S(1)}, u32[]{:S(2)}, u32[]{:S(2)}) collective-permute-start(bf16[256,2048]{1,0:T(8,128)(2,1)S(1)} %slice.28), channel_id=1, source_target_pairs={{4,8},{8,4},{5,9},{9,5},{6,10},{10,6},{7,11},{11,7},{20,24},{24,20... | collective-permute-start | bytes 3145736 | tf_op jit(solution)/shard_map/ppermute | solution.py:269
  199.2 0.9 copy-start.5
  199.2 7.0 %copy-start.8 = (bf16[256,2048]{1,0:T(8,128)(2,1)}, bf16[256,2048]{1,0:T(8,128)(2,1)S(1)}, u32[]{:S(2)}) copy-start(bf16[256,2048]{1,0:T(8,128)(2,1)S(1)} %collective-permute-done.7.refs_6_) | copy-start | bytes 3145732
  200.2 144.0 %all-reduce.3.cloned.1.call-start = ((), (), s32[]{:S(2)}) async-start(), calls=%async_computation.2 | async-start | bytes 458752 | tf_op jit(solution)/shard_map/psum | solution.py:277
  206.2 86.1 %collective-permute-start.9 = (bf16[1024,1792]{1,0:T(8,128)(2,1)}, bf16[1024,1792]{1,0:T(8,128)(2,1)}, u32[]{:S(2)}, u32[]{:S(2)}) collective-permute-start(bf16[1024,1792]{1,0:T(8,128)(2,1)} %pack.3), channel_id=1, source_target_pairs={{0,4},{4,0},{8,12},{12,8},{1,5},{5,1},{9,13},{13,9},{2,6},{6,2},{1... | collective-permute-start | bytes 11010056 | tf_op jit(solution)/shard_map/ppermute | solution.py:311
  216.8 8.2 %copy-start.6 = (bf16[224,2048]{1,0:T(8,128)(2,1)S(1)}, bf16[224,2048]{1,0:T(8,128)(2,1)}, u32[]{:S(2)}) copy-start(bf16[224,2048]{1,0:T(8,128)(2,1)} %copy-done.5) | copy-start | bytes 2752516
  216.8 60.1 %collective-permute-start.8 = (bf16[768,2048]{1,0:T(8,128)(2,1)}, bf16[768,2048]{1,0:T(8,128)(2,1)}, u32[]{:S(2)}, u32[]{:S(2)}) collective-permute-start(bf16[768,2048]{1,0:T(8,128)(2,1)} %slice.29), channel_id=1, source_target_pairs={{4,8},{8,4},{5,9},{9,5},{6,10},{10,6},{7,11},{11,7},{20,24},{24,20... | collective-permute-start | bytes 9437192 | tf_op jit(solution)/shard_map/ppermute | solution.py:306
  243.2 101.1 %collective-permute-start.11 = (bf16[512,2048]{1,0:T(8,128)(2,1)}, bf16[512,2048]{1,0:T(8,128)(2,1)}, u32[]{:S(2)}, u32[]{:S(2)}) collective-permute-start(bf16[512,2048]{1,0:T(8,128)(2,1)} %slice.32), channel_id=1, source_target_pairs={{4,8},{8,4},{5,9},{9,5},{6,10},{10,6},{7,11},{11,7},{20,24},{24,20... | collective-permute-start | bytes 6291464 | tf_op jit(solution)/shard_map/ppermute | solution.py:306
  246.1 98.2 %collective-permute-start.12 = (bf16[768,256]{1,0:T(8,128)(2,1)}, bf16[768,256]{1,0:T(8,128)(2,1)S(1)}, u32[]{:S(2)}, u32[]{:S(2)}) collective-permute-start(bf16[768,256]{1,0:T(8,128)(2,1)} %slice.33), channel_id=1, source_target_pairs={{4,0},{8,12},{5,1},{9,13},{6,2},{10,14},{7,3},{11,15},{20,16},{24,... | collective-permute-start | bytes 1179656 | tf_op jit(solution)/shard_map/ppermute | solution.py:280
  251.1 93.2 %collective-permute-start.13 = (bf16[512,1792]{1,0:T(8,128)(2,1)}, bf16[512,1792]{1,0:T(8,128)(2,1)S(1)}, u32[]{:S(2)}, u32[]{:S(2)}) collective-permute-start(bf16[512,1792]{1,0:T(8,128)(2,1)} %pack.4), channel_id=1, source_target_pairs={{0,4},{4,0},{8,12},{12,8},{1,5},{5,1},{9,13},{13,9},{2,6},{6,2},{1... | collective-permute-start | bytes 5505032 | tf_op jit(solution)/shard_map/ppermute | solution.py:311
  277.0 84.1 %collective-permute-start.10 = (bf16[256,2048]{1,0:T(8,128)(2,1)}, bf16[256,2048]{1,0:T(8,128)(2,1)}, u32[]{:S(2)}, u32[]{:S(2)}) collective-permute-start(bf16[256,2048]{1,0:T(8,128)(2,1)} %slice.31), channel_id=1, source_target_pairs={{4,8},{8,4},{5,9},{9,5},{6,10},{10,6},{7,11},{11,7},{20,24},{24,20... | collective-permute-start | bytes 3145736 | tf_op jit(solution)/shard_map/ppermute | solution.py:306
  292.3 68.8 %collective-permute-start.14 = (bf16[256,1792]{1,0:T(8,128)(2,1)}, bf16[256,1792]{1,0:T(8,128)(2,1)S(1)}, u32[]{:S(2)}, u32[]{:S(2)}) collective-permute-start(bf16[256,1792]{1,0:T(8,128)(2,1)} %pack.5), channel_id=1, source_target_pairs={{0,4},{4,0},{8,12},{12,8},{1,5},{5,1},{9,13},{13,9},{2,6},{6,2},{1... | collective-permute-start | bytes 2752520 | tf_op jit(solution)/shard_map/ppermute | solution.py:311
  344.2 0.8 copy-start.7
  344.3 1.4 copy-start.2
  361.1 17.3 %copy-start.10 = (s32[1,16]{1,0:T(1,128)S(1)}, s32[1,16]{1,0:T(1,128)}, u32[]{:S(2)}) copy-start(s32[1,16]{1,0:T(1,128)} %param.13) | copy-start | bytes 196
  361.1 1.0 copy-start.4
  374.4 46.9 %copy-start.11 = (f32[896,64]{0,1:T(8,128)S(1)}, f32[896,64]{0,1:T(8,128)}, u32[]{:S(2)}) copy-start(f32[896,64]{0,1:T(8,128)} %all-reduce.3.cloned.1.call-done) | copy-start | bytes 688132
  374.4 16.9 %all-to-all-start = ((f32[8,224,128]{2,1,0:T(8,128)}), f32[8,224,128]{2,1,0:T(8,128)S(1)}, u32[]{:S(2)}, u32[]{:S(2)}) async-start(f32[8,224,128]{2,1,0:T(8,128)} %bitcast.49), calls=%async_computation | async-start | bytes 1835008 | tf_op jit(solution)/shard_map/all_to_all | solution.py:321
  391.5 23.6 %collective-permute-start.15 = (f32[224,64]{1,0:T(8,128)S(1)}, f32[224,64]{1,0:T(8,128)S(1)}, u32[]{:S(2)}, u32[]{:S(2)}) collective-permute-start(f32[224,64]{1,0:T(8,128)S(1)} %slice.37), channel_id=1, source_target_pairs={{4,0},{8,12},{5,1},{9,13},{6,2},{10,14},{7,3},{11,15},{20,16},{24,... | collective-permute-start | bytes 172040 | tf_op jit(solution)/shard_map/ppermute | solution.py:324
  421.1 22.1 %copy-start.1 = (bf16[64,3584]{1,0:T(8,128)(2,1)S(1)}, bf16[64,3584]{1,0:T(8,128)(2,1)}, u32[]{:S(2)}) copy-start(bf16[64,3584]{1,0:T(8,128)(2,1)} %param.12) | copy-start | bytes 1376260
Sparse Core Ops, SparseCore 0:
  8.9 96.7 all-gather.8
  107.2 96.5 all-gather.10
  205.7 49.9 all-gather.6
  257.9 31.8 all-reduce.2

commit v3 on v2

--- a/solution.py
+++ b/solution.py
@@ -15,7 +15,7 @@
 UNIT = 256
 FIRST_UNITS = 4
 LATE = ((4, (1, 3)), (2, (2,)), (1, (1,)))
-EARLY_COST = 2 * 10**7
+EARLY_COST = 1 << 10
 LATE_COST = 1 << 20
 VMEM_LIMIT = 58 * 1024 * 1024
 
@@ -69,8 +69,11 @@
 
     @pl.when(jnp.logical_not(inner))
     def _():
-        rows = packed_ref.shape[0] // 4
-        count = packed_ref.shape[1] // UNIT
+        rows, source_rows = packed_ref.shape[0] // 4, self_ref.shape[0]
+        rest = packed_ref.shape[1] - 2 * source_rows
+        if rest:
+            packed_ref[:, 2 * source_rows :] = jnp.zeros((packed_ref.shape[0], rest), packed_ref.dtype)
+        count = source_rows // (2 * rows)
         for piece in range(4):
             source = self_ref if piece < 2 else other_ref
             for at in range(count):
@@ -80,9 +83,8 @@
                 ]
 
 
-def pack(place, first, units, gates, near, near_first):
+def pack(place, first, units, gates, near, near_first, wide):
     tokens_dev = gates[0].shape[0]
-    wide = 2 * tokens_dev
     gate = pl.BlockSpec((tokens_dev, UNIT), lambda i, place: (0, first + i))
     return pl.pallas_call(
         pack_kernel,
@@ -99,11 +101,12 @@
     )(place, *gates, near)
 
 
-def late_kernel(far_pieces, trade_pieces, per, place, *refs):
+def late_kernel(far_pieces, rest_pieces, trade_pieces, per, place, *refs):
     refs = list(refs)
     take = lambda count: [refs.pop(0) for _ in range(count)]
     parts, grads, gate_refs, far_refs = take(2), take(2), take(2), take(far_pieces)
-    guest_grad_ref, proj_ref, sum_ref, rest_ref = take(4)
+    guest_grad_ref, proj_ref, sum_ref = take(3)
+    rest_refs = take(rest_pieces)
     trade_refs = take(len(trade_pieces))
     packed_refs = take(sum(trade_pieces))
     (new_ref,) = refs
@@ -142,13 +145,13 @@
         @pl.when((step // per == group) & jnp.logical_not(inner))
         def _(group=group):
             weight = jnp.concatenate([ref[...] for ref in trade_refs], axis=0)
-            weight = jnp.concatenate([weight, rest_ref[...]], axis=1)
+            weight = jnp.concatenate([weight, *[ref[...] for ref in rest_refs]], axis=1)
             upstream = parts[group][...] + dot_nt(grads[group][0], weight)
             new_ref[:, :rank] = sum_ref[:, :rank] + project(upstream, gate_refs[group][...], True)
             new_ref[:, rank:] = sum_ref[:, rank:]
 
 
-def late_part(place, first, base, parts, grads, fars, trades, rest, gates, guest_grads, proj_out, sums):
+def late_part(place, first, base, parts, grads, fars, trades, rests, gates, guest_grads, proj_out, sums):
     tokens_dev, width = grads[0].shape[1:]
     tile = tokens_dev // 2
     per = tokens_dev // tile
@@ -156,7 +159,7 @@
     units = sum(trade_pieces)
     wide = units * UNIT
     chunk, local = first // units, (first - base) // units
-    trade_width = trades[0].shape[1]
+    trade_width = 2 * tokens_dev
     packed_rows = tile * UNIT // trade_width
     tiles = UNIT // packed_rows
     rank = proj_out.shape[0]
@@ -172,8 +175,8 @@
             pl.BlockSpec((1, tile, width), lambda i, place: (i // per ^ place[0], i % per, 0)),
             pl.BlockSpec((rank, wide), lambda i, place: (0, chunk)),
             summed,
-            pl.BlockSpec((wide, rest.shape[1]), lambda i, place: (local, 0)),
         ]
+        + [pl.BlockSpec((wide, rest.shape[1]), lambda i, place: (local, 0)) for rest in rests]
         + [held(trade) for trade in trades]
         + [
             pl.BlockSpec((packed_rows, trade_width), lambda i, place, u=u: (u * tiles + i, 0))
@@ -182,7 +185,7 @@
         ]
     )
     return pl.pallas_call(
-        functools.partial(late_kernel, len(fars), trade_pieces, per),
+        functools.partial(late_kernel, len(fars), len(rests), trade_pieces, per),
         grid_spec=pltpu.PrefetchScalarGridSpec(
             num_scalar_prefetch=1,
             grid=(2 * per,),
@@ -195,7 +198,7 @@
         cost_estimate=pl.CostEstimate(flops=LATE_COST, bytes_accessed=0, transcendentals=0),
         name="late_part",
     )(
-        place, *parts, *grads, *gates, *fars, guest_grads, proj_out, sums, rest, *trades,
+        place, *parts, *grads, *gates, *fars, guest_grads, proj_out, sums, *rests, *trades,
         *[trade for trade, pieces in zip(trades, trade_pieces) for _ in range(pieces)],
     )
 
@@ -269,15 +272,17 @@
     far_start = lax.ppermute(mate_first[: LATE[0][1][0] * UNIT], "dp", ACROSS)
     part_self = early_part(place, grads_self, own_first, mate_first, near_first)
 
-    mate_second, near_second, gate_other, piece, part_self, share_in, far_start = lax.optimization_barrier(
-        (mate_second, near_second, gate_other, piece, part_self, share_in, far_start)
+    gates = (gate_self, gate_other)
+    ready_far = mate_first[LATE[0][1][0] * UNIT : FIRST_UNITS * UNIT]
+    ready_pack = pack(place, 0, FIRST_UNITS, gates, near_first, 0, trade_width)
+    mate_second, near_second, piece, part_self, share_in, far_start, ready_far, ready_pack = lax.optimization_barrier(
+        (mate_second, near_second, piece, part_self, share_in, far_start, ready_far, ready_pack)
     )
     rest_first = piece[:slot_rows].reshape(slot_rows, slots, lanes).swapaxes(0, 1).reshape(cut, lanes)
     guest_grads = lax.all_gather(piece, ("groups", "fsdp"), axis=0, tiled=True).reshape(2, tokens_dev, width)
     factors_in = lax.psum(share_in, "fsdp")
     mates, nears = (mate_first, mate_second), (near_first, near_second)
-    gates = (gate_self, gate_other)
-    rests = (rest_first, lax.ppermute(near_second[:, trade_width:], "dp", OUTWARD))
+    rests = ([rest_first], [])
     turn = place
     done = []
     parts_first, parts_second = [part_self], []
@@ -291,7 +296,7 @@
     sums = jnp.zeros((2 * tokens_dev, 2 * rank), jnp.float32)
 
     def after(operand, order):
-        return lax.optimization_barrier((operand, done[order - 1]))[0] if order else operand
+        return lax.optimization_barrier((operand, done[2 * order - 2]))[0]
 
     chunks = []
     first = 0
@@ -302,12 +307,15 @@
         at = first
         for count in far_pieces:
             if at:
-                rows = after(mates[half][(at - base) * UNIT : (at - base + count) * UNIT], order)
+                rows = ready_far
+                if order:
+                    rows = after(mates[half][(at - base) * UNIT : (at - base + count) * UNIT], order)
                 fars.append(lax.ppermute(rows, "dp", ACROSS))
             else:
                 fars.append(far_start)
             at += count
-        packed = pack(after(place, order), first, units, gates, nears[half], base)
+        packed = pack(place, first, units, gates, nears[half], base, width) if order else ready_pack
+        packed = after(packed, order) if order else packed
         chunks.append((first, half, base, fars, lax.ppermute(packed, "dp", MATES)))
         first += units
     for first, half, base, fars, trade in chunks:

time: 458 us -> 437 us (0.954)
  waiting for transfers between devices: 178 us -> 162 us
    ppermute x1, waiting for transfers between devices: 55.5 us -> 15.5 us  [line_plan(): piece = lax.ppermute(jnp.where(inner, edge, piece), 'dp', MATES)]
    ppermute x1, waiting for transfers between devices: 0.01 us -> 29.6 us  [line_plan(): gate_other = lax.ppermute(gate_send, 'groups', SWAP)]
    ppermute x1, waiting for transfers between devices: 22.2 us -> 10.1 us  [line_plan(): mine = spread[:, :rank] + lax.ppermute(spread[:, rank:], 'dp', OUTWARD)]
    ppermute x3, waiting for transfers between devices: 13.7 us -> 20 us  [line_plan(): chunks.append((first, half, base, fars, lax.ppermute(packed, 'dp', MATES)))]
    slice x3 -> x2, local copies, waits for them, and re-layouts: 9.89 us -> 5.53 us  [line_plan(): mates[half][(at - base) * UNIT:(at - base + count) * UNIT]]
  transfers between devices with their start and end apart: 21 -> 20, of which waited for: 6 -> 9; matrix products, arithmetic and copies ran while one was open for 8% -> 9% of each run, Pallas kernels for 30% -> 31%
where the time goes in v3:
time: 437 us; the launch traced here: 429 us
  waiting for transfers between devices  162 us (37%)
  Pallas kernels  145 us (33%)
  starting transfers between devices  40.6 us (9%)
  local copies, waits for them, and re-layouts  35.1 us (8%)
  blocking collectives  21.9 us (5%)
  between operations  13.8 us (3%)
  matrix products  7.74 us (2%)
    pallas_call x4, Pallas kernels, early_part(): pl.pallas_call(early_kernel, grid_spec=pltpu.PrefetchScalarGridSpec(num_s...  73.1 us
    ppermute x1, waiting for transfers between devices, line_plan(): grad_other = lax.ppermute(out_grad, 'groups', SWAP)  66.4 us
    pallas_call x3, Pallas kernels, late_part(): pl.pallas_call(functools.partial(late_kernel, len(fars), len(rests), trad...  58.2 us
    ppermute x1, waiting for transfers between devices, line_plan(): gate_other = lax.ppermute(gate_send, 'groups', SWAP)  29.6 us
    ppermute x3, waiting for transfers between devices, line_plan(): chunks.append((first, half, base, fars, lax.ppermute(packed, 'dp', MATES)))  20 us
    all_gather x1, blocking collectives, own_fisher(): lax.all_gather(example_grads.astype(jnp.bfloat16), 'dp', axis=0, tiled=True)  16.1 us
    ppermute x1, waiting for transfers between devices, line_plan(): piece = lax.ppermute(jnp.where(inner, edge, piece), 'dp', MATES)  15.5 us
    pallas_call x3, Pallas kernels, pack(): pl.pallas_call(pack_kernel, grid_spec=pltpu.PrefetchScalarGridSpec(num_sc...  13.6 us
  transfers between devices with their start and end apart: 20, of which 9 were waited for; matrix products, arithmetic and copies ran while one was open for 9% of the time, Pallas kernels for 31%

profile of v3, /device:TPU:0, one launch (start us, length us, event | category | flops | bytes accessed | tf_op | source)
XLA Modules:
  0.0 429.2 jit_solution(11203791395196481731)
XLA Ops:
  7.3 4.8 %constant_dynamic-slice_fusion.4.own_ref = bf16[1024,2048]{1,0:T(8,128)(2,1)} fusion(bf16[3584,2048]{1,0:T(8,128)(2,1)} %param.10, s32[]{:T(128)S(6)} %select_n.40), kind=kLoop, calls=%fused_computation.20 | loop fusion | bytes 8388612 | tf_op jit(solution)/shard_map/dynamic_slice | solution.py:246
  12.1 3.0 collective-permute-start.1
  15.1 2.6 collective-permute-start.2
  17.8 1.5 collective-permute-start
  19.3 4.7 %constant_dynamic-slice_fusion.2.own_ref = bf16[768,2048]{1,0:T(8,128)(2,1)} fusion(bf16[3584,2048]{1,0:T(8,128)(2,1)} %param.10, s32[]{:T(128)S(6)} %select_n.42), kind=kLoop, calls=%fused_computation.18 | loop fusion | bytes 6291460 | tf_op jit(solution)/shard_map/dynamic_slice | solution.py:247
  24.0 1.9 fusion.12
  25.9 6.6 %constant_dynamic-slice_fusion.1 = (bf16[896,1792]{1,0:T(8,128)(2,1)}, bf16[896,1792]{1,0:T(8,128)(2,1)}) fusion(bf16[896,3584]{1,0:T(8,128)(2,1)} %param.9, s32[]{:T(128)S(6)} %select_n.40, s32[]{:T(128)S(6)} %select_n.41), kind=kLoop, calls=%fused_computation.17 | loop fusion | bytes 12845064 | tf_op jit(solution)/shard_map/dynamic_slice | solution.py:252
  32.5 66.4 %collective-permute-done = bf16[896,2048]{1,0:T(8,128)(2,1)} collective-permute-done((bf16[896,2048]{1,0:T(8,128)(2,1)}, bf16[896,2048]{1,0:T(8,128)(2,1)}, u32[]{:S(2)}, u32[]{:S(2)}) %collective-permute-start) | collective-permute-done | bytes 3670048 | tf_op jit(solution)/shard_map/ppermute | solution.py:249
  98.9 7.2 %collective-permute-done.1.mate_ref = bf16[1024,2048]{1,0:T(8,128)(2,1)} collective-permute-done((bf16[1024,2048]{1,0:T(8,128)(2,1)}, bf16[1024,2048]{1,0:T(8,128)(2,1)}, u32[]{:S(2)}, u32[]{:S(2)}) %collective-permute-start.1) | collective-permute-done | bytes 4194336 | tf_op jit(solution)/shard_map/ppermute | solution.py:250
  106.1 1.7 collective-permute-start.7
  107.8 4.6 %collective-permute-start.3 = (bf16[768,2048]{1,0:T(8,128)(2,1)}, bf16[768,2048]{1,0:T(8,128)(2,1)}, u32[]{:S(2)}, u32[]{:S(2)}) collective-permute-start(bf16[768,2048]{1,0:T(8,128)(2,1)} %constant_dynamic-slice_fusion.2.own_ref), channel_id=1, source_target_pairs={{0,4},{4,0},{8,12},{12,8},{1,5},{5,1},{9,13},{13,9},{2,6},{6,2},{1... | collective-permute-start | bytes 9437192 | tf_op jit(solution)/shard_map/ppermute | solution.py:259
  112.4 2.3 collective-permute-start.4
  115.9 1.5 slice.25
  118.1 2.6 bitcast_select_fusion
  120.7 2.6 collective-permute-start.5
  123.9 4.4 %slice.26 = bf16[768,2048]{1,0:T(8,128)(2,1)} slice(bf16[1024,2048]{1,0:T(8,128)(2,1)} %collective-permute-done.1.mate_ref), slice={[256:1024], [0:2048]} | slice | bytes 6291456 | tf_op jit(solution)/shard_map/slice | solution.py:276
  128.3 19.9 %early_part.4.refs_0_ = f32[896,1024]{1,0:T(8,128)} custom-call(s32[6]{0:T(128)} %stack.31.place, bf16[4,896,2048]{2,1,0:T(8,128)(2,1)} %bitcast.36, bf16[1024,2048]{1,0:T(8,128)(2,1)} %constant_dynamic-slice_fusion.4.own_ref, bf16[1024,2048]{1,0:T(8,128)(2,1)} %collective-permute-done.1.mate_ref, bf16[1024,2048]{1,0:T(8,128)(2,1)} %collective-permute-done.2.near_ref), custom_call_target="tpu_custom_call" | custom-call | flops 1048576 | tf_op jit(solution)/shard_map/early_part/pallas_call | solution.py:48
  148.2 29.6 %collective-permute-done.7.other_ref.refs_5_ = bf16[896,1792]{1,0:T(8,128)(2,1)} collective-permute-done((bf16[896,1792]{1,0:T(8,128)(2,1)}, bf16[896,1792]{1,0:T(8,128)(2,1)}, u32[]{:S(2)}, u32[]{:S(2)}) %collective-permute-start.7) | collective-permute-done | bytes 3211296 | tf_op jit(solution)/shard_map/ppermute | solution.py:261
  177.8 6.0 %pack.3 = bf16[1024,1792]{1,0:T(8,128)(2,1)} custom-call(s32[6]{0:T(128)} %stack.31.place, bf16[896,1792]{1,0:T(8,128)(2,1)} %get-tuple-element.57.self_ref.refs_4_, bf16[896,1792]{1,0:T(8,128)(2,1)} %collective-permute-done.7.other_ref.refs_5_, bf16[1024,2048]{1,0:T(8,128)(2,1)} %collective-permute-done.2.near_ref), custom_call_target="tpu_custom_call" | custom-call | bytes 1048576 | tf_op jit(solution)/shard_map/pack/pallas_call | solution.py:89
  183.8 15.5 %collective-permute-done.5 = bf16[224,2048]{1,0:T(8,128)(2,1)S(1)} collective-permute-done((bf16[224,2048]{1,0:T(8,128)(2,1)}, bf16[224,2048]{1,0:T(8,128)(2,1)S(1)}, u32[]{:S(2)}, u32[]{:S(2)}) %collective-permute-start.5) | collective-permute-done | bytes 917536 | tf_op jit(solution)/shard_map/ppermute | solution.py:271
  200.3 2.5 collective-permute-start.8
  202.8 6.6 %collective-permute-start.9 = (bf16[1024,1792]{1,0:T(8,128)(2,1)}, bf16[1024,1792]{1,0:T(8,128)(2,1)}, u32[]{:S(2)}, u32[]{:S(2)}) collective-permute-start(bf16[1024,1792]{1,0:T(8,128)(2,1)} %pack.3), channel_id=1, source_target_pairs={{0,4},{4,0},{8,12},{12,8},{1,5},{5,1},{9,13},{13,9},{2,6},{6,2},{1... | collective-permute-start | bytes 11010056 | tf_op jit(solution)/shard_map/ppermute | solution.py:319
  209.4 3.2 slice.29
  212.6 16.7 %early_part.5.refs_0_ = f32[896,768]{1,0:T(8,128)} custom-call(s32[6]{0:T(128)} %stack.31.place, bf16[4,896,2048]{2,1,0:T(8,128)(2,1)} %bitcast.37, bf16[768,2048]{1,0:T(8,128)(2,1)} %constant_dynamic-slice_fusion.2.own_ref, bf16[768,2048]{1,0:T(8,128)(2,1)} %collective-permute-done.3.mate_ref, bf16[768,2048]{1,0:T(8,128)(2,1)} %collective-permute-done.4.near_ref), custom_call_target="tpu_custom_call" | custom-call | flops 786432 | tf_op jit(solution)/shard_map/early_part/pallas_call | solution.py:48
  229.3 2.0 collective-permute-start.11
  231.3 4.3 %pack.4 = bf16[512,2048]{1,0:T(8,128)(2,1)} custom-call(s32[6]{0:T(128)} %stack.31.place, bf16[896,1792]{1,0:T(8,128)(2,1)} %get-tuple-element.57.self_ref.refs_4_, bf16[896,1792]{1,0:T(8,128)(2,1)} %collective-permute-done.7.other_ref.refs_5_, bf16[768,2048]{1,0:T(8,128)(2,1)} %collective-permute-done.4.near_ref), custom_call_target="tpu_custom_call" | custom-call | bytes 1048576 | tf_op jit(solution)/shard_map/pack/pallas_call | solution.py:89
  235.6 2.0 collective-permute-start.12
  237.7 2.3 slice.28
  240.0 3.3 pack.5
  243.4 20.1 %early_part.6.refs_1_ = f32[896,1024]{1,0:T(8,128)} custom-call(s32[6]{0:T(128)} %stack.31.place, bf16[4,896,2048]{2,1,0:T(8,128)(2,1)} %bitcast.41, bf16[1024,2048]{1,0:T(8,128)(2,1)} %constant_dynamic-slice_fusion.4.own_ref, bf16[1024,2048]{1,0:T(8,128)(2,1)} %collective-permute-done.1.mate_ref, bf16[1024,2048]{1,0:T(8,128)(2,1)} %collective-permute-done.2.near_ref), custom_call_target="tpu_custom_call" | custom-call | flops 1048576 | tf_op jit(solution)/shard_map/early_part/pallas_call | solution.py:48
  263.4 16.5 %early_part.7.refs_1_ = f32[896,768]{1,0:T(8,128)} custom-call(s32[6]{0:T(128)} %stack.31.place, bf16[4,896,2048]{2,1,0:T(8,128)(2,1)} %bitcast.42, bf16[768,2048]{1,0:T(8,128)(2,1)} %constant_dynamic-slice_fusion.2.own_ref, bf16[768,2048]{1,0:T(8,128)(2,1)} %collective-permute-done.3.mate_ref, bf16[768,2048]{1,0:T(8,128)(2,1)} %collective-permute-done.4.near_ref), custom_call_target="tpu_custom_call" | custom-call | flops 786432 | tf_op jit(solution)/shard_map/early_part/pallas_call | solution.py:48
  279.9 1.7 collective-permute-start.10
  281.6 1.5 collective-permute-start.13
  284.7 5.3 %collective-permute-done.9.refs_12_.refs_13_.refs_14_.refs_15_.refs_16_ = bf16[1024,1792]{1,0:T(8,128)(2,1)} collective-permute-done((bf16[1024,1792]{1,0:T(8,128)(2,1)}, bf16[1024,1792]{1,0:T(8,128)(2,1)}, u32[]{:S(2)}, u32[]{:S(2)}) %collective-permute-start.9) | collective-permute-done | bytes 3670048 | tf_op jit(solution)/shard_map/ppermute | solution.py:319
  291.0 32.6 %late_part.3.refs_9_ = f32[1792,128]{1,0:T(8,128)} custom-call(s32[6]{0:T(128)} %stack.31.place, f32[896,1024]{1,0:T(8,128)} %early_part.4.refs_0_, f32[896,1024]{1,0:T(8,128)} %early_part.6.refs_1_, bf16[4,896,2048]{2,1,0:T(8,128)(2,1)} %bitcast.38, bf16[4,896,2048]{2,1,0:T(8,128)(2,1)} %bitcast.43, ...), custom_call_target="tpu_custom_call", output_to_operand_aliasing={{}: (11, {})} | custom-call | flops 1048576 | tf_op jit(solution)/shard_map/late_part/pallas_call | solution.py:187
  323.7 11.1 %collective-permute-done.12.refs_10_.refs_11_.refs_12_ = bf16[512,2048]{1,0:T(8,128)(2,1)S(1)} collective-permute-done((bf16[512,2048]{1,0:T(8,128)(2,1)}, bf16[512,2048]{1,0:T(8,128)(2,1)S(1)}, u32[]{:S(2)}, u32[]{:S(2)}) %collective-permute-start.12) | collective-permute-done | bytes 2097184 | tf_op jit(solution)/shard_map/ppermute | solution.py:319
  334.8 1.4 copy-done.2
  336.2 14.1 %late_part.4.refs_9_ = f32[1792,128]{1,0:T(8,128)} custom-call(s32[6]{0:T(128)} %stack.31.place, f32[896,768]{1,0:T(8,128)} %early_part.5.refs_0_, f32[896,768]{1,0:T(8,128)} %early_part.7.refs_1_, bf16[4,896,2048]{2,1,0:T(8,128)(2,1)} %bitcast.39, bf16[4,896,2048]{2,1,0:T(8,128)(2,1)} %bitcast.44, ...), custom_call_target="tpu_custom_call", output_to_operand_aliasing={{}: (10, {})} | custom-call | flops 1048576 | tf_op jit(solution)/shard_map/late_part/pallas_call | solution.py:187
  350.3 3.6 collective-permute-done.13.refs_10_.refs_11_
  353.9 11.5 %late_part.5 = f32[1792,128]{1,0:T(8,128)} custom-call(s32[6]{0:T(128)} %stack.31.place, f32[896,768]{1,0:T(8,128)} %early_part.5.refs_0_, f32[896,768]{1,0:T(8,128)} %early_part.7.refs_1_, bf16[4,896,2048]{2,1,0:T(8,128)(2,1)} %bitcast.40, bf16[4,896,2048]{2,1,0:T(8,128)(2,1)} %bitcast.45, ...), custom_call_target="tpu_custom_call", output_to_operand_aliasing={{}: (10, {})} | custom-call | flops 1048576 | tf_op jit(solution)/shard_map/late_part/pallas_call | solution.py:187
  365.4 3.7 all-to-all-start
  369.4 12.7 %all-to-all-done = f32[8,224,128]{2,1,0:T(8,128)S(1)} async-done(((f32[8,224,128]{2,1,0:T(8,128)}), f32[8,224,128]{2,1,0:T(8,128)S(1)}, u32[]{:S(2)}, u32[]{:S(2)}) %all-to-all-start) | async-done | bytes 917536 | tf_op jit(solution)/shard_map/all_to_all | solution.py:329
  382.2 1.3 collective-permute-start.14
  383.6 10.1 %collective-permute-done.14 = f32[224,64]{1,0:T(8,128)S(1)} collective-permute-done((f32[224,64]{1,0:T(8,128)S(1)}, f32[224,64]{1,0:T(8,128)S(1)}, u32[]{:S(2)}, u32[]{:S(2)}) %collective-permute-start.14) | collective-permute-done | bytes 57376 | tf_op jit(solution)/shard_map/ppermute | solution.py:332
  393.8 5.8 %all-gather.2 = f32[4,224,64]{1,2,0:T(8,128)S(1)} all-gather(f32[1,224,64]{1,2,0:T(8,128)S(1)} %copy.20), channel_id=1, replica_groups=mesh['groups'=2,'dp'=4,'fsdp'=4] {'fsdp'}, dimensions={0}, use_global_device_ids=true | all-gather | bytes 286720 | tf_op jit(solution)/shard_map/all_gather | solution.py:333
  400.0 3.1 fusion.4
  403.3 16.1 %all_gather.27 = bf16[64,4096]{1,0:T(8,128)(2,1)S(1)} all-gather(bf16[16,4096]{1,0:T(8,128)(2,1)S(1)} %convert_element_type.18), channel_id=1, replica_groups=mesh['groups'=2,'dp'=4,'fsdp'=4] {'dp'}, dimensions={0}, use_global_device_ids=true | all-gather | bytes 655360 | tf_op jit(solution)/shard_map/all_gather | solution.py:221
  419.5 2.7 convolution_multiply_fusion
  (58 shorter events, 8.3 us)
Async XLA Ops:
  6.5 276.6 %copy-start = (bf16[64,3584]{1,0:T(8,128)(2,1)S(1)}, bf16[64,3584]{1,0:T(8,128)(2,1)}, u32[]{:S(2)}) copy-start(bf16[64,3584]{1,0:T(8,128)(2,1)} %param.12) | copy-start | bytes 1376260
  6.5 99.5 %all-gather.9.cloned.1.call-start = ((), (), s32[]{:S(2)}) async-start(), calls=%async_computation.3 | async-start | bytes 18350080 | tf_op jit(solution)/shard_map/all_gather | solution.py:248
  7.3 236.1 %all-gather.11.cloned.1.call-start = ((), (), s32[]{:S(2)}) async-start(), calls=%async_computation.4 | async-start | bytes 18350080 | tf_op jit(solution)/shard_map/all_gather | solution.py:262
  12.1 11.9 %copy-start.7 = (bf16[64,2048]{1,0:T(8,128)(2,1)S(1)}, bf16[64,2048]{1,0:T(8,128)(2,1)}, u32[]{:S(2)}) copy-start(bf16[64,2048]{1,0:T(8,128)(2,1)} %param.11) | copy-start | bytes 786436
  12.1 93.9 %collective-permute-start.1 = (bf16[1024,2048]{1,0:T(8,128)(2,1)}, bf16[1024,2048]{1,0:T(8,128)(2,1)}, u32[]{:S(2)}, u32[]{:S(2)}) collective-permute-start(bf16[1024,2048]{1,0:T(8,128)(2,1)} %constant_dynamic-slice_fusion.4.own_ref), channel_id=1, source_target_pairs={{0,4},{4,0},{8,12},{12,8},{1,5},{5,1},{9,13},{13,9},{2,6},{6,2},{1... | collective-permute-start | bytes 12582920 | tf_op jit(solution)/shard_map/ppermute | solution.py:250
  15.1 90.9 %collective-permute-start.2 = (bf16[1024,2048]{1,0:T(8,128)(2,1)}, bf16[1024,2048]{1,0:T(8,128)(2,1)}, u32[]{:S(2)}, u32[]{:S(2)}) collective-permute-start(bf16[1024,2048]{1,0:T(8,128)(2,1)} %constant_dynamic-slice_fusion.4.own_ref), channel_id=1, source_target_pairs={{4,8},{8,4},{5,9},{9,5},{6,10},{10,6},{7,11},{11,7},{20,24},{24,20... | collective-permute-start | bytes 12582920 | tf_op jit(solution)/shard_map/ppermute | solution.py:251
  17.8 81.1 %collective-permute-start = (bf16[896,2048]{1,0:T(8,128)(2,1)}, bf16[896,2048]{1,0:T(8,128)(2,1)}, u32[]{:S(2)}, u32[]{:S(2)}) collective-permute-start(bf16[896,2048]{1,0:T(8,128)(2,1)} %param.8), channel_id=1, source_target_pairs={{0,16},{16,0},{1,17},{17,1},{2,18},{18,2},{3,19},{19,3},{4,20},{20... | collective-permute-start | bytes 11010056 | tf_op jit(solution)/shard_map/ppermute | solution.py:249
  19.3 4.7 %copy-start.3 = (bf16[896,2048]{1,0:T(8,128)(2,1)S(1)}, bf16[896,2048]{1,0:T(8,128)(2,1)}, u32[]{:S(2)}) copy-start(bf16[896,2048]{1,0:T(8,128)(2,1)} %param.7) | copy-start | bytes 11010052
  106.0 183.9 %all-gather.7.cloned.1.call-start = ((), (), s32[]{:S(2)}) async-start(), calls=%async_computation.1 | async-start | bytes 8257536 | tf_op jit(solution)/shard_map/all_gather | solution.py:282
  106.1 71.7 %collective-permute-start.7 = (bf16[896,1792]{1,0:T(8,128)(2,1)}, bf16[896,1792]{1,0:T(8,128)(2,1)}, u32[]{:S(2)}, u32[]{:S(2)}) collective-permute-start(bf16[896,1792]{1,0:T(8,128)(2,1)} %get-tuple-element.36), channel_id=1, source_target_pairs={{0,16},{16,0},{1,17},{17,1},{2,18},{18,2},{3,19},{19,3},{4,20},{20... | collective-permute-start | bytes 9633800 | tf_op jit(solution)/shard_map/ppermute | solution.py:261
  107.8 91.4 %collective-permute-start.3 = (bf16[768,2048]{1,0:T(8,128)(2,1)}, bf16[768,2048]{1,0:T(8,128)(2,1)}, u32[]{:S(2)}, u32[]{:S(2)}) collective-permute-start(bf16[768,2048]{1,0:T(8,128)(2,1)} %constant_dynamic-slice_fusion.2.own_ref), channel_id=1, source_target_pairs={{0,4},{4,0},{8,12},{12,8},{1,5},{5,1},{9,13},{13,9},{2,6},{6,2},{1... | collective-permute-start | bytes 9437192 | tf_op jit(solution)/shard_map/ppermute | solution.py:259
  112.4 86.8 %collective-permute-start.4 = (bf16[768,2048]{1,0:T(8,128)(2,1)}, bf16[768,2048]{1,0:T(8,128)(2,1)}, u32[]{:S(2)}, u32[]{:S(2)}) collective-permute-start(bf16[768,2048]{1,0:T(8,128)(2,1)} %constant_dynamic-slice_fusion.2.own_ref), channel_id=1, source_target_pairs={{4,8},{8,4},{5,9},{9,5},{6,10},{10,6},{7,11},{11,7},{20,24},{24,20... | collective-permute-start | bytes 9437192 | tf_op jit(solution)/shard_map/ppermute | solution.py:260
  117.4 81.8 %collective-permute-start.6 = (bf16[256,2048]{1,0:T(8,128)(2,1)S(1)}, bf16[256,2048]{1,0:T(8,128)(2,1)S(1)}, u32[]{:S(2)}, u32[]{:S(2)}) collective-permute-start(bf16[256,2048]{1,0:T(8,128)(2,1)S(1)} %slice.25), channel_id=1, source_target_pairs={{4,8},{8,4},{5,9},{9,5},{6,10},{10,6},{7,11},{11,7},{20,24},{24,20... | collective-permute-start | bytes 3145736 | tf_op jit(solution)/shard_map/ppermute | solution.py:272
  120.7 78.5 %collective-permute-start.5 = (bf16[224,2048]{1,0:T(8,128)(2,1)}, bf16[224,2048]{1,0:T(8,128)(2,1)S(1)}, u32[]{:S(2)}, u32[]{:S(2)}) collective-permute-start(bf16[224,2048]{1,0:T(8,128)(2,1)} %bitcast_select_fusion), channel_id=1, source_target_pairs={{0,4},{4,0},{8,12},{12,8},{1,5},{5,1},{9,13},{13,9},{2,6},{6,2},{1... | collective-permute-start | bytes 2752520 | tf_op jit(solution)/shard_map/ppermute | solution.py:271
  199.2 0.9 copy-start.4
  199.2 30.1 %copy-start.6 = (bf16[256,2048]{1,0:T(8,128)(2,1)}, bf16[256,2048]{1,0:T(8,128)(2,1)S(1)}, u32[]{:S(2)}) copy-start(bf16[256,2048]{1,0:T(8,128)(2,1)S(1)} %collective-permute-done.6.refs_6_) | copy-start | bytes 3145732
  200.2 123.5 %all-reduce.3.cloned.1.call-start = ((), (), s32[]{:S(2)}) async-start(), calls=%async_computation.2 | async-start | bytes 458752 | tf_op jit(solution)/shard_map/psum | solution.py:283
  200.3 81.3 %collective-permute-start.8 = (bf16[768,2048]{1,0:T(8,128)(2,1)}, bf16[768,2048]{1,0:T(8,128)(2,1)}, u32[]{:S(2)}, u32[]{:S(2)}) collective-permute-start(bf16[768,2048]{1,0:T(8,128)(2,1)} %slice.26), channel_id=1, source_target_pairs={{4,8},{8,4},{5,9},{9,5},{6,10},{10,6},{7,11},{11,7},{20,24},{24,20... | collective-permute-start | bytes 9437192 | tf_op jit(solution)/shard_map/ppermute | solution.py:313
  202.8 87.2 %collective-permute-start.9 = (bf16[1024,1792]{1,0:T(8,128)(2,1)}, bf16[1024,1792]{1,0:T(8,128)(2,1)}, u32[]{:S(2)}, u32[]{:S(2)}) collective-permute-start(bf16[1024,1792]{1,0:T(8,128)(2,1)} %pack.3), channel_id=1, source_target_pairs={{0,4},{4,0},{8,12},{12,8},{1,5},{5,1},{9,13},{13,9},{2,6},{6,2},{1... | collective-permute-start | bytes 11010056 | tf_op jit(solution)/shard_map/ppermute | solution.py:319
  229.3 94.4 %collective-permute-start.11 = (bf16[512,2048]{1,0:T(8,128)(2,1)}, bf16[512,2048]{1,0:T(8,128)(2,1)}, u32[]{:S(2)}, u32[]{:S(2)}) collective-permute-start(bf16[512,2048]{1,0:T(8,128)(2,1)} %slice.29), channel_id=1, source_target_pairs={{4,8},{8,4},{5,9},{9,5},{6,10},{10,6},{7,11},{11,7},{20,24},{24,20... | collective-permute-start | bytes 6291464 | tf_op jit(solution)/shard_map/ppermute | solution.py:313
  235.6 99.2 %collective-permute-start.12 = (bf16[512,2048]{1,0:T(8,128)(2,1)}, bf16[512,2048]{1,0:T(8,128)(2,1)S(1)}, u32[]{:S(2)}, u32[]{:S(2)}) collective-permute-start(bf16[512,2048]{1,0:T(8,128)(2,1)} %pack.4), channel_id=1, source_target_pairs={{0,4},{4,0},{8,12},{12,8},{1,5},{5,1},{9,13},{13,9},{2,6},{6,2},{1... | collective-permute-start | bytes 6291464 | tf_op jit(solution)/shard_map/ppermute | solution.py:319
  263.4 20.4 %copy-start.5 = (bf16[224,2048]{1,0:T(8,128)(2,1)S(1)}, bf16[224,2048]{1,0:T(8,128)(2,1)}, u32[]{:S(2)}) copy-start(bf16[224,2048]{1,0:T(8,128)(2,1)} %copy-done.4) | copy-start | bytes 2752516
  279.9 70.4 %collective-permute-start.10 = (bf16[256,2048]{1,0:T(8,128)(2,1)}, bf16[256,2048]{1,0:T(8,128)(2,1)}, u32[]{:S(2)}, u32[]{:S(2)}) collective-permute-start(bf16[256,2048]{1,0:T(8,128)(2,1)} %slice.28), channel_id=1, source_target_pairs={{4,8},{8,4},{5,9},{9,5},{6,10},{10,6},{7,11},{11,7},{20,24},{24,20... | collective-permute-start | bytes 3145736 | tf_op jit(solution)/shard_map/ppermute | solution.py:313
  281.6 72.3 %collective-permute-start.13 = (bf16[256,2048]{1,0:T(8,128)(2,1)}, bf16[256,2048]{1,0:T(8,128)(2,1)}, u32[]{:S(2)}, u32[]{:S(2)}) collective-permute-start(bf16[256,2048]{1,0:T(8,128)(2,1)} %pack.5), channel_id=1, source_target_pairs={{0,4},{4,0},{8,12},{12,8},{1,5},{5,1},{9,13},{13,9},{2,6},{6,2},{1... | collective-permute-start | bytes 3145736 | tf_op jit(solution)/shard_map/ppermute | solution.py:319
  334.8 1.4 copy-start.2
  350.3 18.8 %copy-start.8 = (s32[1,16]{1,0:T(1,128)S(1)}, s32[1,16]{1,0:T(1,128)}, u32[]{:S(2)}) copy-start(s32[1,16]{1,0:T(1,128)} %param.13) | copy-start | bytes 196
  365.4 34.6 %copy-start.9 = (f32[896,64]{0,1:T(8,128)S(1)}, f32[896,64]{0,1:T(8,128)}, u32[]{:S(2)}) copy-start(f32[896,64]{0,1:T(8,128)} %all-reduce.3.cloned.1.call-done) | copy-start | bytes 688132
  365.4 16.7 %all-to-all-start = ((f32[8,224,128]{2,1,0:T(8,128)}), f32[8,224,128]{2,1,0:T(8,128)S(1)}, u32[]{:S(2)}, u32[]{:S(2)}) async-start(f32[8,224,128]{2,1,0:T(8,128)} %bitcast.49), calls=%async_computation | async-start | bytes 1835008 | tf_op jit(solution)/shard_map/all_to_all | solution.py:329
  382.2 11.5 %collective-permute-start.14 = (f32[224,64]{1,0:T(8,128)S(1)}, f32[224,64]{1,0:T(8,128)S(1)}, u32[]{:S(2)}, u32[]{:S(2)}) collective-permute-start(f32[224,64]{1,0:T(8,128)S(1)} %slice.33), channel_id=1, source_target_pairs={{4,0},{8,12},{5,1},{9,13},{6,2},{10,14},{7,3},{11,15},{20,16},{24,... | collective-permute-start | bytes 172040 | tf_op jit(solution)/shard_map/ppermute | solution.py:332
  399.8 22.5 %copy-start.1 = (bf16[64,3584]{1,0:T(8,128)(2,1)S(1)}, bf16[64,3584]{1,0:T(8,128)(2,1)}, u32[]{:S(2)}) copy-start(bf16[64,3584]{1,0:T(8,128)(2,1)} %param.12) | copy-start | bytes 1376260
Sparse Core Ops, SparseCore 0:
  8.9 96.7 all-gather.8
  107.2 96.5 all-gather.10
  205.7 49.9 all-gather.6
  283.2 31.4 all-reduce.2

commit v4 on v3

--- a/solution.py
+++ b/solution.py
@@ -14,7 +14,7 @@
 SWAP = [(0, 1), (1, 0)]
 UNIT = 256
 FIRST_UNITS = 4
-LATE = ((4, (1, 3)), (2, (2,)), (1, (1,)))
+LATE = ((4, (192, 832)), (2, (512,)), (1, (256,)))
 EARLY_COST = 1 << 10
 LATE_COST = 1 << 20
 VMEM_LIMIT = 58 * 1024 * 1024
@@ -115,8 +115,8 @@
     step = pl.program_id(0)
 
     def project(upstream, gate, exact):
-        gate = gate.astype(jnp.float32)
-        up_grad = upstream * (gate / (1.0 + jnp.exp(-gate)))
+        half = 0.5 * gate.astype(jnp.float32)
+        up_grad = upstream * (half + half * jnp.tanh(half))
         high = up_grad.astype(jnp.bfloat16)
         total = dot_nt(high, proj_ref[...])
         if exact:
@@ -269,11 +269,11 @@
     edge = near_first[:, trade_width:].reshape(slots, slot_rows, lanes).swapaxes(0, 1).reshape(slot_rows, width)
     edge = jnp.pad(edge, ((0, piece_rows - slot_rows), (0, 0)))
     piece = lax.ppermute(jnp.where(inner, edge, piece), "dp", MATES)
-    far_start = lax.ppermute(mate_first[: LATE[0][1][0] * UNIT], "dp", ACROSS)
+    far_start = lax.ppermute(mate_first[: LATE[0][1][0]], "dp", ACROSS)
     part_self = early_part(place, grads_self, own_first, mate_first, near_first)
 
     gates = (gate_self, gate_other)
-    ready_far = mate_first[LATE[0][1][0] * UNIT : FIRST_UNITS * UNIT]
+    ready_far = mate_first[LATE[0][1][0] :]
     ready_pack = pack(place, 0, FIRST_UNITS, gates, near_first, 0, trade_width)
     mate_second, near_second, piece, part_self, share_in, far_start, ready_far, ready_pack = lax.optimization_barrier(
         (mate_second, near_second, piece, part_self, share_in, far_start, ready_far, ready_pack)
@@ -304,12 +304,12 @@
         half = int(first * UNIT >= cut)
         base = half * FIRST_UNITS
         fars = []
-        at = first
+        at = first * UNIT
         for count in far_pieces:
             if at:
                 rows = ready_far
                 if order:
-                    rows = after(mates[half][(at - base) * UNIT : (at - base + count) * UNIT], order)
+                    rows = after(mates[half][at - base * UNIT : at - base * UNIT + count], order)
                 fars.append(lax.ppermute(rows, "dp", ACROSS))
             else:
                 fars.append(far_start)

time: 437 us -> 432 us (0.989)
  Pallas kernels: 145 us -> 134 us
  waiting for transfers between devices: 162 us -> 172 us
    pallas_call x3, Pallas kernels: 58.2 us -> 47.7 us  [late_part(): pl.pallas_call(functools.partial(late_kernel, len(fars), len(rests), trad...]
    ppermute x3, waiting for transfers between devices: 20 us -> 26.6 us  [line_plan(): chunks.append((first, half, base, fars, lax.ppermute(packed, 'dp', MATES)))]
  transfers between devices with their start and end apart: 20 -> 20, of which waited for: 9 -> 10; matrix products, arithmetic and copies ran while one was open for 9% -> 9% of each run, Pallas kernels for 31% -> 29%
where the time goes in v4:
time: 432 us; the launch traced here: 425 us
  waiting for transfers between devices  172 us (40%)
  Pallas kernels  134 us (31%)
  starting transfers between devices  37.1 us (9%)
  local copies, waits for them, and re-layouts  36.8 us (9%)
  blocking collectives  22.1 us (5%)
  between operations  13.6 us (3%)
  matrix products  7.72 us (2%)
    pallas_call x4, Pallas kernels, early_part(): pl.pallas_call(early_kernel, grid_spec=pltpu.PrefetchScalarGridSpec(num_s...  73.4 us
    ppermute x1, waiting for transfers between devices, line_plan(): grad_other = lax.ppermute(out_grad, 'groups', SWAP)  66.5 us
    pallas_call x3, Pallas kernels, late_part(): pl.pallas_call(functools.partial(late_kernel, len(fars), len(rests), trad...  47.7 us
    ppermute x1, waiting for transfers between devices, line_plan(): gate_other = lax.ppermute(gate_send, 'groups', SWAP)  30.4 us
    ppermute x3, waiting for transfers between devices, line_plan(): chunks.append((first, half, base, fars, lax.ppermute(packed, 'dp', MATES)))  26.6 us
    all_gather x1, blocking collectives, own_fisher(): lax.all_gather(example_grads.astype(jnp.bfloat16), 'dp', axis=0, tiled=True)  16.1 us
    ppermute x1, waiting for transfers between devices, line_plan(): piece = lax.ppermute(jnp.where(inner, edge, piece), 'dp', MATES)  15.4 us
    pallas_call x3, Pallas kernels, pack(): pl.pallas_call(pack_kernel, grid_spec=pltpu.PrefetchScalarGridSpec(num_sc...  13.1 us
  transfers between devices with their start and end apart: 20, of which 10 were waited for; matrix products, arithmetic and copies ran while one was open for 9% of the time, Pallas kernels for 29%

profile of v4, /device:TPU:0, one launch (start us, length us, event | category | flops | bytes accessed | tf_op | source)
XLA Modules:
  0.0 424.8 jit_solution(16439580971554839271)
XLA Ops:
  7.3 4.8 %constant_dynamic-slice_fusion.4.own_ref = bf16[1024,2048]{1,0:T(8,128)(2,1)} fusion(bf16[3584,2048]{1,0:T(8,128)(2,1)} %param.10, s32[]{:T(128)S(6)} %select_n.40), kind=kLoop, calls=%fused_computation.20 | loop fusion | bytes 8388612 | tf_op jit(solution)/shard_map/dynamic_slice | solution.py:246
  12.1 3.0 collective-permute-start.1
  15.1 2.6 collective-permute-start.2
  17.8 1.5 collective-permute-start
  19.3 4.7 %constant_dynamic-slice_fusion.2.own_ref = bf16[768,2048]{1,0:T(8,128)(2,1)} fusion(bf16[3584,2048]{1,0:T(8,128)(2,1)} %param.10, s32[]{:T(128)S(6)} %select_n.42), kind=kLoop, calls=%fused_computation.18 | loop fusion | bytes 6291460 | tf_op jit(solution)/shard_map/dynamic_slice | solution.py:247
  24.0 1.9 fusion.12
  25.9 6.5 %constant_dynamic-slice_fusion.1 = (bf16[896,1792]{1,0:T(8,128)(2,1)}, bf16[896,1792]{1,0:T(8,128)(2,1)}) fusion(bf16[896,3584]{1,0:T(8,128)(2,1)} %param.9, s32[]{:T(128)S(6)} %select_n.40, s32[]{:T(128)S(6)} %select_n.41), kind=kLoop, calls=%fused_computation.17 | loop fusion | bytes 12845064 | tf_op jit(solution)/shard_map/dynamic_slice | solution.py:252
  32.4 66.5 %collective-permute-done = bf16[896,2048]{1,0:T(8,128)(2,1)} collective-permute-done((bf16[896,2048]{1,0:T(8,128)(2,1)}, bf16[896,2048]{1,0:T(8,128)(2,1)}, u32[]{:S(2)}, u32[]{:S(2)}) %collective-permute-start) | collective-permute-done | bytes 3670048 | tf_op jit(solution)/shard_map/ppermute | solution.py:249
  98.9 7.2 %collective-permute-done.1.mate_ref = bf16[1024,2048]{1,0:T(8,128)(2,1)} collective-permute-done((bf16[1024,2048]{1,0:T(8,128)(2,1)}, bf16[1024,2048]{1,0:T(8,128)(2,1)}, u32[]{:S(2)}, u32[]{:S(2)}) %collective-permute-start.1) | collective-permute-done | bytes 4194336 | tf_op jit(solution)/shard_map/ppermute | solution.py:250
  106.1 1.7 collective-permute-start.7
  107.8 4.6 %collective-permute-start.3 = (bf16[768,2048]{1,0:T(8,128)(2,1)}, bf16[768,2048]{1,0:T(8,128)(2,1)}, u32[]{:S(2)}, u32[]{:S(2)}) collective-permute-start(bf16[768,2048]{1,0:T(8,128)(2,1)} %constant_dynamic-slice_fusion.2.own_ref), channel_id=1, source_target_pairs={{0,4},{4,0},{8,12},{12,8},{1,5},{5,1},{9,13},{13,9},{2,6},{6,2},{1... | collective-permute-start | bytes 9437192 | tf_op jit(solution)/shard_map/ppermute | solution.py:259
  112.4 2.4 collective-permute-start.4
  116.0 1.6 bitcast_select_fusion
  117.6 1.3 collective-permute-start.5
  118.8 2.3 slice.25
  122.4 5.1 %slice.26 = bf16[832,2048]{1,0:T(8,128)(2,1)} slice(bf16[1024,2048]{1,0:T(8,128)(2,1)} %collective-permute-done.1.mate_ref), slice={[192:1024], [0:2048]} | slice | bytes 6815744 | tf_op jit(solution)/shard_map/slice | solution.py:276
  127.5 19.9 %early_part.4.refs_0_ = f32[896,1024]{1,0:T(8,128)} custom-call(s32[6]{0:T(128)} %stack.31.place, bf16[4,896,2048]{2,1,0:T(8,128)(2,1)} %bitcast.36, bf16[1024,2048]{1,0:T(8,128)(2,1)} %constant_dynamic-slice_fusion.4.own_ref, bf16[1024,2048]{1,0:T(8,128)(2,1)} %collective-permute-done.1.mate_ref, bf16[1024,2048]{1,0:T(8,128)(2,1)} %collective-permute-done.2.near_ref), custom_call_target="tpu_custom_call" | custom-call | flops 1048576 | tf_op jit(solution)/shard_map/early_part/pallas_call | solution.py:48
  147.4 30.4 %collective-permute-done.7.other_ref.refs_5_ = bf16[896,1792]{1,0:T(8,128)(2,1)} collective-permute-done((bf16[896,1792]{1,0:T(8,128)(2,1)}, bf16[896,1792]{1,0:T(8,128)(2,1)}, u32[]{:S(2)}, u32[]{:S(2)}) %collective-permute-start.7) | collective-permute-done | bytes 3211296 | tf_op jit(solution)/shard_map/ppermute | solution.py:261
  177.8 6.0 %pack.3 = bf16[1024,1792]{1,0:T(8,128)(2,1)} custom-call(s32[6]{0:T(128)} %stack.31.place, bf16[896,1792]{1,0:T(8,128)(2,1)} %get-tuple-element.57.self_ref.refs_4_, bf16[896,1792]{1,0:T(8,128)(2,1)} %collective-permute-done.7.other_ref.refs_5_, bf16[1024,2048]{1,0:T(8,128)(2,1)} %collective-permute-done.2.near_ref), custom_call_target="tpu_custom_call" | custom-call | bytes 1048576 | tf_op jit(solution)/shard_map/pack/pallas_call | solution.py:89
  183.8 15.4 %collective-permute-done.5 = bf16[224,2048]{1,0:T(8,128)(2,1)S(1)} collective-permute-done((bf16[224,2048]{1,0:T(8,128)(2,1)S(1)}, bf16[224,2048]{1,0:T(8,128)(2,1)S(1)}, u32[]{:S(2)}, u32[]{:S(2)}) %collective-permute-start.5) | collective-permute-done | bytes 917536 | tf_op jit(solution)/shard_map/ppermute | solution.py:271
  200.2 2.6 collective-permute-start.8
  202.8 2.7 collective-permute-start.9
  205.6 3.2 slice.29
  208.7 17.0 %early_part.5.refs_0_ = f32[896,768]{1,0:T(8,128)} custom-call(s32[6]{0:T(128)} %stack.31.place, bf16[4,896,2048]{2,1,0:T(8,128)(2,1)} %bitcast.37, bf16[768,2048]{1,0:T(8,128)(2,1)} %constant_dynamic-slice_fusion.2.own_ref, bf16[768,2048]{1,0:T(8,128)(2,1)} %collective-permute-done.3.mate_ref, bf16[768,2048]{1,0:T(8,128)(2,1)} %collective-permute-done.4.near_ref), custom_call_target="tpu_custom_call" | custom-call | flops 786432 | tf_op jit(solution)/shard_map/early_part/pallas_call | solution.py:48
  225.7 2.0 collective-permute-start.11
  227.7 3.9 pack.4
  231.7 2.7 slice.28
  234.3 3.2 pack.5
  237.6 20.0 %early_part.6.refs_1_ = f32[896,1024]{1,0:T(8,128)} custom-call(s32[6]{0:T(128)} %stack.31.place, bf16[4,896,2048]{2,1,0:T(8,128)(2,1)} %bitcast.41, bf16[1024,2048]{1,0:T(8,128)(2,1)} %constant_dynamic-slice_fusion.4.own_ref, bf16[1024,2048]{1,0:T(8,128)(2,1)} %collective-permute-done.1.mate_ref, bf16[1024,2048]{1,0:T(8,128)(2,1)} %collective-permute-done.2.near_ref), custom_call_target="tpu_custom_call" | custom-call | flops 1048576 | tf_op jit(solution)/shard_map/early_part/pallas_call | solution.py:48
  257.6 16.5 %early_part.7.refs_1_ = f32[896,768]{1,0:T(8,128)} custom-call(s32[6]{0:T(128)} %stack.31.place, bf16[4,896,2048]{2,1,0:T(8,128)(2,1)} %bitcast.42, bf16[768,2048]{1,0:T(8,128)(2,1)} %constant_dynamic-slice_fusion.2.own_ref, bf16[768,2048]{1,0:T(8,128)(2,1)} %collective-permute-done.3.mate_ref, bf16[768,2048]{1,0:T(8,128)(2,1)} %collective-permute-done.4.near_ref), custom_call_target="tpu_custom_call" | custom-call | flops 786432 | tf_op jit(solution)/shard_map/early_part/pallas_call | solution.py:48
  274.1 1.7 collective-permute-start.10
  275.8 5.1 %collective-permute-start.13 = (bf16[256,2048]{1,0:T(8,128)(2,1)}, bf16[256,2048]{1,0:T(8,128)(2,1)}, u32[]{:S(2)}, u32[]{:S(2)}) collective-permute-start(bf16[256,2048]{1,0:T(8,128)(2,1)} %pack.5), channel_id=1, source_target_pairs={{0,4},{4,0},{8,12},{12,8},{1,5},{5,1},{9,13},{13,9},{2,6},{6,2},{1... | collective-permute-start | bytes 3145736 | tf_op jit(solution)/shard_map/ppermute | solution.py:319
  282.5 3.6 collective-permute-done.9.refs_12_.refs_13_.refs_14_.refs_15_.refs_16_
  287.1 22.6 %late_part.3.refs_9_ = f32[1792,128]{1,0:T(8,128)} custom-call(s32[6]{0:T(128)} %stack.31.place, f32[896,1024]{1,0:T(8,128)} %early_part.4.refs_0_, f32[896,1024]{1,0:T(8,128)} %early_part.6.refs_1_, bf16[4,896,2048]{2,1,0:T(8,128)(2,1)} %bitcast.38, bf16[4,896,2048]{2,1,0:T(8,128)(2,1)} %bitcast.43, ...), custom_call_target="tpu_custom_call", output_to_operand_aliasing={{}: (11, {})} | custom-call | flops 1048576 | tf_op jit(solution)/shard_map/late_part/pallas_call | solution.py:187
  309.8 2.1 all-reduce.3.cloned.1.call-done
  311.9 19.1 %collective-permute-done.12.refs_10_.refs_11_.refs_12_ = bf16[512,2048]{1,0:T(8,128)(2,1)S(1)} collective-permute-done((bf16[512,2048]{1,0:T(8,128)(2,1)}, bf16[512,2048]{1,0:T(8,128)(2,1)S(1)}, u32[]{:S(2)}, u32[]{:S(2)}) %collective-permute-start.12) | collective-permute-done | bytes 2097184 | tf_op jit(solution)/shard_map/ppermute | solution.py:319
  331.0 1.3 copy-done.2
  332.3 13.8 %late_part.4.refs_9_ = f32[1792,128]{1,0:T(8,128)} custom-call(s32[6]{0:T(128)} %stack.31.place, f32[896,768]{1,0:T(8,128)} %early_part.5.refs_0_, f32[896,768]{1,0:T(8,128)} %early_part.7.refs_1_, bf16[4,896,2048]{2,1,0:T(8,128)(2,1)} %bitcast.39, bf16[4,896,2048]{2,1,0:T(8,128)(2,1)} %bitcast.44, ...), custom_call_target="tpu_custom_call", output_to_operand_aliasing={{}: (10, {})} | custom-call | flops 1048576 | tf_op jit(solution)/shard_map/late_part/pallas_call | solution.py:187
  346.2 3.9 collective-permute-done.13.refs_10_.refs_11_
  350.1 11.2 %late_part.5 = f32[1792,128]{1,0:T(8,128)} custom-call(s32[6]{0:T(128)} %stack.31.place, f32[896,768]{1,0:T(8,128)} %early_part.5.refs_0_, f32[896,768]{1,0:T(8,128)} %early_part.7.refs_1_, bf16[4,896,2048]{2,1,0:T(8,128)(2,1)} %bitcast.40, bf16[4,896,2048]{2,1,0:T(8,128)(2,1)} %bitcast.45, ...), custom_call_target="tpu_custom_call", output_to_operand_aliasing={{}: (10, {})} | custom-call | flops 1048576 | tf_op jit(solution)/shard_map/late_part/pallas_call | solution.py:187
  361.2 3.7 all-to-all-start
  365.2 12.7 %all-to-all-done = f32[8,224,128]{2,1,0:T(8,128)S(1)} async-done(((f32[8,224,128]{2,1,0:T(8,128)}), f32[8,224,128]{2,1,0:T(8,128)S(1)}, u32[]{:S(2)}, u32[]{:S(2)}) %all-to-all-start) | async-done | bytes 917536 | tf_op jit(solution)/shard_map/all_to_all | solution.py:329
  378.1 1.3 collective-permute-start.14
  379.5 9.9 %collective-permute-done.14 = f32[224,64]{1,0:T(8,128)S(1)} collective-permute-done((f32[224,64]{1,0:T(8,128)S(1)}, f32[224,64]{1,0:T(8,128)S(1)}, u32[]{:S(2)}, u32[]{:S(2)}) %collective-permute-start.14) | collective-permute-done | bytes 57376 | tf_op jit(solution)/shard_map/ppermute | solution.py:332
  389.5 6.0 %all-gather.2 = f32[4,224,64]{1,2,0:T(8,128)S(1)} all-gather(f32[1,224,64]{1,2,0:T(8,128)S(1)} %copy.20), channel_id=1, replica_groups=mesh['groups'=2,'dp'=4,'fsdp'=4] {'fsdp'}, dimensions={0}, use_global_device_ids=true | all-gather | bytes 286720 | tf_op jit(solution)/shard_map/all_gather | solution.py:333
  395.8 3.1 fusion.4
  399.2 16.1 %all_gather.27 = bf16[64,4096]{1,0:T(8,128)(2,1)S(1)} all-gather(bf16[16,4096]{1,0:T(8,128)(2,1)S(1)} %convert_element_type.18), channel_id=1, replica_groups=mesh['groups'=2,'dp'=4,'fsdp'=4] {'dp'}, dimensions={0}, use_global_device_ids=true | all-gather | bytes 655360 | tf_op jit(solution)/shard_map/all_gather | solution.py:221
  415.3 2.7 convolution_multiply_fusion
  (58 shorter events, 8.3 us)
Async XLA Ops:
  6.5 274.3 %copy-start = (bf16[64,3584]{1,0:T(8,128)(2,1)S(1)}, bf16[64,3584]{1,0:T(8,128)(2,1)}, u32[]{:S(2)}) copy-start(bf16[64,3584]{1,0:T(8,128)(2,1)} %param.12) | copy-start | bytes 1376260
  6.5 99.5 %all-gather.9.cloned.1.call-start = ((), (), s32[]{:S(2)}) async-start(), calls=%async_computation.3 | async-start | bytes 18350080 | tf_op jit(solution)/shard_map/all_gather | solution.py:248
  7.3 230.3 %all-gather.11.cloned.1.call-start = ((), (), s32[]{:S(2)}) async-start(), calls=%async_computation.4 | async-start | bytes 18350080 | tf_op jit(solution)/shard_map/all_gather | solution.py:262
  12.1 11.9 %copy-start.7 = (bf16[64,2048]{1,0:T(8,128)(2,1)S(1)}, bf16[64,2048]{1,0:T(8,128)(2,1)}, u32[]{:S(2)}) copy-start(bf16[64,2048]{1,0:T(8,128)(2,1)} %param.11) | copy-start | bytes 786436
  12.1 93.9 %collective-permute-start.1 = (bf16[1024,2048]{1,0:T(8,128)(2,1)}, bf16[1024,2048]{1,0:T(8,128)(2,1)}, u32[]{:S(2)}, u32[]{:S(2)}) collective-permute-start(bf16[1024,2048]{1,0:T(8,128)(2,1)} %constant_dynamic-slice_fusion.4.own_ref), channel_id=1, source_target_pairs={{0,4},{4,0},{8,12},{12,8},{1,5},{5,1},{9,13},{13,9},{2,6},{6,2},{1... | collective-permute-start | bytes 12582920 | tf_op jit(solution)/shard_map/ppermute | solution.py:250
  15.1 90.9 %collective-permute-start.2 = (bf16[1024,2048]{1,0:T(8,128)(2,1)}, bf16[1024,2048]{1,0:T(8,128)(2,1)}, u32[]{:S(2)}, u32[]{:S(2)}) collective-permute-start(bf16[1024,2048]{1,0:T(8,128)(2,1)} %constant_dynamic-slice_fusion.4.own_ref), channel_id=1, source_target_pairs={{4,8},{8,4},{5,9},{9,5},{6,10},{10,6},{7,11},{11,7},{20,24},{24,20... | collective-permute-start | bytes 12582920 | tf_op jit(solution)/shard_map/ppermute | solution.py:251
  17.8 81.1 %collective-permute-start = (bf16[896,2048]{1,0:T(8,128)(2,1)}, bf16[896,2048]{1,0:T(8,128)(2,1)}, u32[]{:S(2)}, u32[]{:S(2)}) collective-permute-start(bf16[896,2048]{1,0:T(8,128)(2,1)} %param.8), channel_id=1, source_target_pairs={{0,16},{16,0},{1,17},{17,1},{2,18},{18,2},{3,19},{19,3},{4,20},{20... | collective-permute-start | bytes 11010056 | tf_op jit(solution)/shard_map/ppermute | solution.py:249
  19.3 4.7 %copy-start.3 = (bf16[896,2048]{1,0:T(8,128)(2,1)S(1)}, bf16[896,2048]{1,0:T(8,128)(2,1)}, u32[]{:S(2)}) copy-start(bf16[896,2048]{1,0:T(8,128)(2,1)} %param.7) | copy-start | bytes 11010052
  106.0 180.1 %all-gather.7.cloned.1.call-start = ((), (), s32[]{:S(2)}) async-start(), calls=%async_computation.1 | async-start | bytes 8257536 | tf_op jit(solution)/shard_map/all_gather | solution.py:282
  106.1 71.7 %collective-permute-start.7 = (bf16[896,1792]{1,0:T(8,128)(2,1)}, bf16[896,1792]{1,0:T(8,128)(2,1)}, u32[]{:S(2)}, u32[]{:S(2)}) collective-permute-start(bf16[896,1792]{1,0:T(8,128)(2,1)} %get-tuple-element.36), channel_id=1, source_target_pairs={{0,16},{16,0},{1,17},{17,1},{2,18},{18,2},{3,19},{19,3},{4,20},{20... | collective-permute-start | bytes 9633800 | tf_op jit(solution)/shard_map/ppermute | solution.py:261
  107.8 91.4 %collective-permute-start.3 = (bf16[768,2048]{1,0:T(8,128)(2,1)}, bf16[768,2048]{1,0:T(8,128)(2,1)}, u32[]{:S(2)}, u32[]{:S(2)}) collective-permute-start(bf16[768,2048]{1,0:T(8,128)(2,1)} %constant_dynamic-slice_fusion.2.own_ref), channel_id=1, source_target_pairs={{0,4},{4,0},{8,12},{12,8},{1,5},{5,1},{9,13},{13,9},{2,6},{6,2},{1... | collective-permute-start | bytes 9437192 | tf_op jit(solution)/shard_map/ppermute | solution.py:259
  112.4 86.8 %collective-permute-start.4 = (bf16[768,2048]{1,0:T(8,128)(2,1)}, bf16[768,2048]{1,0:T(8,128)(2,1)}, u32[]{:S(2)}, u32[]{:S(2)}) collective-permute-start(bf16[768,2048]{1,0:T(8,128)(2,1)} %constant_dynamic-slice_fusion.2.own_ref), channel_id=1, source_target_pairs={{4,8},{8,4},{5,9},{9,5},{6,10},{10,6},{7,11},{11,7},{20,24},{24,20... | collective-permute-start | bytes 9437192 | tf_op jit(solution)/shard_map/ppermute | solution.py:260
  117.6 81.7 %collective-permute-start.5 = (bf16[224,2048]{1,0:T(8,128)(2,1)S(1)}, bf16[224,2048]{1,0:T(8,128)(2,1)S(1)}, u32[]{:S(2)}, u32[]{:S(2)}) collective-permute-start(bf16[224,2048]{1,0:T(8,128)(2,1)S(1)} %bitcast_select_fusion), channel_id=1, source_target_pairs={{0,4},{4,0},{8,12},{12,8},{1,5},{5,1},{9,13},{13,9},{2,6},{6,2},{1... | collective-permute-start | bytes 2752520 | tf_op jit(solution)/shard_map/ppermute | solution.py:271
  121.1 62.7 %collective-permute-start.6 = (bf16[192,2048]{1,0:T(8,128)(2,1)}, bf16[192,2048]{1,0:T(8,128)(2,1)S(1)}, u32[]{:S(2)}, u32[]{:S(2)}) collective-permute-start(bf16[192,2048]{1,0:T(8,128)(2,1)} %slice.25), channel_id=1, source_target_pairs={{4,8},{8,4},{5,9},{9,5},{6,10},{10,6},{7,11},{11,7},{20,24},{24,20... | collective-permute-start | bytes 2359304 | tf_op jit(solution)/shard_map/ppermute | solution.py:272
  183.8 41.9 %copy-start.6 = (bf16[192,2048]{1,0:T(8,128)(2,1)}, bf16[192,2048]{1,0:T(8,128)(2,1)S(1)}, u32[]{:S(2)}) copy-start(bf16[192,2048]{1,0:T(8,128)(2,1)S(1)} %collective-permute-done.6.refs_6_) | copy-start | bytes 2359300
  199.2 0.9 copy-start.4
  200.2 111.7 %all-reduce.3.cloned.1.call-start = ((), (), s32[]{:S(2)}) async-start(), calls=%async_computation.2 | async-start | bytes 458752 | tf_op jit(solution)/shard_map/psum | solution.py:283
  200.2 75.6 %collective-permute-start.8 = (bf16[832,2048]{1,0:T(8,128)(2,1)}, bf16[832,2048]{1,0:T(8,128)(2,1)}, u32[]{:S(2)}, u32[]{:S(2)}) collective-permute-start(bf16[832,2048]{1,0:T(8,128)(2,1)} %slice.26), channel_id=1, source_target_pairs={{4,8},{8,4},{5,9},{9,5},{6,10},{10,6},{7,11},{11,7},{20,24},{24,20... | collective-permute-start | bytes 10223624 | tf_op jit(solution)/shard_map/ppermute | solution.py:313
  202.8 83.3 %collective-permute-start.9 = (bf16[1024,1792]{1,0:T(8,128)(2,1)}, bf16[1024,1792]{1,0:T(8,128)(2,1)}, u32[]{:S(2)}, u32[]{:S(2)}) collective-permute-start(bf16[1024,1792]{1,0:T(8,128)(2,1)} %pack.3), channel_id=1, source_target_pairs={{0,4},{4,0},{8,12},{12,8},{1,5},{5,1},{9,13},{13,9},{2,6},{6,2},{1... | collective-permute-start | bytes 11010056 | tf_op jit(solution)/shard_map/ppermute | solution.py:319
  225.7 86.2 %collective-permute-start.11 = (bf16[512,2048]{1,0:T(8,128)(2,1)}, bf16[512,2048]{1,0:T(8,128)(2,1)}, u32[]{:S(2)}, u32[]{:S(2)}) collective-permute-start(bf16[512,2048]{1,0:T(8,128)(2,1)} %slice.29), channel_id=1, source_target_pairs={{4,8},{8,4},{5,9},{9,5},{6,10},{10,6},{7,11},{11,7},{20,24},{24,20... | collective-permute-start | bytes 6291464 | tf_op jit(solution)/shard_map/ppermute | solution.py:313
  231.5 99.4 %collective-permute-start.12 = (bf16[512,2048]{1,0:T(8,128)(2,1)}, bf16[512,2048]{1,0:T(8,128)(2,1)S(1)}, u32[]{:S(2)}, u32[]{:S(2)}) collective-permute-start(bf16[512,2048]{1,0:T(8,128)(2,1)} %pack.4), channel_id=1, source_target_pairs={{0,4},{4,0},{8,12},{12,8},{1,5},{5,1},{9,13},{13,9},{2,6},{6,2},{1... | collective-permute-start | bytes 6291464 | tf_op jit(solution)/shard_map/ppermute | solution.py:319
  257.6 24.0 %copy-start.5 = (bf16[224,2048]{1,0:T(8,128)(2,1)S(1)}, bf16[224,2048]{1,0:T(8,128)(2,1)}, u32[]{:S(2)}) copy-start(bf16[224,2048]{1,0:T(8,128)(2,1)} %copy-done.4) | copy-start | bytes 2752516
  274.1 72.0 %collective-permute-start.10 = (bf16[256,2048]{1,0:T(8,128)(2,1)}, bf16[256,2048]{1,0:T(8,128)(2,1)}, u32[]{:S(2)}, u32[]{:S(2)}) collective-permute-start(bf16[256,2048]{1,0:T(8,128)(2,1)} %slice.28), channel_id=1, source_target_pairs={{4,8},{8,4},{5,9},{9,5},{6,10},{10,6},{7,11},{11,7},{20,24},{24,20... | collective-permute-start | bytes 3145736 | tf_op jit(solution)/shard_map/ppermute | solution.py:313
  275.8 74.3 %collective-permute-start.13 = (bf16[256,2048]{1,0:T(8,128)(2,1)}, bf16[256,2048]{1,0:T(8,128)(2,1)}, u32[]{:S(2)}, u32[]{:S(2)}) collective-permute-start(bf16[256,2048]{1,0:T(8,128)(2,1)} %pack.5), channel_id=1, source_target_pairs={{0,4},{4,0},{8,12},{12,8},{1,5},{5,1},{9,13},{13,9},{2,6},{6,2},{1... | collective-permute-start | bytes 3145736 | tf_op jit(solution)/shard_map/ppermute | solution.py:319
  331.0 1.3 copy-start.2
  346.1 18.8 %copy-start.8 = (s32[1,16]{1,0:T(1,128)S(1)}, s32[1,16]{1,0:T(1,128)}, u32[]{:S(2)}) copy-start(s32[1,16]{1,0:T(1,128)} %param.13) | copy-start | bytes 196
  361.2 34.6 %copy-start.9 = (f32[896,64]{0,1:T(8,128)S(1)}, f32[896,64]{0,1:T(8,128)}, u32[]{:S(2)}) copy-start(f32[896,64]{0,1:T(8,128)} %all-reduce.3.cloned.1.call-done) | copy-start | bytes 688132
  361.2 16.7 %all-to-all-start = ((f32[8,224,128]{2,1,0:T(8,128)}), f32[8,224,128]{2,1,0:T(8,128)S(1)}, u32[]{:S(2)}, u32[]{:S(2)}) async-start(f32[8,224,128]{2,1,0:T(8,128)} %bitcast.49), calls=%async_computation | async-start | bytes 1835008 | tf_op jit(solution)/shard_map/all_to_all | solution.py:329
  378.1 11.3 %collective-permute-start.14 = (f32[224,64]{1,0:T(8,128)S(1)}, f32[224,64]{1,0:T(8,128)S(1)}, u32[]{:S(2)}, u32[]{:S(2)}) collective-permute-start(f32[224,64]{1,0:T(8,128)S(1)} %slice.33), channel_id=1, source_target_pairs={{4,0},{8,12},{5,1},{9,13},{6,2},{10,14},{7,3},{11,15},{20,16},{24,... | collective-permute-start | bytes 172040 | tf_op jit(solution)/shard_map/ppermute | solution.py:332
  395.6 22.5 %copy-start.1 = (bf16[64,3584]{1,0:T(8,128)(2,1)S(1)}, bf16[64,3584]{1,0:T(8,128)(2,1)}, u32[]{:S(2)}) copy-start(bf16[64,3584]{1,0:T(8,128)(2,1)} %param.12) | copy-start | bytes 1376260
Sparse Core Ops, SparseCore 0:
  8.9 96.7 all-gather.8
  107.2 96.5 all-gather.10
  205.7 49.9 all-gather.6
  281.0 30.8 all-reduce.2

commit v5 on v4

--- a/solution.py
+++ b/solution.py
@@ -18,6 +18,7 @@
 EARLY_COST = 1 << 10
 LATE_COST = 1 << 20
 VMEM_LIMIT = 58 * 1024 * 1024
+EARLY_VMEM = 32 * 1024 * 1024
 
 
 def dot_nt(left, right):
@@ -54,7 +55,7 @@
             out_specs=pl.BlockSpec((tile, hidden), lambda i, k, place: (i, 0)),
         ),
         out_shape=jax.ShapeDtypeStruct((tokens_dev, hidden), jnp.float32),
-        compiler_params=pltpu.CompilerParams(vmem_limit_bytes=VMEM_LIMIT),
+        compiler_params=pltpu.CompilerParams(vmem_limit_bytes=EARLY_VMEM),
         cost_estimate=pl.CostEstimate(flops=EARLY_COST * hidden, bytes_accessed=0, transcendentals=0),
         name="early_part",
     )(place, grads, own, mate, near)
@@ -95,7 +96,7 @@
             out_specs=pl.BlockSpec((UNIT, wide), lambda i, place: (i, 0)),
         ),
         out_shape=jax.ShapeDtypeStruct((units * UNIT, wide), near.dtype),
-        compiler_params=pltpu.CompilerParams(vmem_limit_bytes=VMEM_LIMIT),
+        compiler_params=pltpu.CompilerParams(vmem_limit_bytes=EARLY_VMEM),
         cost_estimate=pl.CostEstimate(flops=0, bytes_accessed=1 << 20, transcendentals=0),
         name="pack",
     )(place, *gates, near)

time: 432 us -> 431 us (level)
  Pallas kernels: 134 us -> 124 us
  starting transfers between devices: 37.1 us -> 41.5 us
    pallas_call x4, Pallas kernels: 73.4 us -> 66.2 us  [early_part(): pl.pallas_call(early_kernel, grid_spec=pltpu.PrefetchScalarGridSpec(num_s...]
  transfers between devices with their start and end apart: 20 -> 20, of which waited for: 10 -> 10; matrix products, arithmetic and copies ran while one was open for 9% -> 9% of each run, Pallas kernels for 29% -> 27%
where the time goes in v5:
time: 431 us; the launch traced here: 424 us
  waiting for transfers between devices  174 us (40%)
  Pallas kernels  124 us (29%)
  starting transfers between devices  41.5 us (10%)
  local copies, waits for them, and re-layouts  39.5 us (9%)
  blocking collectives  22.1 us (5%)
  between operations  13.7 us (3%)
  matrix products  7.76 us (2%)
    ppermute x1, waiting for transfers between devices, line_plan(): grad_other = lax.ppermute(out_grad, 'groups', SWAP)  66.5 us
    pallas_call x4, Pallas kernels, early_part(): pl.pallas_call(early_kernel, grid_spec=pltpu.PrefetchScalarGridSpec(num_s...  66.2 us
    pallas_call x3, Pallas kernels, late_part(): pl.pallas_call(functools.partial(late_kernel, len(fars), len(rests), trad...  47.7 us
    ppermute x1, waiting for transfers between devices, line_plan(): gate_other = lax.ppermute(gate_send, 'groups', SWAP)  32.2 us
    ppermute x3, waiting for transfers between devices, line_plan(): chunks.append((first, half, base, fars, lax.ppermute(packed, 'dp', MATES)))  27.9 us
    all_gather x1, blocking collectives, own_fisher(): lax.all_gather(example_grads.astype(jnp.bfloat16), 'dp', axis=0, tiled=True)  16.1 us
    ppermute x1, waiting for transfers between devices, line_plan(): piece = lax.ppermute(jnp.where(inner, edge, piece), 'dp', MATES)  15.7 us
    all_to_all x1, waiting for transfers between devices, line_plan(): lax.all_to_all(sums.reshape(2 * fsdp_count, piece_rows, 2 * rank), ('grou...  12.7 us
  transfers between devices with their start and end apart: 20, of which 10 were waited for; matrix products, arithmetic and copies ran while one was open for 9% of the time, Pallas kernels for 27%

profile of v5, /device:TPU:0, one launch (start us, length us, event | category | flops | bytes accessed | tf_op | source)
XLA Modules:
  0.0 424.0 jit_solution(8843791871483242181)
XLA Ops:
  7.3 4.8 %constant_dynamic-slice_fusion.4.own_ref = bf16[1024,2048]{1,0:T(8,128)(2,1)} fusion(bf16[3584,2048]{1,0:T(8,128)(2,1)} %param.10, s32[]{:T(128)S(6)} %select_n.40), kind=kLoop, calls=%fused_computation.20 | loop fusion | bytes 8388612 | tf_op jit(solution)/shard_map/dynamic_slice | solution.py:247
  12.1 3.0 collective-permute-start.1
  15.1 2.6 collective-permute-start.2
  17.8 1.5 collective-permute-start
  19.3 4.7 %constant_dynamic-slice_fusion.2.own_ref = bf16[768,2048]{1,0:T(8,128)(2,1)} fusion(bf16[3584,2048]{1,0:T(8,128)(2,1)} %param.10, s32[]{:T(128)S(6)} %select_n.42), kind=kLoop, calls=%fused_computation.18 | loop fusion | bytes 6291460 | tf_op jit(solution)/shard_map/dynamic_slice | solution.py:248
  24.0 1.9 fusion.12
  25.9 6.5 %constant_dynamic-slice_fusion.1 = (bf16[896,1792]{1,0:T(8,128)(2,1)}, bf16[896,1792]{1,0:T(8,128)(2,1)}) fusion(bf16[896,3584]{1,0:T(8,128)(2,1)} %param.9, s32[]{:T(128)S(6)} %select_n.40, s32[]{:T(128)S(6)} %select_n.41), kind=kLoop, calls=%fused_computation.17 | loop fusion | bytes 12845064 | tf_op jit(solution)/shard_map/dynamic_slice | solution.py:253
  32.4 66.5 %collective-permute-done = bf16[896,2048]{1,0:T(8,128)(2,1)} collective-permute-done((bf16[896,2048]{1,0:T(8,128)(2,1)}, bf16[896,2048]{1,0:T(8,128)(2,1)}, u32[]{:S(2)}, u32[]{:S(2)}) %collective-permute-start) | collective-permute-done | bytes 3670048 | tf_op jit(solution)/shard_map/ppermute | solution.py:250
  98.9 7.1 %collective-permute-done.1.mate_ref = bf16[1024,2048]{1,0:T(8,128)(2,1)} collective-permute-done((bf16[1024,2048]{1,0:T(8,128)(2,1)}, bf16[1024,2048]{1,0:T(8,128)(2,1)}, u32[]{:S(2)}, u32[]{:S(2)}) %collective-permute-start.1) | collective-permute-done | bytes 4194336 | tf_op jit(solution)/shard_map/ppermute | solution.py:251
  106.1 1.7 collective-permute-start.7
  107.8 4.6 %collective-permute-start.3 = (bf16[768,2048]{1,0:T(8,128)(2,1)}, bf16[768,2048]{1,0:T(8,128)(2,1)}, u32[]{:S(2)}, u32[]{:S(2)}) collective-permute-start(bf16[768,2048]{1,0:T(8,128)(2,1)} %constant_dynamic-slice_fusion.2.own_ref), channel_id=1, source_target_pairs={{0,4},{4,0},{8,12},{12,8},{1,5},{5,1},{9,13},{13,9},{2,6},{6,2},{1... | collective-permute-start | bytes 9437192 | tf_op jit(solution)/shard_map/ppermute | solution.py:260
  112.4 2.4 collective-permute-start.4
  116.0 1.6 bitcast_select_fusion
  118.8 2.3 slice.25
  121.9 4.8 %slice.26 = bf16[832,2048]{1,0:T(8,128)(2,1)} slice(bf16[1024,2048]{1,0:T(8,128)(2,1)} %collective-permute-done.1.mate_ref), slice={[192:1024], [0:2048]} | slice | bytes 6815744 | tf_op jit(solution)/shard_map/slice | solution.py:277
  126.7 18.9 %early_part.4.refs_0_ = f32[896,1024]{1,0:T(8,128)S(1)} custom-call(s32[6]{0:T(128)S(1)} %stack.31.place, bf16[4,896,2048]{2,1,0:T(8,128)(2,1)} %bitcast.36, bf16[1024,2048]{1,0:T(8,128)(2,1)} %constant_dynamic-slice_fusion.4.own_ref, bf16[1024,2048]{1,0:T(8,128)(2,1)} %collective-permute-done.1.mate_ref, bf16[1024,2048]{1,0:T(8,128)(2,1)} %collective-permute-done.2.near_ref), custom_call_target="tpu_custom_call" | custom-call | flops 1048576 | tf_op jit(solution)/shard_map/early_part/pallas_call | solution.py:49
  145.6 32.2 %collective-permute-done.7.other_ref.refs_5_ = bf16[896,1792]{1,0:T(8,128)(2,1)} collective-permute-done((bf16[896,1792]{1,0:T(8,128)(2,1)}, bf16[896,1792]{1,0:T(8,128)(2,1)}, u32[]{:S(2)}, u32[]{:S(2)}) %collective-permute-start.7) | collective-permute-done | bytes 3211296 | tf_op jit(solution)/shard_map/ppermute | solution.py:262
  177.8 3.9 pack.3
  181.8 1.8 copy-done.10
  183.6 15.7 %collective-permute-done.5 = bf16[224,2048]{1,0:T(8,128)(2,1)S(1)} collective-permute-done((bf16[224,2048]{1,0:T(8,128)(2,1)S(1)}, bf16[224,2048]{1,0:T(8,128)(2,1)S(1)}, u32[]{:S(2)}, u32[]{:S(2)}) %collective-permute-start.5) | collective-permute-done | bytes 917536 | tf_op jit(solution)/shard_map/ppermute | solution.py:272
  200.2 2.7 collective-permute-start.8
  203.0 2.9 collective-permute-start.9
  205.8 3.2 slice.29
  209.0 14.6 %early_part.5.refs_0_ = f32[896,768]{1,0:T(8,128)S(1)} custom-call(s32[6]{0:T(128)S(1)} %stack.31.place, bf16[4,896,2048]{2,1,0:T(8,128)(2,1)} %bitcast.37, bf16[768,2048]{1,0:T(8,128)(2,1)S(1)} %copy-done.4, bf16[768,2048]{1,0:T(8,128)(2,1)} %collective-permute-done.3.mate_ref, bf16[768,2048]{1,0:T(8,128)(2,1)} %collective-permute-done.4.near_ref), custom_call_target="tpu_custom_call" | custom-call | flops 786432 | tf_op jit(solution)/shard_map/early_part/pallas_call | solution.py:49
  223.6 2.2 collective-permute-start.11
  225.7 2.5 pack.4
  228.5 2.4 slice.28
  230.8 3.4 pack.5
  234.3 18.8 %early_part.6.refs_1_ = f32[896,1024]{1,0:T(8,128)S(1)} custom-call(s32[6]{0:T(128)S(1)} %stack.31.place, bf16[4,896,2048]{2,1,0:T(8,128)(2,1)} %bitcast.41, bf16[1024,2048]{1,0:T(8,128)(2,1)} %constant_dynamic-slice_fusion.4.own_ref, bf16[1024,2048]{1,0:T(8,128)(2,1)} %collective-permute-done.1.mate_ref, bf16[1024,2048]{1,0:T(8,128)(2,1)} %collective-permute-done.2.near_ref), custom_call_target="tpu_custom_call" | custom-call | flops 1048576 | tf_op jit(solution)/shard_map/early_part/pallas_call | solution.py:49
  253.1 1.8 copy-done.9
  255.0 13.9 %early_part.7.refs_1_ = f32[896,768]{1,0:T(8,128)S(1)} custom-call(s32[6]{0:T(128)S(1)} %stack.31.place, bf16[4,896,2048]{2,1,0:T(8,128)(2,1)} %bitcast.42, bf16[768,2048]{1,0:T(8,128)(2,1)S(1)} %copy-done.5, bf16[768,2048]{1,0:T(8,128)(2,1)} %collective-permute-done.3.mate_ref, bf16[768,2048]{1,0:T(8,128)(2,1)} %collective-permute-done.4.near_ref), custom_call_target="tpu_custom_call" | custom-call | flops 786432 | tf_op jit(solution)/shard_map/early_part/pallas_call | solution.py:49
  268.9 1.5 copy-done.7
  270.4 1.6 collective-permute-start.10
  272.1 9.0 %collective-permute-start.13 = (bf16[256,2048]{1,0:T(8,128)(2,1)}, bf16[256,2048]{1,0:T(8,128)(2,1)}, u32[]{:S(2)}, u32[]{:S(2)}) collective-permute-start(bf16[256,2048]{1,0:T(8,128)(2,1)} %pack.5), channel_id=1, source_target_pairs={{0,4},{4,0},{8,12},{12,8},{1,5},{5,1},{9,13},{13,9},{2,6},{6,2},{1... | collective-permute-start | bytes 3145736 | tf_op jit(solution)/shard_map/ppermute | solution.py:320
  282.8 3.6 collective-permute-done.9.refs_12_.refs_13_.refs_14_.refs_15_.refs_16_
  287.4 22.7 %late_part.3.refs_9_ = f32[1792,128]{1,0:T(8,128)} custom-call(s32[6]{0:T(128)} %copy-done.11, f32[896,1024]{1,0:T(8,128)} %copy-done.8, f32[896,1024]{1,0:T(8,128)} %copy-done.9, bf16[4,896,2048]{2,1,0:T(8,128)(2,1)} %bitcast.38, bf16[4,896,2048]{2,1,0:T(8,128)(2,1)} %bitcast.43, ...), custom_call_target="tpu_custom_call", output_to_operand_aliasing={{}: (11, {})} | custom-call | flops 1048576 | tf_op jit(solution)/shard_map/late_part/pallas_call | solution.py:188
  310.1 2.1 all-reduce.3.cloned.1.call-done
  312.2 19.2 %collective-permute-done.12.refs_10_.refs_11_.refs_12_ = bf16[512,2048]{1,0:T(8,128)(2,1)} collective-permute-done((bf16[512,2048]{1,0:T(8,128)(2,1)S(1)}, bf16[512,2048]{1,0:T(8,128)(2,1)}, u32[]{:S(2)}, u32[]{:S(2)}) %collective-permute-start.12) | collective-permute-done | bytes 2097184 | tf_op jit(solution)/shard_map/ppermute | solution.py:320
  331.3 13.9 %late_part.4.refs_9_ = f32[1792,128]{1,0:T(8,128)} custom-call(s32[6]{0:T(128)} %copy-done.11, f32[896,768]{1,0:T(8,128)} %copy-done.6, f32[896,768]{1,0:T(8,128)} %copy-done.7, bf16[4,896,2048]{2,1,0:T(8,128)(2,1)} %bitcast.39, bf16[4,896,2048]{2,1,0:T(8,128)(2,1)} %bitcast.44, ...), custom_call_target="tpu_custom_call", output_to_operand_aliasing={{}: (10, {})} | custom-call | flops 1048576 | tf_op jit(solution)/shard_map/late_part/pallas_call | solution.py:188
  345.2 5.1 %collective-permute-done.13.refs_10_.refs_11_ = bf16[256,2048]{1,0:T(8,128)(2,1)} collective-permute-done((bf16[256,2048]{1,0:T(8,128)(2,1)}, bf16[256,2048]{1,0:T(8,128)(2,1)}, u32[]{:S(2)}, u32[]{:S(2)}) %collective-permute-start.13) | collective-permute-done | bytes 1048608 | tf_op jit(solution)/shard_map/ppermute | solution.py:320
  350.3 11.2 %late_part.5 = f32[1792,128]{1,0:T(8,128)} custom-call(s32[6]{0:T(128)} %copy-done.11, f32[896,768]{1,0:T(8,128)} %copy-done.6, f32[896,768]{1,0:T(8,128)} %copy-done.7, bf16[4,896,2048]{2,1,0:T(8,128)(2,1)} %bitcast.40, bf16[4,896,2048]{2,1,0:T(8,128)(2,1)} %bitcast.45, ...), custom_call_target="tpu_custom_call", output_to_operand_aliasing={{}: (10, {})} | custom-call | flops 1048576 | tf_op jit(solution)/shard_map/late_part/pallas_call | solution.py:188
  361.5 3.7 all-to-all-start
  365.5 12.7 %all-to-all-done = f32[8,224,128]{2,1,0:T(8,128)S(1)} async-done(((f32[8,224,128]{2,1,0:T(8,128)}), f32[8,224,128]{2,1,0:T(8,128)S(1)}, u32[]{:S(2)}, u32[]{:S(2)}) %all-to-all-start) | async-done | bytes 917536 | tf_op jit(solution)/shard_map/all_to_all | solution.py:330
  379.7 8.8 %collective-permute-done.14 = f32[224,64]{1,0:T(8,128)S(1)} collective-permute-done((f32[224,64]{1,0:T(8,128)S(1)}, f32[224,64]{1,0:T(8,128)S(1)}, u32[]{:S(2)}, u32[]{:S(2)}) %collective-permute-start.14) | collective-permute-done | bytes 57376 | tf_op jit(solution)/shard_map/ppermute | solution.py:333
  388.7 6.0 %all-gather.2 = f32[4,224,64]{1,2,0:T(8,128)S(1)} all-gather(f32[1,224,64]{1,2,0:T(8,128)S(1)} %copy.20), channel_id=1, replica_groups=mesh['groups'=2,'dp'=4,'fsdp'=4] {'fsdp'}, dimensions={0}, use_global_device_ids=true | all-gather | bytes 286720 | tf_op jit(solution)/shard_map/all_gather | solution.py:334
  395.0 3.1 fusion.4
  398.4 16.1 %all_gather.27 = bf16[64,4096]{1,0:T(8,128)(2,1)S(1)} all-gather(bf16[16,4096]{1,0:T(8,128)(2,1)S(1)} %convert_element_type.18), channel_id=1, replica_groups=mesh['groups'=2,'dp'=4,'fsdp'=4] {'dp'}, dimensions={0}, use_global_device_ids=true | all-gather | bytes 655360 | tf_op jit(solution)/shard_map/all_gather | solution.py:222
  414.5 2.7 convolution_multiply_fusion
  (76 shorter events, 10.4 us)
Async XLA Ops:
  6.5 274.6 %copy-start = (bf16[64,3584]{1,0:T(8,128)(2,1)S(1)}, bf16[64,3584]{1,0:T(8,128)(2,1)}, u32[]{:S(2)}) copy-start(bf16[64,3584]{1,0:T(8,128)(2,1)} %param.12) | copy-start | bytes 1376260
  6.5 99.5 %all-gather.9.cloned.1.call-start = ((), (), s32[]{:S(2)}) async-start(), calls=%async_computation.3 | async-start | bytes 18350080 | tf_op jit(solution)/shard_map/all_gather | solution.py:249
  7.3 227.0 %all-gather.11.cloned.1.call-start = ((), (), s32[]{:S(2)}) async-start(), calls=%async_computation.4 | async-start | bytes 18350080 | tf_op jit(solution)/shard_map/all_gather | solution.py:263
  12.1 11.9 %copy-start.16 = (bf16[64,2048]{1,0:T(8,128)(2,1)S(1)}, bf16[64,2048]{1,0:T(8,128)(2,1)}, u32[]{:S(2)}) copy-start(bf16[64,2048]{1,0:T(8,128)(2,1)} %param.11) | copy-start | bytes 786436
  12.1 93.9 %collective-permute-start.1 = (bf16[1024,2048]{1,0:T(8,128)(2,1)}, bf16[1024,2048]{1,0:T(8,128)(2,1)}, u32[]{:S(2)}, u32[]{:S(2)}) collective-permute-start(bf16[1024,2048]{1,0:T(8,128)(2,1)} %constant_dynamic-slice_fusion.4.own_ref), channel_id=1, source_target_pairs={{0,4},{4,0},{8,12},{12,8},{1,5},{5,1},{9,13},{13,9},{2,6},{6,2},{1... | collective-permute-start | bytes 12582920 | tf_op jit(solution)/shard_map/ppermute | solution.py:251
  15.1 90.9 %collective-permute-start.2 = (bf16[1024,2048]{1,0:T(8,128)(2,1)}, bf16[1024,2048]{1,0:T(8,128)(2,1)}, u32[]{:S(2)}, u32[]{:S(2)}) collective-permute-start(bf16[1024,2048]{1,0:T(8,128)(2,1)} %constant_dynamic-slice_fusion.4.own_ref), channel_id=1, source_target_pairs={{4,8},{8,4},{5,9},{9,5},{6,10},{10,6},{7,11},{11,7},{20,24},{24,20... | collective-permute-start | bytes 12582920 | tf_op jit(solution)/shard_map/ppermute | solution.py:252
  17.8 81.1 %collective-permute-start = (bf16[896,2048]{1,0:T(8,128)(2,1)}, bf16[896,2048]{1,0:T(8,128)(2,1)}, u32[]{:S(2)}, u32[]{:S(2)}) collective-permute-start(bf16[896,2048]{1,0:T(8,128)(2,1)} %param.8), channel_id=1, source_target_pairs={{0,16},{16,0},{1,17},{17,1},{2,18},{18,2},{3,19},{19,3},{4,20},{20... | collective-permute-start | bytes 11010056 | tf_op jit(solution)/shard_map/ppermute | solution.py:250
  19.2 4.7 %copy-start.12 = (bf16[896,2048]{1,0:T(8,128)(2,1)S(1)}, bf16[896,2048]{1,0:T(8,128)(2,1)}, u32[]{:S(2)}) copy-start(bf16[896,2048]{1,0:T(8,128)(2,1)} %param.7) | copy-start | bytes 11010052
  106.0 180.3 %all-gather.7.cloned.1.call-start = ((), (), s32[]{:S(2)}) async-start(), calls=%async_computation.1 | async-start | bytes 8257536 | tf_op jit(solution)/shard_map/all_gather | solution.py:283
  106.1 71.7 %collective-permute-start.7 = (bf16[896,1792]{1,0:T(8,128)(2,1)}, bf16[896,1792]{1,0:T(8,128)(2,1)}, u32[]{:S(2)}, u32[]{:S(2)}) collective-permute-start(bf16[896,1792]{1,0:T(8,128)(2,1)} %get-tuple-element.36), channel_id=1, source_target_pairs={{0,16},{16,0},{1,17},{17,1},{2,18},{18,2},{3,19},{19,3},{4,20},{20... | collective-permute-start | bytes 9633800 | tf_op jit(solution)/shard_map/ppermute | solution.py:262
  107.8 91.4 %collective-permute-start.3 = (bf16[768,2048]{1,0:T(8,128)(2,1)}, bf16[768,2048]{1,0:T(8,128)(2,1)}, u32[]{:S(2)}, u32[]{:S(2)}) collective-permute-start(bf16[768,2048]{1,0:T(8,128)(2,1)} %constant_dynamic-slice_fusion.2.own_ref), channel_id=1, source_target_pairs={{0,4},{4,0},{8,12},{12,8},{1,5},{5,1},{9,13},{13,9},{2,6},{6,2},{1... | collective-permute-start | bytes 9437192 | tf_op jit(solution)/shard_map/ppermute | solution.py:260
  112.4 86.8 %collective-permute-start.4 = (bf16[768,2048]{1,0:T(8,128)(2,1)}, bf16[768,2048]{1,0:T(8,128)(2,1)}, u32[]{:S(2)}, u32[]{:S(2)}) collective-permute-start(bf16[768,2048]{1,0:T(8,128)(2,1)} %constant_dynamic-slice_fusion.2.own_ref), channel_id=1, source_target_pairs={{4,8},{8,4},{5,9},{9,5},{6,10},{10,6},{7,11},{11,7},{20,24},{24,20... | collective-permute-start | bytes 9437192 | tf_op jit(solution)/shard_map/ppermute | solution.py:261
  117.6 81.7 %collective-permute-start.5 = (bf16[224,2048]{1,0:T(8,128)(2,1)S(1)}, bf16[224,2048]{1,0:T(8,128)(2,1)S(1)}, u32[]{:S(2)}, u32[]{:S(2)}) collective-permute-start(bf16[224,2048]{1,0:T(8,128)(2,1)S(1)} %bitcast_select_fusion), channel_id=1, source_target_pairs={{0,4},{4,0},{8,12},{12,8},{1,5},{5,1},{9,13},{13,9},{2,6},{6,2},{1... | collective-permute-start | bytes 2752520 | tf_op jit(solution)/shard_map/ppermute | solution.py:272
  121.1 62.5 %collective-permute-start.6 = (bf16[192,2048]{1,0:T(8,128)(2,1)}, bf16[192,2048]{1,0:T(8,128)(2,1)S(1)}, u32[]{:S(2)}, u32[]{:S(2)}) collective-permute-start(bf16[192,2048]{1,0:T(8,128)(2,1)} %slice.25), channel_id=1, source_target_pairs={{4,8},{8,4},{5,9},{9,5},{6,10},{10,6},{7,11},{11,7},{20,24},{24,20... | collective-permute-start | bytes 2359304 | tf_op jit(solution)/shard_map/ppermute | solution.py:273
  121.9 131.2 %copy-start.11 = (s32[6]{0:T(128)}, s32[6]{0:T(128)S(1)}, u32[]{:S(2)}) copy-start(s32[6]{0:T(128)S(1)} %stack.31.place) | copy-start | bytes 76
  126.7 51.1 %copy-start.2 = (bf16[896,1792]{1,0:T(8,128)(2,1)S(1)}, bf16[896,1792]{1,0:T(8,128)(2,1)}, u32[]{:S(2)}) copy-start(bf16[896,1792]{1,0:T(8,128)(2,1)} %get-tuple-element.57.self_ref.refs_4_) | copy-start | bytes 9633796
  145.6 36.1 %copy-start.8 = (f32[896,1024]{1,0:T(8,128)}, f32[896,1024]{1,0:T(8,128)S(1)}, u32[]{:S(2)}) copy-start(f32[896,1024]{1,0:T(8,128)S(1)} %early_part.4.refs_0_) | copy-start | bytes 11010052
  181.7 1.8 copy-start.10
  183.6 40.0 %copy-start.15 = (bf16[192,2048]{1,0:T(8,128)(2,1)}, bf16[192,2048]{1,0:T(8,128)(2,1)S(1)}, u32[]{:S(2)}) copy-start(bf16[192,2048]{1,0:T(8,128)(2,1)S(1)} %collective-permute-done.6.refs_6_) | copy-start | bytes 2359300
  199.2 0.9 copy-start.13
  200.2 112.0 %all-reduce.3.cloned.1.call-start = ((), (), s32[]{:S(2)}) async-start(), calls=%async_computation.2 | async-start | bytes 458752 | tf_op jit(solution)/shard_map/psum | solution.py:284
  200.2 8.8 %copy-start.4 = (bf16[768,2048]{1,0:T(8,128)(2,1)S(1)}, bf16[768,2048]{1,0:T(8,128)(2,1)}, u32[]{:S(2)}) copy-start(bf16[768,2048]{1,0:T(8,128)(2,1)} %constant_dynamic-slice_fusion.2.own_ref) | copy-start | bytes 9437188
  200.2 71.8 %collective-permute-start.8 = (bf16[832,2048]{1,0:T(8,128)(2,1)}, bf16[832,2048]{1,0:T(8,128)(2,1)}, u32[]{:S(2)}, u32[]{:S(2)}) collective-permute-start(bf16[832,2048]{1,0:T(8,128)(2,1)} %slice.26), channel_id=1, source_target_pairs={{4,8},{8,4},{5,9},{9,5},{6,10},{10,6},{7,11},{11,7},{20,24},{24,20... | collective-permute-start | bytes 10223624 | tf_op jit(solution)/shard_map/ppermute | solution.py:314
  203.0 83.4 %collective-permute-start.9 = (bf16[1024,1792]{1,0:T(8,128)(2,1)}, bf16[1024,1792]{1,0:T(8,128)(2,1)}, u32[]{:S(2)}, u32[]{:S(2)}) collective-permute-start(bf16[1024,1792]{1,0:T(8,128)(2,1)} %copy-done.10), channel_id=1, source_target_pairs={{0,4},{4,0},{8,12},{12,8},{1,5},{5,1},{9,13},{13,9},{2,6},{6,2},{1... | collective-permute-start | bytes 11010056 | tf_op jit(solution)/shard_map/ppermute | solution.py:320
  209.0 16.8 %copy-start.3 = (bf16[896,1792]{1,0:T(8,128)(2,1)S(1)}, bf16[896,1792]{1,0:T(8,128)(2,1)}, u32[]{:S(2)}) copy-start(bf16[896,1792]{1,0:T(8,128)(2,1)} %get-tuple-element.57.self_ref.refs_4_) | copy-start | bytes 9633796
  223.5 4.8 %copy-start.6 = (f32[896,768]{1,0:T(8,128)}, f32[896,768]{1,0:T(8,128)S(1)}, u32[]{:S(2)}) copy-start(f32[896,768]{1,0:T(8,128)S(1)} %early_part.5.refs_0_) | copy-start | bytes 8257540
  223.6 88.6 %collective-permute-start.11 = (bf16[512,2048]{1,0:T(8,128)(2,1)}, bf16[512,2048]{1,0:T(8,128)(2,1)}, u32[]{:S(2)}, u32[]{:S(2)}) collective-permute-start(bf16[512,2048]{1,0:T(8,128)(2,1)} %slice.29), channel_id=1, source_target_pairs={{4,8},{8,4},{5,9},{9,5},{6,10},{10,6},{7,11},{11,7},{20,24},{24,20... | collective-permute-start | bytes 6291464 | tf_op jit(solution)/shard_map/ppermute | solution.py:314
  228.3 103.0 %collective-permute-start.12 = (bf16[512,2048]{1,0:T(8,128)(2,1)S(1)}, bf16[512,2048]{1,0:T(8,128)(2,1)}, u32[]{:S(2)}, u32[]{:S(2)}) collective-permute-start(bf16[512,2048]{1,0:T(8,128)(2,1)S(1)} %pack.4), channel_id=1, source_target_pairs={{0,4},{4,0},{8,12},{12,8},{1,5},{5,1},{9,13},{13,9},{2,6},{6,2},{1... | collective-permute-start | bytes 6291464 | tf_op jit(solution)/shard_map/ppermute | solution.py:320
  234.3 20.7 %copy-start.5 = (bf16[768,2048]{1,0:T(8,128)(2,1)S(1)}, bf16[768,2048]{1,0:T(8,128)(2,1)}, u32[]{:S(2)}) copy-start(bf16[768,2048]{1,0:T(8,128)(2,1)} %constant_dynamic-slice_fusion.2.own_ref) | copy-start | bytes 9437188
  253.1 1.8 copy-start.9
  254.9 26.9 %copy-start.14 = (bf16[224,2048]{1,0:T(8,128)(2,1)S(1)}, bf16[224,2048]{1,0:T(8,128)(2,1)}, u32[]{:S(2)}) copy-start(bf16[224,2048]{1,0:T(8,128)(2,1)} %copy-done.13) | copy-start | bytes 2752516
  268.9 1.6 copy-start.7
  270.4 74.8 %collective-permute-start.10 = (bf16[256,2048]{1,0:T(8,128)(2,1)}, bf16[256,2048]{1,0:T(8,128)(2,1)}, u32[]{:S(2)}, u32[]{:S(2)}) collective-permute-start(bf16[256,2048]{1,0:T(8,128)(2,1)} %slice.28), channel_id=1, source_target_pairs={{4,8},{8,4},{5,9},{9,5},{6,10},{10,6},{7,11},{11,7},{20,24},{24,20... | collective-permute-start | bytes 3145736 | tf_op jit(solution)/shard_map/ppermute | solution.py:314
  272.1 78.3 %collective-permute-start.13 = (bf16[256,2048]{1,0:T(8,128)(2,1)}, bf16[256,2048]{1,0:T(8,128)(2,1)}, u32[]{:S(2)}, u32[]{:S(2)}) collective-permute-start(bf16[256,2048]{1,0:T(8,128)(2,1)} %pack.5), channel_id=1, source_target_pairs={{0,4},{4,0},{8,12},{12,8},{1,5},{5,1},{9,13},{13,9},{2,6},{6,2},{1... | collective-permute-start | bytes 3145736 | tf_op jit(solution)/shard_map/ppermute | solution.py:320
  345.2 20.0 %copy-start.17 = (s32[1,16]{1,0:T(1,128)S(1)}, s32[1,16]{1,0:T(1,128)}, u32[]{:S(2)}) copy-start(s32[1,16]{1,0:T(1,128)} %param.13) | copy-start | bytes 196
  361.5 33.5 %copy-start.18 = (f32[896,64]{0,1:T(8,128)S(1)}, f32[896,64]{0,1:T(8,128)}, u32[]{:S(2)}) copy-start(f32[896,64]{0,1:T(8,128)} %all-reduce.3.cloned.1.call-done) | copy-start | bytes 688132
  361.5 16.7 %all-to-all-start = ((f32[8,224,128]{2,1,0:T(8,128)}), f32[8,224,128]{2,1,0:T(8,128)S(1)}, u32[]{:S(2)}, u32[]{:S(2)}) async-start(f32[8,224,128]{2,1,0:T(8,128)} %bitcast.49), calls=%async_computation | async-start | bytes 1835008 | tf_op jit(solution)/shard_map/all_to_all | solution.py:330
  378.3 10.2 %collective-permute-start.14 = (f32[224,64]{1,0:T(8,128)S(1)}, f32[224,64]{1,0:T(8,128)S(1)}, u32[]{:S(2)}, u32[]{:S(2)}) collective-permute-start(f32[224,64]{1,0:T(8,128)S(1)} %slice.33), channel_id=1, source_target_pairs={{4,0},{8,12},{5,1},{9,13},{6,2},{10,14},{7,3},{11,15},{20,16},{24,... | collective-permute-start | bytes 172040 | tf_op jit(solution)/shard_map/ppermute | solution.py:333
  394.8 22.4 %copy-start.1 = (bf16[64,3584]{1,0:T(8,128)(2,1)S(1)}, bf16[64,3584]{1,0:T(8,128)(2,1)}, u32[]{:S(2)}) copy-start(bf16[64,3584]{1,0:T(8,128)(2,1)} %param.12) | copy-start | bytes 1376260
Sparse Core Ops, SparseCore 0:
  8.9 96.7 all-gather.8
  107.2 96.5 all-gather.10
  205.7 49.9 all-gather.6
  281.2 30.8 all-reduce.2
